TPU v7x, 256 devices: a whole 4x4x8 slice. The times are simulated.
256 devices in a mesh: ctx: 32 (over z, x), head: 8 (over y, core).
Axes of the slice: x: 4, y: 4, z: 8, core: 2. Of those that a mesh axis runs over, the one named last changes fastest.
Arguments:
- hidden: bfloat16 [8192, 2304], P('ctx', 'head'), may hold values from -10 to 10
- qkv_weight: bfloat16 [3, 2304, 4096], P(None, None, 'head'), may hold values from -0.125 to 0.125
- conv_weight: float32 [4, 3, 4096], P(None, None, 'head'), may hold values from -2 to 2
- w_beta: bfloat16 [2304, 32], P(None, 'head'), may hold values from -1 to 1
- gate_down: bfloat16 [2304, 128], replicated, may hold values from -0.125 to 0.125
- gate_up: bfloat16 [128, 4096], P(None, 'head'), may hold values from -0.5 to 0.5
- a_log: float32 [32], P('head'), may hold values from -30 to -2
- dt_bias: float32 [4096], P('head'), may hold values from -3 to 3
- norm_gain: float32 [128], replicated, may hold values from 0.25 to 1.75
- prompt_lengths: int32 [4], replicated, may hold values from 1 to 7424, 8192 in all
- send_slot: int32 [8192], P('ctx'), may hold values from 0 to 511, as said below
- gather_src: int32 [8192], P('ctx'), may hold values from 0 to 511, as said below
Outputs:
- attention: bfloat16 [8192, 4096], P('ctx', 'head')
Inputs may be any that keep to these rules, and one draw needn't show every extreme that they name: `send_slot`: slot d * 16 + place of the row's context device d; the rows of one owner name distinct slots, at most 16 rows of one owner go to one context device, every context device receives 256 rows in all, and some owner fills all 16 slots for some context device. `gather_src`: received slot o * 16 + place, o the sending owner; the entries of one context device are distinct and name exactly the slots that owners filled for it.
All inputs are finite; a program needn't handle non-finite values.
Results may differ from a plain program's by a relative error of at most 0.0045.
Values may be sent and summed in bfloat16 or wider, within the bound.
A program may use at most 128 MiB of HBM per device.

v0:
```python
import jax
import jax.numpy as jnp
from jax import lax
from jax.sharding import PartitionSpec as P

CONV = 4
SPAN = 64


def shifted_2(block, axis, distance):
    devices = range(lax.axis_size(axis))
    route = [(i - distance, i) for i in devices if i - distance in devices]
    return lax.ppermute(block, axis, route)


def doc_ids(lengths, positions):
    prompt_ends = jnp.cumsum(lengths)
    ended = jnp.sum((prompt_ends[None, :] <= positions[:, None]).astype(jnp.int32), axis=1)
    return jnp.where(positions < 0, -1, ended)


def unit_norm(values):
    return values / jnp.sqrt(jnp.sum(values * values, axis=-1, keepdims=True) + 1e-06)


def compose_heads(left_maps, right_maps):
    return jnp.einsum("hij,hjk->hik", left_maps, right_maps, precision=lax.Precision.HIGHEST)


def span_pieces(query, key_rows, value_rows, decay_log, strength, segments, seg_before):
    highest = lax.Precision.HIGHEST
    block_len = query.shape[-2]
    channels = query.shape[-1]
    cumulative = jnp.cumsum(decay_log, axis=-2)
    last_cum = cumulative[..., -1:, :]
    key_up = key_rows * jnp.exp(cumulative)
    key_down = key_rows * jnp.exp(-cumulative)
    query_up = query * jnp.exp(cumulative)
    same_doc = segments[..., :, None] == segments[..., None, :]
    row_ids = jnp.arange(block_len)
    strict_mask = (row_ids[:, None] > row_ids[None, :]) & same_doc
    incl_mask = (row_ids[:, None] >= row_ids[None, :]) & same_doc
    first_doc = (segments == seg_before[..., None]).astype(jnp.float32)[..., None]
    last_doc = (segments == segments[..., -1:]).astype(jnp.float32)[..., None]
    carry_flag = (segments[..., -1] == seg_before).astype(jnp.float32)
    key_mix = jnp.einsum("...td,...sd->...ts", key_up, key_down, precision=highest)
    strict_part = jnp.where(strict_mask, strength[..., :, None] * key_mix, 0.0)
    eye_small = jnp.eye(block_len, dtype=jnp.float32)
    right_side = jnp.concatenate(
        [strength[..., None] * value_rows, strength[..., None] * key_up * first_doc], axis=-1
    )
    solved = jax.scipy.linalg.solve_triangular(
        eye_small + strict_part, right_side, lower=True, unit_diagonal=True
    )
    scores = jnp.where(
        incl_mask, jnp.einsum("...td,...sd->...ts", query_up, key_down, precision=highest), 0.0
    )
    combined = jnp.einsum("...ts,...se->...te", scores, solved, precision=highest)
    out_local = combined[..., :channels]
    lift = query_up * first_doc - combined[..., channels:]
    key_end = key_rows * jnp.exp(last_cum - cumulative) * last_doc
    summary = jnp.einsum("...sd,...se->...de", key_end, solved, precision=highest)
    state_feed = summary[..., :channels]
    eye_channels = jnp.eye(channels, dtype=jnp.float32)
    keep_diag = jnp.exp(last_cum[..., 0, :])[..., :, None] * eye_channels
    state_map = carry_flag[..., None, None] * keep_diag - summary[..., channels:]
    return (out_local, lift, state_map, state_feed)


def on_device(
    hidden,
    qkv_weight,
    conv_weight,
    w_beta,
    gate_down,
    gate_up,
    a_log,
    dt_bias,
    norm_gain,
    prompt_lengths,
    send_slot,
    gather_src,
):
    row_count = send_slot.shape[0]
    ctx_count = lax.axis_size("ctx")
    ctx_place = lax.axis_index("ctx")
    heads_here = a_log.shape[0]
    channels = norm_gain.shape[0]
    full_rows = lax.all_gather(hidden, "head", axis=1, tiled=True)
    buffer_rows = (
        jnp.zeros((2 * row_count, full_rows.shape[1]), full_rows.dtype).at[send_slot].set(full_rows)
    )
    landed = lax.all_to_all(buffer_rows, "ctx", split_axis=0, concat_axis=0, tiled=True)
    packed = landed[gather_src]
    proj_total = jnp.einsum("rd,jdc->jrc", packed, qkv_weight, preferred_element_type=jnp.float32)
    gate_total = jnp.dot(packed, gate_down, preferred_element_type=jnp.float32)
    beta_total = jnp.dot(packed, w_beta, preferred_element_type=jnp.float32)
    projected = proj_total.astype(jnp.bfloat16)
    low_rank = gate_total.astype(jnp.bfloat16)
    strength = jax.nn.sigmoid(beta_total)
    drive = jnp.dot(low_rank, gate_up, preferred_element_type=jnp.float32) + dt_bias[None, :]
    decay_log = -jnp.exp(a_log)[None, :, None] * jax.nn.softplus(
        drive.reshape(row_count, heads_here, channels)
    )
    rim_rows = shifted_2(projected[:, row_count - (CONV - 1) :, :], "ctx", 1)
    extended = jnp.concatenate([rim_rows, projected], axis=1)
    ext_positions = (
        ctx_place * row_count - (CONV - 1) + jnp.arange(row_count + CONV - 1, dtype=jnp.int32)
    )
    ext_ids = doc_ids(prompt_lengths, ext_positions)
    own_ids = ext_ids[CONV - 1 :]
    convolved = jnp.zeros(projected.shape, jnp.float32)
    for tap_index in range(CONV):
        shifted = extended[:, tap_index : tap_index + row_count, :].astype(jnp.float32)
        valid = (ext_ids[tap_index : tap_index + row_count] == own_ids).astype(jnp.float32)
        convolved = convolved + conv_weight[tap_index][:, None, :] * shifted * valid[None, :, None]
    activated = jax.nn.silu(convolved).reshape(3, row_count, heads_here, channels)
    query = unit_norm(activated[0]) * channels ** (-0.5)
    key_rows = unit_norm(activated[1])
    value_rows = activated[2]
    blocks = row_count // SPAN
    segments = own_ids.reshape(blocks, SPAN)
    seg_before = ext_ids[CONV - 2 : CONV - 2 + row_count : SPAN]

    def to_blocks(values):
        return jnp.transpose(values, (1, 0, 2)).reshape(heads_here, blocks, SPAN, channels)

    out_local, lift, state_map, state_feed = span_pieces(
        to_blocks(query),
        to_blocks(key_rows),
        to_blocks(value_rows),
        to_blocks(decay_log),
        strength.T.reshape(heads_here, blocks, SPAN),
        segments,
        seg_before,
    )
    map_steps = jnp.moveaxis(state_map, 1, 0)
    feed_steps = jnp.moveaxis(state_feed, 1, 0)
    eye_heads = jnp.broadcast_to(
        jnp.eye(channels, dtype=jnp.float32), (heads_here, channels, channels)
    )
    zero_states = jnp.zeros((heads_here, channels, channels), jnp.float32)

    def compose_blocks(carried, block_piece):
        whole_map, whole_feed = carried
        step_map, step_feed = block_piece
        return (
            (compose_heads(step_map, whole_map), compose_heads(step_map, whole_feed) + step_feed),
            None,
        )

    (block_map, block_feed), _ = lax.scan(
        compose_blocks, (eye_heads, zero_states), (map_steps, feed_steps)
    )

    def relay_state(step_index, incoming):
        return shifted_2(compose_heads(block_map, incoming) + block_feed, "ctx", 1)

    entry_state = lax.fori_loop(0, ctx_count - 1, relay_state, zero_states)

    def advance(carried, block_piece):
        out_part, lift_part, map_part, feed_part = block_piece
        emitted = out_part + jnp.einsum(
            "hcj,hjk->hck", lift_part, carried, precision=lax.Precision.HIGHEST
        )
        return (compose_heads(map_part, carried) + feed_part, emitted)

    _, emitted_all = lax.scan(
        advance,
        entry_state,
        (jnp.moveaxis(out_local, 1, 0), jnp.moveaxis(lift, 1, 0), map_steps, feed_steps),
    )
    result = jnp.moveaxis(emitted_all, 0, 1).reshape(heads_here, row_count, channels)
    scaled = (
        result * lax.rsqrt(jnp.mean(result * result, axis=-1, keepdims=True) + 1e-05) * norm_gain
    )
    return (
        jnp.transpose(scaled, (1, 0, 2))
        .reshape(row_count, heads_here * channels)
        .astype(jnp.bfloat16)
    )


def solution(mesh):
    placed = (
        P("ctx", "head"),
        P(None, None, "head"),
        P(None, None, "head"),
        P(None, "head"),
        P(),
        P(None, "head"),
        P("head"),
        P("head"),
        P(),
        P(),
        P("ctx"),
        P("ctx"),
    )
    return jax.shard_map(
        on_device, mesh=mesh, in_specs=placed, out_specs=P("ctx", "head"), check_vma=False
    )
```

profile of v0, /device:TPU:128, one launch (start us, length us, event | category | flops | bytes accessed | tf_op | source)
XLA Modules:
  0.0 656.1 jit_solution(103050760296904829)
XLA Ops:
  7.9 29.0 %all-gather.2.cloned.1.call-done = bf16[256,2304]{0,1:T(8,128)(2,1)} async-done(((bf16[256,288]{0,1:T(8,128)(2,1)}), bf16[256,2304]{0,1:T(8,128)(2,1)}) %all-gather.2.cloned.1.call-update) | async-done | bytes 1179664 | tf_op jit(solution)/shard_map/all_gather | solution.py:89
  42.6 9.9 %all-to-all-start = ((bf16[32,16,2304]{2,1,0:T(8,128)(2,1)}), bf16[32,16,2304]{2,1,0:T(8,128)(2,1)S(1)}, u32[]{:S(2)}, u32[]{:S(2)}) async-start(bf16[32,16,2304]{2,1,0:T(8,128)(2,1)} %bitcast.129), calls=%async_computation | async-start | bytes 4718592 | tf_op jit(solution)/shard_map/all_to_all | solution.py:93
  56.7 49.0 %all-to-all-done = bf16[32,16,2304]{2,1,0:T(8,128)(2,1)S(1)} async-done(((bf16[32,16,2304]{2,1,0:T(8,128)(2,1)}), bf16[32,16,2304]{2,1,0:T(8,128)(2,1)S(1)}, u32[]{:S(2)}, u32[]{:S(2)}) %all-to-all-start) | async-done | bytes 2359328 | tf_op jit(solution)/shard_map/all_to_all | solution.py:93
  128.3 79.3 %custom-call.4 = f32[4,4,1,64,64]{3,4,2,1,0:T(8,128)} custom-call(f32[4,4,1,64,64]{4,3,2,1,0:T(8,128)S(1)} %fusion.24), custom_call_target="InvertDiagBlocksLowerTriangular" | custom-call | tf_op jit(solution)/shard_map/jit(_solve_triangular)/vmap(vmap())/triangular_solve | solution.py:52
  220.1 415.8 %while.35 = (s32[]{:T(128)}, f32[4,128,128]{2,1,0:T(8,128)S(1)}, f32[4,128,128]{2,1,0:T(8,128)S(1)}, f32[4,128,128]{2,1,0:T(8,128)S(1)}, s32[]{:T(128)}) while((s32[]{:T(128)}, f32[4,128,128]{2,1,0:T(8,128)S(1)}, f32[4,128,128]{2,1,0:T(8,128)S(1)}, f32[4,128,128]{2,1,0:T(8,128)S(1)}, s32[]{:T(128)}) %tuple.75), condition=%wide.region_8.9_spmd, body=%wide.region_7.8_spmd.sunk | while | flops 100728832 | bytes 2097253 | solution.py:159
  223.1 9.9 %collective-permute-done = f32[4,128,128]{2,1,0:T(8,128)S(1)} collective-permute-done((f32[4,128,128]{2,1,0:T(8,128)}, f32[4,128,128]{2,1,0:T(8,128)S(1)}, u32[]{:S(2)}, u32[]{:S(2)}) %collective-permute-start) | collective-permute-done | bytes 262176 | tf_op jit(solution)/shard_map/while/body/eval_jaxpr/ppermute | solution.py:13
  236.0 9.9 %collective-permute-done = f32[4,128,128]{2,1,0:T(8,128)S(1)} collective-permute-done((f32[4,128,128]{2,1,0:T(8,128)}, f32[4,128,128]{2,1,0:T(8,128)S(1)}, u32[]{:S(2)}, u32[]{:S(2)}) %collective-permute-start) | collective-permute-done | bytes 262176 | tf_op jit(solution)/shard_map/while/body/eval_jaxpr/ppermute | solution.py:13
  248.9 9.9 %collective-permute-done = f32[4,128,128]{2,1,0:T(8,128)S(1)} collective-permute-done((f32[4,128,128]{2,1,0:T(8,128)}, f32[4,128,128]{2,1,0:T(8,128)S(1)}, u32[]{:S(2)}, u32[]{:S(2)}) %collective-permute-start) | collective-permute-done | bytes 262176 | tf_op jit(solution)/shard_map/while/body/eval_jaxpr/ppermute | solution.py:13
  261.8 9.9 %collective-permute-done = f32[4,128,128]{2,1,0:T(8,128)S(1)} collective-permute-done((f32[4,128,128]{2,1,0:T(8,128)}, f32[4,128,128]{2,1,0:T(8,128)S(1)}, u32[]{:S(2)}, u32[]{:S(2)}) %collective-permute-start) | collective-permute-done | bytes 262176 | tf_op jit(solution)/shard_map/while/body/eval_jaxpr/ppermute | solution.py:13
  274.6 10.1 %collective-permute-done = f32[4,128,128]{2,1,0:T(8,128)S(1)} collective-permute-done((f32[4,128,128]{2,1,0:T(8,128)}, f32[4,128,128]{2,1,0:T(8,128)S(1)}, u32[]{:S(2)}, u32[]{:S(2)}) %collective-permute-start) | collective-permute-done | bytes 262176 | tf_op jit(solution)/shard_map/while/body/eval_jaxpr/ppermute | solution.py:13
  287.8 11.2 %collective-permute-done = f32[4,128,128]{2,1,0:T(8,128)S(1)} collective-permute-done((f32[4,128,128]{2,1,0:T(8,128)}, f32[4,128,128]{2,1,0:T(8,128)S(1)}, u32[]{:S(2)}, u32[]{:S(2)}) %collective-permute-start) | collective-permute-done | bytes 262176 | tf_op jit(solution)/shard_map/while/body/eval_jaxpr/ppermute | solution.py:13
  302.0 12.3 %collective-permute-done = f32[4,128,128]{2,1,0:T(8,128)S(1)} collective-permute-done((f32[4,128,128]{2,1,0:T(8,128)}, f32[4,128,128]{2,1,0:T(8,128)S(1)}, u32[]{:S(2)}, u32[]{:S(2)}) %collective-permute-start) | collective-permute-done | bytes 262176 | tf_op jit(solution)/shard_map/while/body/eval_jaxpr/ppermute | solution.py:13
  317.3 11.9 %collective-permute-done = f32[4,128,128]{2,1,0:T(8,128)S(1)} collective-permute-done((f32[4,128,128]{2,1,0:T(8,128)}, f32[4,128,128]{2,1,0:T(8,128)S(1)}, u32[]{:S(2)}, u32[]{:S(2)}) %collective-permute-start) | collective-permute-done | bytes 262176 | tf_op jit(solution)/shard_map/while/body/eval_jaxpr/ppermute | solution.py:13
  332.2 11.0 %collective-permute-done = f32[4,128,128]{2,1,0:T(8,128)S(1)} collective-permute-done((f32[4,128,128]{2,1,0:T(8,128)}, f32[4,128,128]{2,1,0:T(8,128)S(1)}, u32[]{:S(2)}, u32[]{:S(2)}) %collective-permute-start) | collective-permute-done | bytes 262176 | tf_op jit(solution)/shard_map/while/body/eval_jaxpr/ppermute | solution.py:13
  346.2 10.1 %collective-permute-done = f32[4,128,128]{2,1,0:T(8,128)S(1)} collective-permute-done((f32[4,128,128]{2,1,0:T(8,128)}, f32[4,128,128]{2,1,0:T(8,128)S(1)}, u32[]{:S(2)}, u32[]{:S(2)}) %collective-permute-start) | collective-permute-done | bytes 262176 | tf_op jit(solution)/shard_map/while/body/eval_jaxpr/ppermute | solution.py:13
  359.4 9.9 %collective-permute-done = f32[4,128,128]{2,1,0:T(8,128)S(1)} collective-permute-done((f32[4,128,128]{2,1,0:T(8,128)}, f32[4,128,128]{2,1,0:T(8,128)S(1)}, u32[]{:S(2)}, u32[]{:S(2)}) %collective-permute-start) | collective-permute-done | bytes 262176 | tf_op jit(solution)/shard_map/while/body/eval_jaxpr/ppermute | solution.py:13
  372.3 9.9 %collective-permute-done = f32[4,128,128]{2,1,0:T(8,128)S(1)} collective-permute-done((f32[4,128,128]{2,1,0:T(8,128)}, f32[4,128,128]{2,1,0:T(8,128)S(1)}, u32[]{:S(2)}, u32[]{:S(2)}) %collective-permute-start) | collective-permute-done | bytes 262176 | tf_op jit(solution)/shard_map/while/body/eval_jaxpr/ppermute | solution.py:13
  385.1 9.9 %collective-permute-done = f32[4,128,128]{2,1,0:T(8,128)S(1)} collective-permute-done((f32[4,128,128]{2,1,0:T(8,128)}, f32[4,128,128]{2,1,0:T(8,128)S(1)}, u32[]{:S(2)}, u32[]{:S(2)}) %collective-permute-start) | collective-permute-done | bytes 262176 | tf_op jit(solution)/shard_map/while/body/eval_jaxpr/ppermute | solution.py:13
  398.0 9.9 %collective-permute-done = f32[4,128,128]{2,1,0:T(8,128)S(1)} collective-permute-done((f32[4,128,128]{2,1,0:T(8,128)}, f32[4,128,128]{2,1,0:T(8,128)S(1)}, u32[]{:S(2)}, u32[]{:S(2)}) %collective-permute-start) | collective-permute-done | bytes 262176 | tf_op jit(solution)/shard_map/while/body/eval_jaxpr/ppermute | solution.py:13
  410.9 9.9 %collective-permute-done = f32[4,128,128]{2,1,0:T(8,128)S(1)} collective-permute-done((f32[4,128,128]{2,1,0:T(8,128)}, f32[4,128,128]{2,1,0:T(8,128)S(1)}, u32[]{:S(2)}, u32[]{:S(2)}) %collective-permute-start) | collective-permute-done | bytes 262176 | tf_op jit(solution)/shard_map/while/body/eval_jaxpr/ppermute | solution.py:13
  423.8 10.1 %collective-permute-done = f32[4,128,128]{2,1,0:T(8,128)S(1)} collective-permute-done((f32[4,128,128]{2,1,0:T(8,128)}, f32[4,128,128]{2,1,0:T(8,128)S(1)}, u32[]{:S(2)}, u32[]{:S(2)}) %collective-permute-start) | collective-permute-done | bytes 262176 | tf_op jit(solution)/shard_map/while/body/eval_jaxpr/ppermute | solution.py:13
  436.9 11.2 %collective-permute-done = f32[4,128,128]{2,1,0:T(8,128)S(1)} collective-permute-done((f32[4,128,128]{2,1,0:T(8,128)}, f32[4,128,128]{2,1,0:T(8,128)S(1)}, u32[]{:S(2)}, u32[]{:S(2)}) %collective-permute-start) | collective-permute-done | bytes 262176 | tf_op jit(solution)/shard_map/while/body/eval_jaxpr/ppermute | solution.py:13
  451.1 12.3 %collective-permute-done = f32[4,128,128]{2,1,0:T(8,128)S(1)} collective-permute-done((f32[4,128,128]{2,1,0:T(8,128)}, f32[4,128,128]{2,1,0:T(8,128)S(1)}, u32[]{:S(2)}, u32[]{:S(2)}) %collective-permute-start) | collective-permute-done | bytes 262176 | tf_op jit(solution)/shard_map/while/body/eval_jaxpr/ppermute | solution.py:13
  466.4 11.9 %collective-permute-done = f32[4,128,128]{2,1,0:T(8,128)S(1)} collective-permute-done((f32[4,128,128]{2,1,0:T(8,128)}, f32[4,128,128]{2,1,0:T(8,128)S(1)}, u32[]{:S(2)}, u32[]{:S(2)}) %collective-permute-start) | collective-permute-done | bytes 262176 | tf_op jit(solution)/shard_map/while/body/eval_jaxpr/ppermute | solution.py:13
  481.3 11.0 %collective-permute-done = f32[4,128,128]{2,1,0:T(8,128)S(1)} collective-permute-done((f32[4,128,128]{2,1,0:T(8,128)}, f32[4,128,128]{2,1,0:T(8,128)S(1)}, u32[]{:S(2)}, u32[]{:S(2)}) %collective-permute-start) | collective-permute-done | bytes 262176 | tf_op jit(solution)/shard_map/while/body/eval_jaxpr/ppermute | solution.py:13
  495.4 10.1 %collective-permute-done = f32[4,128,128]{2,1,0:T(8,128)S(1)} collective-permute-done((f32[4,128,128]{2,1,0:T(8,128)}, f32[4,128,128]{2,1,0:T(8,128)S(1)}, u32[]{:S(2)}, u32[]{:S(2)}) %collective-permute-start) | collective-permute-done | bytes 262176 | tf_op jit(solution)/shard_map/while/body/eval_jaxpr/ppermute | solution.py:13
  521.4 9.9 %collective-permute-done = f32[4,128,128]{2,1,0:T(8,128)S(1)} collective-permute-done((f32[4,128,128]{2,1,0:T(8,128)}, f32[4,128,128]{2,1,0:T(8,128)S(1)}, u32[]{:S(2)}, u32[]{:S(2)}) %collective-permute-start) | collective-permute-done | bytes 262176 | tf_op jit(solution)/shard_map/while/body/eval_jaxpr/ppermute | solution.py:13
  534.3 9.9 %collective-permute-done = f32[4,128,128]{2,1,0:T(8,128)S(1)} collective-permute-done((f32[4,128,128]{2,1,0:T(8,128)}, f32[4,128,128]{2,1,0:T(8,128)S(1)}, u32[]{:S(2)}, u32[]{:S(2)}) %collective-permute-start) | collective-permute-done | bytes 262176 | tf_op jit(solution)/shard_map/while/body/eval_jaxpr/ppermute | solution.py:13
  547.2 9.9 %collective-permute-done = f32[4,128,128]{2,1,0:T(8,128)S(1)} collective-permute-done((f32[4,128,128]{2,1,0:T(8,128)}, f32[4,128,128]{2,1,0:T(8,128)S(1)}, u32[]{:S(2)}, u32[]{:S(2)}) %collective-permute-start) | collective-permute-done | bytes 262176 | tf_op jit(solution)/shard_map/while/body/eval_jaxpr/ppermute | solution.py:13
  572.9 10.1 %collective-permute-done = f32[4,128,128]{2,1,0:T(8,128)S(1)} collective-permute-done((f32[4,128,128]{2,1,0:T(8,128)}, f32[4,128,128]{2,1,0:T(8,128)S(1)}, u32[]{:S(2)}, u32[]{:S(2)}) %collective-permute-start) | collective-permute-done | bytes 262176 | tf_op jit(solution)/shard_map/while/body/eval_jaxpr/ppermute | solution.py:13
  586.0 11.2 %collective-permute-done = f32[4,128,128]{2,1,0:T(8,128)S(1)} collective-permute-done((f32[4,128,128]{2,1,0:T(8,128)}, f32[4,128,128]{2,1,0:T(8,128)S(1)}, u32[]{:S(2)}, u32[]{:S(2)}) %collective-permute-start) | collective-permute-done | bytes 262176 | tf_op jit(solution)/shard_map/while/body/eval_jaxpr/ppermute | solution.py:13
  600.2 9.9 %collective-permute-done = f32[4,128,128]{2,1,0:T(8,128)S(1)} collective-permute-done((f32[4,128,128]{2,1,0:T(8,128)}, f32[4,128,128]{2,1,0:T(8,128)S(1)}, u32[]{:S(2)}, u32[]{:S(2)}) %collective-permute-start) | collective-permute-done | bytes 262176 | tf_op jit(solution)/shard_map/while/body/eval_jaxpr/ppermute | solution.py:13
  (214 shorter events, 204.6 us)
Async XLA Ops:
  6.5 30.4 %all-gather.2.cloned.1.call-start = ((), (), s32[]{:S(2)}) async-start(), calls=%async_computation.1 | async-start | bytes 1327104 | tf_op jit(solution)/shard_map/all_gather | solution.py:89
  42.6 63.2 %all-to-all-start = ((bf16[32,16,2304]{2,1,0:T(8,128)(2,1)}), bf16[32,16,2304]{2,1,0:T(8,128)(2,1)S(1)}, u32[]{:S(2)}, u32[]{:S(2)}) async-start(bf16[32,16,2304]{2,1,0:T(8,128)(2,1)} %bitcast.129), calls=%async_computation | async-start | bytes 4718592 | tf_op jit(solution)/shard_map/all_to_all | solution.py:93
  221.2 11.8 %collective-permute-start = (f32[4,128,128]{2,1,0:T(8,128)}, f32[4,128,128]{2,1,0:T(8,128)S(1)}, u32[]{:S(2)}, u32[]{:S(2)}) collective-permute-start(f32[4,128,128]{2,1,0:T(8,128)} %convolution_add_fusion.8), channel_id=1, source_target_pairs={{0,8},{8,16},{16,24},{24,32},{32,40},{40,48},{48,56},{56,64},{64,7... | collective-permute-start | bytes 786440 | tf_op jit(solution)/shard_map/while/body/eval_jaxpr/ppermute | solution.py:13
  234.1 11.8 %collective-permute-start = (f32[4,128,128]{2,1,0:T(8,128)}, f32[4,128,128]{2,1,0:T(8,128)S(1)}, u32[]{:S(2)}, u32[]{:S(2)}) collective-permute-start(f32[4,128,128]{2,1,0:T(8,128)} %convolution_add_fusion.8), channel_id=1, source_target_pairs={{0,8},{8,16},{16,24},{24,32},{32,40},{40,48},{48,56},{56,64},{64,7... | collective-permute-start | bytes 786440 | tf_op jit(solution)/shard_map/while/body/eval_jaxpr/ppermute | solution.py:13
  247.0 11.8 %collective-permute-start = (f32[4,128,128]{2,1,0:T(8,128)}, f32[4,128,128]{2,1,0:T(8,128)S(1)}, u32[]{:S(2)}, u32[]{:S(2)}) collective-permute-start(f32[4,128,128]{2,1,0:T(8,128)} %convolution_add_fusion.8), channel_id=1, source_target_pairs={{0,8},{8,16},{16,24},{24,32},{32,40},{40,48},{48,56},{56,64},{64,7... | collective-permute-start | bytes 786440 | tf_op jit(solution)/shard_map/while/body/eval_jaxpr/ppermute | solution.py:13
  259.8 11.8 %collective-permute-start = (f32[4,128,128]{2,1,0:T(8,128)}, f32[4,128,128]{2,1,0:T(8,128)S(1)}, u32[]{:S(2)}, u32[]{:S(2)}) collective-permute-start(f32[4,128,128]{2,1,0:T(8,128)} %convolution_add_fusion.8), channel_id=1, source_target_pairs={{0,8},{8,16},{16,24},{24,32},{32,40},{40,48},{48,56},{56,64},{64,7... | collective-permute-start | bytes 786440 | tf_op jit(solution)/shard_map/while/body/eval_jaxpr/ppermute | solution.py:13
  272.7 12.0 %collective-permute-start = (f32[4,128,128]{2,1,0:T(8,128)}, f32[4,128,128]{2,1,0:T(8,128)S(1)}, u32[]{:S(2)}, u32[]{:S(2)}) collective-permute-start(f32[4,128,128]{2,1,0:T(8,128)} %convolution_add_fusion.8), channel_id=1, source_target_pairs={{0,8},{8,16},{16,24},{24,32},{32,40},{40,48},{48,56},{56,64},{64,7... | collective-permute-start | bytes 786440 | tf_op jit(solution)/shard_map/while/body/eval_jaxpr/ppermute | solution.py:13
  285.8 13.1 %collective-permute-start = (f32[4,128,128]{2,1,0:T(8,128)}, f32[4,128,128]{2,1,0:T(8,128)S(1)}, u32[]{:S(2)}, u32[]{:S(2)}) collective-permute-start(f32[4,128,128]{2,1,0:T(8,128)} %convolution_add_fusion.8), channel_id=1, source_target_pairs={{0,8},{8,16},{16,24},{24,32},{32,40},{40,48},{48,56},{56,64},{64,7... | collective-permute-start | bytes 786440 | tf_op jit(solution)/shard_map/while/body/eval_jaxpr/ppermute | solution.py:13
  300.0 14.2 %collective-permute-start = (f32[4,128,128]{2,1,0:T(8,128)}, f32[4,128,128]{2,1,0:T(8,128)S(1)}, u32[]{:S(2)}, u32[]{:S(2)}) collective-permute-start(f32[4,128,128]{2,1,0:T(8,128)} %convolution_add_fusion.8), channel_id=1, source_target_pairs={{0,8},{8,16},{16,24},{24,32},{32,40},{40,48},{48,56},{56,64},{64,7... | collective-permute-start | bytes 786440 | tf_op jit(solution)/shard_map/while/body/eval_jaxpr/ppermute | solution.py:13
  315.4 13.8 %collective-permute-start = (f32[4,128,128]{2,1,0:T(8,128)}, f32[4,128,128]{2,1,0:T(8,128)S(1)}, u32[]{:S(2)}, u32[]{:S(2)}) collective-permute-start(f32[4,128,128]{2,1,0:T(8,128)} %convolution_add_fusion.8), channel_id=1, source_target_pairs={{0,8},{8,16},{16,24},{24,32},{32,40},{40,48},{48,56},{56,64},{64,7... | collective-permute-start | bytes 786440 | tf_op jit(solution)/shard_map/while/body/eval_jaxpr/ppermute | solution.py:13
  330.3 13.0 %collective-permute-start = (f32[4,128,128]{2,1,0:T(8,128)}, f32[4,128,128]{2,1,0:T(8,128)S(1)}, u32[]{:S(2)}, u32[]{:S(2)}) collective-permute-start(f32[4,128,128]{2,1,0:T(8,128)} %convolution_add_fusion.8), channel_id=1, source_target_pairs={{0,8},{8,16},{16,24},{24,32},{32,40},{40,48},{48,56},{56,64},{64,7... | collective-permute-start | bytes 786440 | tf_op jit(solution)/shard_map/while/body/eval_jaxpr/ppermute | solution.py:13
  344.3 12.0 %collective-permute-start = (f32[4,128,128]{2,1,0:T(8,128)}, f32[4,128,128]{2,1,0:T(8,128)S(1)}, u32[]{:S(2)}, u32[]{:S(2)}) collective-permute-start(f32[4,128,128]{2,1,0:T(8,128)} %convolution_add_fusion.8), channel_id=1, source_target_pairs={{0,8},{8,16},{16,24},{24,32},{32,40},{40,48},{48,56},{56,64},{64,7... | collective-permute-start | bytes 786440 | tf_op jit(solution)/shard_map/while/body/eval_jaxpr/ppermute | solution.py:13
  357.5 11.8 %collective-permute-start = (f32[4,128,128]{2,1,0:T(8,128)}, f32[4,128,128]{2,1,0:T(8,128)S(1)}, u32[]{:S(2)}, u32[]{:S(2)}) collective-permute-start(f32[4,128,128]{2,1,0:T(8,128)} %convolution_add_fusion.8), channel_id=1, source_target_pairs={{0,8},{8,16},{16,24},{24,32},{32,40},{40,48},{48,56},{56,64},{64,7... | collective-permute-start | bytes 786440 | tf_op jit(solution)/shard_map/while/body/eval_jaxpr/ppermute | solution.py:13
  370.3 11.8 %collective-permute-start = (f32[4,128,128]{2,1,0:T(8,128)}, f32[4,128,128]{2,1,0:T(8,128)S(1)}, u32[]{:S(2)}, u32[]{:S(2)}) collective-permute-start(f32[4,128,128]{2,1,0:T(8,128)} %convolution_add_fusion.8), channel_id=1, source_target_pairs={{0,8},{8,16},{16,24},{24,32},{32,40},{40,48},{48,56},{56,64},{64,7... | collective-permute-start | bytes 786440 | tf_op jit(solution)/shard_map/while/body/eval_jaxpr/ppermute | solution.py:13
  383.2 11.8 %collective-permute-start = (f32[4,128,128]{2,1,0:T(8,128)}, f32[4,128,128]{2,1,0:T(8,128)S(1)}, u32[]{:S(2)}, u32[]{:S(2)}) collective-permute-start(f32[4,128,128]{2,1,0:T(8,128)} %convolution_add_fusion.8), channel_id=1, source_target_pairs={{0,8},{8,16},{16,24},{24,32},{32,40},{40,48},{48,56},{56,64},{64,7... | collective-permute-start | bytes 786440 | tf_op jit(solution)/shard_map/while/body/eval_jaxpr/ppermute | solution.py:13
  396.1 11.8 %collective-permute-start = (f32[4,128,128]{2,1,0:T(8,128)}, f32[4,128,128]{2,1,0:T(8,128)S(1)}, u32[]{:S(2)}, u32[]{:S(2)}) collective-permute-start(f32[4,128,128]{2,1,0:T(8,128)} %convolution_add_fusion.8), channel_id=1, source_target_pairs={{0,8},{8,16},{16,24},{24,32},{32,40},{40,48},{48,56},{56,64},{64,7... | collective-permute-start | bytes 786440 | tf_op jit(solution)/shard_map/while/body/eval_jaxpr/ppermute | solution.py:13
  409.0 11.8 %collective-permute-start = (f32[4,128,128]{2,1,0:T(8,128)}, f32[4,128,128]{2,1,0:T(8,128)S(1)}, u32[]{:S(2)}, u32[]{:S(2)}) collective-permute-start(f32[4,128,128]{2,1,0:T(8,128)} %convolution_add_fusion.8), channel_id=1, source_target_pairs={{0,8},{8,16},{16,24},{24,32},{32,40},{40,48},{48,56},{56,64},{64,7... | collective-permute-start | bytes 786440 | tf_op jit(solution)/shard_map/while/body/eval_jaxpr/ppermute | solution.py:13
  421.9 12.0 %collective-permute-start = (f32[4,128,128]{2,1,0:T(8,128)}, f32[4,128,128]{2,1,0:T(8,128)S(1)}, u32[]{:S(2)}, u32[]{:S(2)}) collective-permute-start(f32[4,128,128]{2,1,0:T(8,128)} %convolution_add_fusion.8), channel_id=1, source_target_pairs={{0,8},{8,16},{16,24},{24,32},{32,40},{40,48},{48,56},{56,64},{64,7... | collective-permute-start | bytes 786440 | tf_op jit(solution)/shard_map/while/body/eval_jaxpr/ppermute | solution.py:13
  435.0 13.1 %collective-permute-start = (f32[4,128,128]{2,1,0:T(8,128)}, f32[4,128,128]{2,1,0:T(8,128)S(1)}, u32[]{:S(2)}, u32[]{:S(2)}) collective-permute-start(f32[4,128,128]{2,1,0:T(8,128)} %convolution_add_fusion.8), channel_id=1, source_target_pairs={{0,8},{8,16},{16,24},{24,32},{32,40},{40,48},{48,56},{56,64},{64,7... | collective-permute-start | bytes 786440 | tf_op jit(solution)/shard_map/while/body/eval_jaxpr/ppermute | solution.py:13
  449.2 14.2 %collective-permute-start = (f32[4,128,128]{2,1,0:T(8,128)}, f32[4,128,128]{2,1,0:T(8,128)S(1)}, u32[]{:S(2)}, u32[]{:S(2)}) collective-permute-start(f32[4,128,128]{2,1,0:T(8,128)} %convolution_add_fusion.8), channel_id=1, source_target_pairs={{0,8},{8,16},{16,24},{24,32},{32,40},{40,48},{48,56},{56,64},{64,7... | collective-permute-start | bytes 786440 | tf_op jit(solution)/shard_map/while/body/eval_jaxpr/ppermute | solution.py:13
  464.5 13.8 %collective-permute-start = (f32[4,128,128]{2,1,0:T(8,128)}, f32[4,128,128]{2,1,0:T(8,128)S(1)}, u32[]{:S(2)}, u32[]{:S(2)}) collective-permute-start(f32[4,128,128]{2,1,0:T(8,128)} %convolution_add_fusion.8), channel_id=1, source_target_pairs={{0,8},{8,16},{16,24},{24,32},{32,40},{40,48},{48,56},{56,64},{64,7... | collective-permute-start | bytes 786440 | tf_op jit(solution)/shard_map/while/body/eval_jaxpr/ppermute | solution.py:13
  479.4 13.0 %collective-permute-start = (f32[4,128,128]{2,1,0:T(8,128)}, f32[4,128,128]{2,1,0:T(8,128)S(1)}, u32[]{:S(2)}, u32[]{:S(2)}) collective-permute-start(f32[4,128,128]{2,1,0:T(8,128)} %convolution_add_fusion.8), channel_id=1, source_target_pairs={{0,8},{8,16},{16,24},{24,32},{32,40},{40,48},{48,56},{56,64},{64,7... | collective-permute-start | bytes 786440 | tf_op jit(solution)/shard_map/while/body/eval_jaxpr/ppermute | solution.py:13
  493.5 12.0 %collective-permute-start = (f32[4,128,128]{2,1,0:T(8,128)}, f32[4,128,128]{2,1,0:T(8,128)S(1)}, u32[]{:S(2)}, u32[]{:S(2)}) collective-permute-start(f32[4,128,128]{2,1,0:T(8,128)} %convolution_add_fusion.8), channel_id=1, source_target_pairs={{0,8},{8,16},{16,24},{24,32},{32,40},{40,48},{48,56},{56,64},{64,7... | collective-permute-start | bytes 786440 | tf_op jit(solution)/shard_map/while/body/eval_jaxpr/ppermute | solution.py:13
  506.6 11.8 %collective-permute-start = (f32[4,128,128]{2,1,0:T(8,128)}, f32[4,128,128]{2,1,0:T(8,128)S(1)}, u32[]{:S(2)}, u32[]{:S(2)}) collective-permute-start(f32[4,128,128]{2,1,0:T(8,128)} %convolution_add_fusion.8), channel_id=1, source_target_pairs={{0,8},{8,16},{16,24},{24,32},{32,40},{40,48},{48,56},{56,64},{64,7... | collective-permute-start | bytes 786440 | tf_op jit(solution)/shard_map/while/body/eval_jaxpr/ppermute | solution.py:13
  519.5 11.8 %collective-permute-start = (f32[4,128,128]{2,1,0:T(8,128)}, f32[4,128,128]{2,1,0:T(8,128)S(1)}, u32[]{:S(2)}, u32[]{:S(2)}) collective-permute-start(f32[4,128,128]{2,1,0:T(8,128)} %convolution_add_fusion.8), channel_id=1, source_target_pairs={{0,8},{8,16},{16,24},{24,32},{32,40},{40,48},{48,56},{56,64},{64,7... | collective-permute-start | bytes 786440 | tf_op jit(solution)/shard_map/while/body/eval_jaxpr/ppermute | solution.py:13
  532.4 11.8 %collective-permute-start = (f32[4,128,128]{2,1,0:T(8,128)}, f32[4,128,128]{2,1,0:T(8,128)S(1)}, u32[]{:S(2)}, u32[]{:S(2)}) collective-permute-start(f32[4,128,128]{2,1,0:T(8,128)} %convolution_add_fusion.8), channel_id=1, source_target_pairs={{0,8},{8,16},{16,24},{24,32},{32,40},{40,48},{48,56},{56,64},{64,7... | collective-permute-start | bytes 786440 | tf_op jit(solution)/shard_map/while/body/eval_jaxpr/ppermute | solution.py:13
  545.2 11.8 %collective-permute-start = (f32[4,128,128]{2,1,0:T(8,128)}, f32[4,128,128]{2,1,0:T(8,128)S(1)}, u32[]{:S(2)}, u32[]{:S(2)}) collective-permute-start(f32[4,128,128]{2,1,0:T(8,128)} %convolution_add_fusion.8), channel_id=1, source_target_pairs={{0,8},{8,16},{16,24},{24,32},{32,40},{40,48},{48,56},{56,64},{64,7... | collective-permute-start | bytes 786440 | tf_op jit(solution)/shard_map/while/body/eval_jaxpr/ppermute | solution.py:13
  558.1 11.8 %collective-permute-start = (f32[4,128,128]{2,1,0:T(8,128)}, f32[4,128,128]{2,1,0:T(8,128)S(1)}, u32[]{:S(2)}, u32[]{:S(2)}) collective-permute-start(f32[4,128,128]{2,1,0:T(8,128)} %convolution_add_fusion.8), channel_id=1, source_target_pairs={{0,8},{8,16},{16,24},{24,32},{32,40},{40,48},{48,56},{56,64},{64,7... | collective-permute-start | bytes 786440 | tf_op jit(solution)/shard_map/while/body/eval_jaxpr/ppermute | solution.py:13
  571.0 12.0 %collective-permute-start = (f32[4,128,128]{2,1,0:T(8,128)}, f32[4,128,128]{2,1,0:T(8,128)S(1)}, u32[]{:S(2)}, u32[]{:S(2)}) collective-permute-start(f32[4,128,128]{2,1,0:T(8,128)} %convolution_add_fusion.8), channel_id=1, source_target_pairs={{0,8},{8,16},{16,24},{24,32},{32,40},{40,48},{48,56},{56,64},{64,7... | collective-permute-start | bytes 786440 | tf_op jit(solution)/shard_map/while/body/eval_jaxpr/ppermute | solution.py:13
  584.1 13.1 %collective-permute-start = (f32[4,128,128]{2,1,0:T(8,128)}, f32[4,128,128]{2,1,0:T(8,128)S(1)}, u32[]{:S(2)}, u32[]{:S(2)}) collective-permute-start(f32[4,128,128]{2,1,0:T(8,128)} %convolution_add_fusion.8), channel_id=1, source_target_pairs={{0,8},{8,16},{16,24},{24,32},{32,40},{40,48},{48,56},{56,64},{64,7... | collective-permute-start | bytes 786440 | tf_op jit(solution)/shard_map/while/body/eval_jaxpr/ppermute | solution.py:13
  598.3 11.8 %collective-permute-start = (f32[4,128,128]{2,1,0:T(8,128)}, f32[4,128,128]{2,1,0:T(8,128)S(1)}, u32[]{:S(2)}, u32[]{:S(2)}) collective-permute-start(f32[4,128,128]{2,1,0:T(8,128)} %convolution_add_fusion.8), channel_id=1, source_target_pairs={{0,8},{8,16},{16,24},{24,32},{32,40},{40,48},{48,56},{56,64},{64,7... | collective-permute-start | bytes 786440 | tf_op jit(solution)/shard_map/while/body/eval_jaxpr/ppermute | solution.py:13
  611.2 11.8 %collective-permute-start = (f32[4,128,128]{2,1,0:T(8,128)}, f32[4,128,128]{2,1,0:T(8,128)S(1)}, u32[]{:S(2)}, u32[]{:S(2)}) collective-permute-start(f32[4,128,128]{2,1,0:T(8,128)} %convolution_add_fusion.8), channel_id=1, source_target_pairs={{0,8},{8,16},{16,24},{24,32},{32,40},{40,48},{48,56},{56,64},{64,7... | collective-permute-start | bytes 786440 | tf_op jit(solution)/shard_map/while/body/eval_jaxpr/ppermute | solution.py:13
  (23 other events, 232.9 us)
Sparse Core Ops, SparseCore 0:
  9.2 27.7 all-gather.1
where the time goes:
time: 658 us; the launch traced here: 656 us
  waiting for transfers between devices  405 us (62%)
  other arithmetic  91.9 us (14%)
  starting transfers between devices  71.1 us (11%)
  matrix products  60.1 us (9%)
  between operations  14 us (2%)
  local copies, waits for them, and re-layouts  13.5 us (2%)
    ppermute x32, waiting for transfers between devices, shifted_2(): return lax.ppermute(block, axis, route)  326 us
    another operation x4, other arithmetic, span_pieces(): jax.scipy.linalg.solve_triangular(eye_small + strict_part, right_side, lo...  80.6 us
    ppermute x32, starting transfers between devices, shifted_2(): return lax.ppermute(block, axis, route)  61.2 us
    all_to_all x1, waiting for transfers between devices, on_device(): lax.all_to_all(buffer_rows, 'ctx', split_axis=0, concat_axis=0, tiled=True)  49 us
    dot_general x43, matrix products, compose_heads(): jnp.einsum('hij,hjk->hik', left_maps, right_maps, precision=lax.Precision...  38.7 us
    all_gather x1, waiting for transfers between devices, on_device(): full_rows = lax.all_gather(hidden, 'head', axis=1, tiled=True)  29 us
  transfers between devices with their start and end apart: 34, of which 34 were waited for; matrix products, arithmetic and copies ran while one was open for 1% of the time, Pallas kernels for 0%

commit v1 on v0

v1 whole, which is shorter than its diff:
```python
import functools

import jax
import jax.numpy as jnp
from jax import lax
from jax.experimental import pallas as pl
from jax.experimental.pallas import tpu as pltpu
from jax.sharding import PartitionSpec as P

CONV = 4
SPAN = 64
RIM = 16
X_SIZE = 4
CORES = 2
MESH = pl.DeviceIdType.MESH
F32 = jnp.float32
BF16 = jnp.bfloat16
VMEM = pl.BlockSpec(memory_space=pltpu.VMEM)
SMEM = pl.BlockSpec(memory_space=pltpu.SMEM)
ANY = pl.BlockSpec(memory_space=pl.ANY)

NN = (((1,), (0,)), ((), ()))
NT = (((1,), (1,)), ((), ()))
TN = (((0,), (0,)), ((), ()))


def mm(a, b, dims=NN):
    return lax.dot_general(a, b, dims, preferred_element_type=F32)


def split(v):
    high = v.astype(BF16)
    return high, (v - high.astype(F32)).astype(BF16)


def mm3(a, b, dims=NN):
    return mm(a[0], b[0], dims) + (mm(a[0], b[1], dims) + mm(a[1], b[0], dims))


def gather_kernel(
    slot_ref, src_ref, hidden_ref, wqkv_hbm, wdown_hbm, wbeta_hbm,
    ext_ref, low_ref, beta_ref,
    send_buf, landed, shards, w_qkv, w_down, w_beta, acc, acc_low, acc_beta, rim_buf,
    w_sem, s_sem, r_sem, hs_sem, hf_sem, hr_sem, rim_sem,
):
    n_ctx = lax.axis_size("ctx")
    n_head = lax.axis_size("head")
    n_y = n_head // CORES
    me = lax.axis_index("ctx")
    head = lax.axis_index("head")
    y = head // CORES
    core = head % CORES
    sibling = y * CORES + (1 - core)
    rows, width = hidden_ref.shape
    slots = send_buf.shape[0]
    cap = slots // n_ctx

    weights = [
        pltpu.make_async_copy(wqkv_hbm, w_qkv, w_sem.at[0]),
        pltpu.make_async_copy(wdown_hbm, w_down, w_sem.at[1]),
        pltpu.make_async_copy(wbeta_hbm, w_beta, w_sem.at[2]),
    ]
    for copy in weights:
        copy.start()

    barrier = pltpu.get_barrier_semaphore()

    def greet(k, carry):
        pl.semaphore_signal(
            barrier, inc=1, device_id={"ctx": lax.rem(me + k, n_ctx), "head": head}, device_id_type=MESH
        )
        return carry

    lax.fori_loop(1, n_ctx, greet, 0)
    for dy in range(1, n_y):
        other = lax.rem(y + dy, n_y) * CORES + core
        pl.semaphore_signal(barrier, inc=1, device_id={"ctx": me, "head": other}, device_id_type=MESH)
    pl.semaphore_signal(barrier, inc=1, device_id={"ctx": me, "head": sibling}, device_id_type=MESH)

    slot_ids = lax.broadcasted_iota(jnp.int32, (slots, rows), 0)
    place = (slot_ids == slot_ref[...]).astype(F32).astype(BF16)
    send_buf[...] = mm(place, hidden_ref[...]).astype(BF16)
    pick = (slot_ids == src_ref[...]).astype(F32).astype(BF16)

    pl.semaphore_wait(barrier, n_ctx - 1 + n_y)

    def piece(buf, index):
        return buf.at[pl.ds(pl.multiple_of(index * cap, cap), cap), :]

    def send(k, carry):
        to = lax.rem(me + k, n_ctx)
        pltpu.make_async_remote_copy(
            src_ref=piece(send_buf, to), dst_ref=piece(landed, me),
            send_sem=s_sem.at[to], recv_sem=r_sem.at[me],
            device_id={"ctx": to, "head": head}, device_id_type=MESH,
        ).start()
        return carry

    lax.fori_loop(1, n_ctx, send, 0)
    own = pl.ds(pl.multiple_of(me * cap, cap), cap)
    landed[own, :] = send_buf[own, :]

    def arrive(k, carry):
        frm = lax.rem(me + k, n_ctx)
        pltpu.make_async_remote_copy(
            src_ref=piece(send_buf, frm), dst_ref=piece(landed, frm),
            send_sem=s_sem.at[frm], recv_sem=r_sem.at[frm],
            device_id={"ctx": frm, "head": head}, device_id_type=MESH,
        ).wait_recv()
        return carry

    lax.fori_loop(1, n_ctx, arrive, 0)
    shards[head] = mm(pick, landed[...], TN).astype(BF16)

    def shard_copy(index, to, send_sem):
        return pltpu.make_async_remote_copy(
            src_ref=shards.at[index], dst_ref=shards.at[index],
            send_sem=send_sem, recv_sem=hr_sem.at[index],
            device_id={"ctx": me, "head": to}, device_id_type=MESH,
        )

    outgoing = [shard_copy(head, lax.rem(y + dy, n_y) * CORES + core, hs_sem.at[dy]) for dy in range(1, n_y)]
    outgoing.append(shard_copy(head, sibling, hs_sem.at[0]))
    for copy in outgoing:
        copy.start()
    for copy in weights:
        copy.wait()

    def multiply(index, first=False):
        part = shards[index]
        chunk = pl.ds(pl.multiple_of(index * width, 16), width)
        products = [(acc, j, mm(part, w_qkv[j, chunk, :])) for j in range(3)]
        for ref, j, value in products:
            ref[j] = value if first else ref[j] + value
        low = mm(part, w_down[chunk, :])
        beta = mm(part, w_beta[chunk, :])
        acc_low[...] = low if first else acc_low[...] + low
        acc_beta[...] = beta if first else acc_beta[...] + beta

    multiply(head, True)
    shard_copy(sibling, sibling, hs_sem.at[0]).wait_recv()
    multiply(sibling)
    order = [dy for dy in (1, n_y - 1) if 0 < dy < n_y]
    order = sorted(set(order)) + [dy for dy in range(1, n_y) if dy not in order]
    pending = []
    for dy in order:
        index = lax.rem(y + dy, n_y) * CORES + core
        shard_copy(index, sibling, hf_sem.at[dy]).wait_recv()
        forward = shard_copy(index, sibling, hf_sem.at[dy])
        forward.start()
        outgoing.append(forward)
        multiply(index)
        pending.append(lax.rem(y + dy, n_y) * CORES + (1 - core))
    for index in pending:
        shard_copy(index, sibling, hs_sem.at[0]).wait_recv()
        multiply(index)

    columns = acc.shape[2]
    for j in range(3):
        ext_ref[RIM:, j * columns : (j + 1) * columns] = acc[j].astype(BF16)
    rim = pltpu.make_async_remote_copy(
        src_ref=ext_ref.at[pl.ds(rows, RIM), :], dst_ref=rim_buf,
        send_sem=rim_sem.at[0], recv_sem=rim_sem.at[1],
        device_id={"ctx": lax.rem(me + 1, n_ctx), "head": head}, device_id_type=MESH,
    )
    rim.start()
    low_ref[...] = acc_low[...].astype(BF16)
    beta_ref[...] = acc_beta[...]
    for copy in outgoing:
        copy.wait_send()

    def sent(k, carry):
        to = lax.rem(me + k, n_ctx)
        pltpu.make_async_remote_copy(
            src_ref=piece(send_buf, to), dst_ref=piece(landed, me),
            send_sem=s_sem.at[to], recv_sem=r_sem.at[me],
            device_id={"ctx": to, "head": head}, device_id_type=MESH,
        ).wait_send()
        return carry

    lax.fori_loop(1, n_ctx, sent, 0)
    rim.wait()
    ext_ref[:RIM, :] = rim_buf[...]


def gather_and_project(hidden, qkv_weight, gate_down, w_beta, send_slot, gather_src):
    rows, width = hidden.shape
    _, features, columns = qkv_weight.shape
    n_ctx, n_head = lax.axis_size("ctx"), lax.axis_size("head")
    slots = 2 * rows
    rank, betas = gate_down.shape[1], w_beta.shape[1]
    return pl.pallas_call(
        gather_kernel,
        out_shape=(
            jax.ShapeDtypeStruct((RIM + rows, 3 * columns), BF16),
            jax.ShapeDtypeStruct((rows, rank), BF16),
            jax.ShapeDtypeStruct((rows, betas), F32),
        ),
        in_specs=[VMEM, VMEM, VMEM, ANY, ANY, ANY],
        out_specs=(VMEM, VMEM, VMEM),
        scratch_shapes=[
            pltpu.VMEM((slots, width), BF16),
            pltpu.VMEM((slots, width), BF16),
            pltpu.VMEM((n_head, rows, width), BF16),
            pltpu.VMEM((3, features, columns), BF16),
            pltpu.VMEM((features, rank), BF16),
            pltpu.VMEM((features, betas), BF16),
            pltpu.VMEM((3, rows, columns), F32),
            pltpu.VMEM((rows, rank), F32),
            pltpu.VMEM((rows, betas), F32),
            pltpu.VMEM((RIM, 3 * columns), BF16),
            pltpu.SemaphoreType.DMA((3,)),
            pltpu.SemaphoreType.DMA((n_ctx,)),
            pltpu.SemaphoreType.DMA((n_ctx,)),
            pltpu.SemaphoreType.DMA((n_head // CORES,)),
            pltpu.SemaphoreType.DMA((n_head // CORES,)),
            pltpu.SemaphoreType.DMA((n_head,)),
            pltpu.SemaphoreType.DMA((2,)),
        ],
        compiler_params=pltpu.CompilerParams(
            collective_id=0, has_side_effects=True, vmem_limit_bytes=48 * 1024 * 1024
        ),
        name="gather_project",
    )(send_slot.reshape(1, rows), gather_src.reshape(1, rows), hidden, qkv_weight, gate_down, w_beta)


def chunk_pieces(
    lengths_ref, rate_ref, ext_ref, low_ref, beta_ref, conv_ref, up_ref, bias_ref,
    ab_ref, local_ref, lift_ref, base,
):
    rows = low_ref.shape[0]
    channels = local_ref.shape[2]
    heads = local_ref.shape[0]
    columns = heads * channels
    blocks = rows // SPAN

    ends, total = [], 0
    for i in range(lengths_ref.shape[0]):
        total = total + lengths_ref[i]
        ends.append(total)

    def doc_of(positions):
        ended = sum((positions >= end).astype(jnp.int32) for end in ends)
        return jnp.where(positions < 0, -1, ended)

    pos = base + lax.broadcasted_iota(jnp.int32, (rows, channels), 0)
    doc = doc_of(pos)
    valid = [None] + [(doc_of(pos - shift) == doc).astype(F32) for shift in range(1, CONV)]
    before = doc_of(jnp.zeros((1, channels), jnp.int32) + (base - 1))
    final = doc_of(jnp.zeros((1, channels), jnp.int32) + (base + rows - 1))
    first_doc = (doc == before).astype(F32)
    last_doc = (doc == final).astype(F32)
    carry = (final == before).astype(F32)

    row = lax.broadcasted_iota(jnp.int32, (rows, rows), 0)
    col = lax.broadcasted_iota(jnp.int32, (rows, rows), 1)
    same = doc_of(base + row) == doc_of(base + col)
    strict = (row > col) & same
    inclusive = (row >= col) & same
    apart = row ^ col
    running = ((row >= col) & (apart < SPAN)).astype(F32).astype(BF16)
    eye = (row == col).astype(F32)
    eye_channels = (
        lax.broadcasted_iota(jnp.int32, (channels, channels), 0)
        == lax.broadcasted_iota(jnp.int32, (channels, channels), 1)
    ).astype(F32)

    low = low_ref[...]
    betas = 1.0 / (1.0 + jnp.exp(-beta_ref[...]))

    def activated(j, h):
        at = j * columns + h * channels
        values = ext_ref[:, at : at + channels].astype(F32)
        total = None
        for tap in range(CONV):
            shift = CONV - 1 - tap
            weight = conv_ref[tap, j : j + 1, h * channels : (h + 1) * channels]
            part = weight * values[RIM - shift : RIM - shift + rows]
            if shift:
                part = part * valid[shift]
            total = part if total is None else total + part
        return total / (1.0 + jnp.exp(-total))

    def unit(values):
        return values * lax.rsqrt(jnp.sum(values * values, axis=-1, keepdims=True) + 1e-06)

    for h in range(heads):
        lanes = slice(h * channels, (h + 1) * channels)
        query = unit(activated(0, h)) * channels ** (-0.5)
        key = unit(activated(1, h))
        value = activated(2, h)
        drive = mm(low, up_ref[:, lanes]) + bias_ref[:, lanes]
        soft = jnp.maximum(drive, 0.0) + jnp.log1p(jnp.exp(-jnp.abs(drive)))
        rate = jnp.exp(jnp.full((1, channels), rate_ref[h], F32))
        decay = -rate * soft
        d_high, d_rest = split(decay)
        d_mid = d_rest
        d_low = (decay - d_high.astype(F32) - d_mid.astype(F32)).astype(BF16)
        cum = mm(running, d_high) + (mm(running, d_mid) + mm(running, d_low))
        strength = jnp.broadcast_to(betas[:, h : h + 1], (rows, channels))

        grow = jnp.exp(cum)
        key_up = key * grow
        query_up = query * grow
        key_down = key * jnp.exp(-cum)
        lasts = [cum[(b + 1) * SPAN - 1 : (b + 1) * SPAN] for b in range(blocks)]
        part_of = lambda v, b: v[b * SPAN : (b + 1) * SPAN]
        key_tail = [part_of(key, b) * jnp.exp(lasts[b] - part_of(cum, b)) for b in range(blocks)]

        mixes, scores = [], []
        for i in range(blocks):
            cols = []
            for b in range(blocks):
                if b < i:
                    between = sum(lasts[b + 1 : i], jnp.zeros_like(lasts[0]))
                    cols.append(key_tail[b] * jnp.exp(between))
                elif b == i:
                    cols.append(part_of(key_down, b))
                else:
                    cols.append(jnp.zeros((SPAN, channels), F32))
            left = split(jnp.concatenate([part_of(key_up, i), part_of(query_up, i)], axis=0))
            product = mm3(left, split(jnp.concatenate(cols, axis=0)), NT)
            mixes.append(product[:SPAN])
            scores.append(product[SPAN:])
        strength_wide = jnp.broadcast_to(betas[:, h : h + 1], (rows, rows))
        lower = jnp.where(strict, strength_wide * jnp.concatenate(mixes, axis=0), 0.0)
        score = jnp.where(inclusive, jnp.concatenate(scores, axis=0), 0.0)

        small = jnp.where(apart < 8, lower, 0.0)
        power = split(small)
        square = mm3(power, power)
        power = split(square)
        inverse = eye - small
        inverse = inverse + mm3(split(inverse), power)
        fourth = mm3(power, power)
        inverse = inverse + mm3(split(inverse), split(fourth))
        size = 8
        while size < rows:
            off = jnp.where((apart >= size) & (apart < 2 * size), lower, 0.0)
            parts = split(inverse)
            inverse = inverse - mm3(parts, split(mm3(split(off), parts)))
            size *= 2

        prefix = jnp.zeros_like(lasts[0])
        ups, tails, q_ups = [], [], []
        for b in range(blocks):
            scale = jnp.exp(prefix)
            ups.append(part_of(key_up, b) * scale)
            q_ups.append(part_of(query_up, b) * scale)
            prefix = prefix + lasts[b]
            tails.append(key_tail[b] * jnp.exp(sum(lasts[b + 1 :], jnp.zeros_like(lasts[0]))))
        key_full = jnp.concatenate(ups, axis=0) * first_doc
        query_full = jnp.concatenate(q_ups, axis=0) * first_doc
        tail = jnp.concatenate(tails, axis=0) * last_doc
        right = jnp.concatenate([strength * key_full, strength * value], axis=1)
        solved = split(mm3(split(inverse), split(right)))
        summary = mm3(split(tail), solved, TN)
        keep = carry * jnp.exp(prefix)
        ab_ref[h, :, :channels] = keep * eye_channels - summary[:, :channels]
        ab_ref[h, :, channels:] = summary[:, channels:]
        combined = mm3(split(score), solved)
        lift_ref[h] = query_full - combined[:, :channels]
        local_ref[h] = combined[:, channels:]


def chunk_kernel(base_ref, *refs):
    chunk_pieces(*refs, base_ref[0])


def delta_chunk(ext, low, beta, conv_weight, gate_up, a_log, dt_bias, prompt_lengths, base, channels):
    rows = low.shape[0]
    heads = a_log.shape[0]
    return pl.pallas_call(
        chunk_kernel,
        out_shape=(
            jax.ShapeDtypeStruct((heads, channels, 2 * channels), F32),
            jax.ShapeDtypeStruct((heads, rows, channels), F32),
            jax.ShapeDtypeStruct((heads, rows, channels), F32),
        ),
        in_specs=[SMEM, SMEM, SMEM] + [VMEM] * 6,
        out_specs=(VMEM, VMEM, VMEM),
        compiler_params=pltpu.CompilerParams(vmem_limit_bytes=48 * 1024 * 1024),
        name="delta_chunk",
    )(base, prompt_lengths, a_log, ext, low, beta, conv_weight, gate_up, dt_bias.reshape(1, -1))


def relay_kernel(
    ab_ref, local_ref, lift_ref, gain_ref, out_ref,
    maps, passed, arrived, entry_out, entry,
    xs_sem, xr_sem, c_sem, bs_sem, br_sem,
):
    n_z = lax.axis_size("ctx") // X_SIZE
    me = lax.axis_index("ctx")
    head = lax.axis_index("head")
    z, x = me // X_SIZE, me % X_SIZE
    heads, rows, channels = local_ref.shape

    def at(ctx):
        return {"ctx": ctx, "head": head}

    barrier = pltpu.get_barrier_semaphore()
    for dx in range(1, X_SIZE):
        pl.semaphore_signal(
            barrier, inc=1, device_id=at(z * X_SIZE + lax.rem(x + dx, X_SIZE)), device_id_type=MESH
        )

    @pl.when(z > 0)
    def _():
        pl.semaphore_signal(barrier, inc=1, device_id=at(me - X_SIZE), device_id_type=MESH)

    @pl.when(z < n_z - 1)
    def _():
        pl.semaphore_signal(barrier, inc=1, device_id=at(me + X_SIZE), device_id_type=MESH)

    greeted = X_SIZE - 1 + (z > 0).astype(jnp.int32) + (z < n_z - 1).astype(jnp.int32)
    pl.semaphore_wait(barrier, greeted)

    def map_copy(dx):
        to = lax.rem(x + dx, X_SIZE)
        return pltpu.make_async_remote_copy(
            src_ref=ab_ref.at[to], dst_ref=maps.at[x],
            send_sem=xs_sem.at[dx], recv_sem=xr_sem.at[x],
            device_id=at(z * X_SIZE + to), device_id_type=MESH,
        )

    copies = [map_copy(dx) for dx in range(1, X_SIZE)]
    for copy in copies:
        copy.start()
    maps[x] = ab_ref[x]
    for dx in range(1, X_SIZE):
        frm = lax.rem(x + dx, X_SIZE)
        pltpu.make_async_remote_copy(
            src_ref=ab_ref.at[frm], dst_ref=maps.at[frm],
            send_sem=xs_sem.at[dx], recv_sem=xr_sem.at[frm],
            device_id=at(z * X_SIZE + frm), device_id_type=MESH,
        ).wait_recv()

    whole = maps[0]
    prefixes = [whole]
    for j in range(1, X_SIZE):
        step = maps[j]
        product = mm3(split(step[:, :channels]), split(whole))
        whole = jnp.concatenate([product[:, :channels], product[:, channels:] + step[:, channels:]], axis=1)
        prefixes.append(whole)
    group_map = split(whole[:, :channels])
    group_feed = whole[:, channels:]

    chain = pltpu.make_async_remote_copy(
        src_ref=passed, dst_ref=arrived, send_sem=c_sem.at[0], recv_sem=c_sem.at[1],
        device_id=at(lax.rem(me + X_SIZE, n_z * X_SIZE)), device_id_type=MESH,
    )

    @pl.when(z == 0)
    def _():
        arrived[...] = jnp.zeros_like(arrived)

    @pl.when(z > 0)
    def _():
        chain.wait_recv()

    state = arrived[...]
    state_parts = split(state)
    passed[...] = mm3(group_map, state_parts) + group_feed

    @pl.when(z < n_z - 1)
    def _():
        chain.start()

    entry_out[0] = state
    for j in range(1, X_SIZE):
        before = prefixes[j - 1]
        entry_out[j] = mm3(split(before[:, :channels]), state_parts) + before[:, channels:]

    def entry_copy(dx):
        to = lax.rem(x + dx, X_SIZE)
        return pltpu.make_async_remote_copy(
            src_ref=entry_out.at[to], dst_ref=entry.at[x],
            send_sem=bs_sem.at[dx], recv_sem=br_sem.at[x],
            device_id=at(z * X_SIZE + to), device_id_type=MESH,
        )

    returns = [entry_copy(dx) for dx in range(1, X_SIZE)]
    for copy in returns:
        copy.start()
    entry[x] = entry_out[x]
    for dx in range(1, X_SIZE):
        frm = lax.rem(x + dx, X_SIZE)
        pltpu.make_async_remote_copy(
            src_ref=entry_out.at[frm], dst_ref=entry.at[frm],
            send_sem=bs_sem.at[dx], recv_sem=br_sem.at[frm],
            device_id=at(z * X_SIZE + frm), device_id_type=MESH,
        ).wait_recv()

    for h in range(heads):
        result = local_ref[h] + mm3(split(lift_ref[h]), split(entry[h]))
        mean = jnp.mean(result * result, axis=-1, keepdims=True)
        scaled = result * lax.rsqrt(mean + 1e-05) * gain_ref[...]
        out_ref[:, h * channels : (h + 1) * channels] = scaled.astype(BF16)

    for copy in copies + returns:
        copy.wait_send()

    @pl.when(z < n_z - 1)
    def _():
        chain.wait_send()


def relay(ab, local, lift, norm_gain):
    heads, rows, channels = local.shape
    state = (channels, channels)
    return pl.pallas_call(
        relay_kernel,
        out_shape=jax.ShapeDtypeStruct((rows, heads * channels), BF16),
        in_specs=[VMEM] * 4,
        out_specs=VMEM,
        scratch_shapes=[
            pltpu.VMEM((X_SIZE, channels, 2 * channels), F32),
            pltpu.VMEM(state, F32),
            pltpu.VMEM(state, F32),
            pltpu.VMEM((X_SIZE,) + state, F32),
            pltpu.VMEM((X_SIZE,) + state, F32),
            pltpu.SemaphoreType.DMA((X_SIZE,)),
            pltpu.SemaphoreType.DMA((X_SIZE,)),
            pltpu.SemaphoreType.DMA((2,)),
            pltpu.SemaphoreType.DMA((X_SIZE,)),
            pltpu.SemaphoreType.DMA((X_SIZE,)),
        ],
        compiler_params=pltpu.CompilerParams(
            collective_id=1, has_side_effects=True, vmem_limit_bytes=32 * 1024 * 1024
        ),
        name="relay",
    )(ab, local, lift, norm_gain.reshape(1, channels))


def on_device(
    hidden, qkv_weight, conv_weight, w_beta, gate_down, gate_up,
    a_log, dt_bias, norm_gain, prompt_lengths, send_slot, gather_src,
):
    rows = send_slot.shape[0]
    channels = norm_gain.shape[0]
    ext, low, beta = gather_and_project(hidden, qkv_weight, gate_down, w_beta, send_slot, gather_src)
    base = (lax.axis_index("ctx") * rows).astype(jnp.int32).reshape(1)
    ab, local, lift = delta_chunk(
        ext, low, beta, conv_weight, gate_up, a_log, dt_bias, prompt_lengths, base, channels
    )
    return relay(ab, local, lift, norm_gain)


def solution(mesh):
    placed = (
        P("ctx", "head"),
        P(None, None, "head"),
        P(None, None, "head"),
        P(None, "head"),
        P(),
        P(None, "head"),
        P("head"),
        P("head"),
        P(),
        P(),
        P("ctx"),
        P("ctx"),
    )
    return jax.shard_map(
        on_device, mesh=mesh, in_specs=placed, out_specs=P("ctx", "head"), check_vma=False
    )
```

time: 658 us -> 108 us (0.16)
  the two profiles are of different devices: /device:TPU:128 before, /device:TPU:224 now
where the time goes in v1:
time: 108 us; the launch traced here: 107 us
  Pallas kernels  101 us (94%)
  local copies, waits for them, and re-layouts  6.1 us (6%)
    pallas_call x1, Pallas kernels, relay(): pl.pallas_call(relay_kernel, out_shape=jax.ShapeDtypeStruct((rows, heads...  40.7 us
    pallas_call x1, Pallas kernels, gather_and_project(): pl.pallas_call(gather_kernel, out_shape=(jax.ShapeDtypeStruct((RIM + rows...  36.7 us
    pallas_call x1, Pallas kernels, delta_chunk(): pl.pallas_call(chunk_kernel, out_shape=(jax.ShapeDtypeStruct((heads, chan...  23.7 us
    unnamed x20, local copies, waits for them, and re-layouts  6.1 us

profile of v1, /device:TPU:224, one launch (start us, length us, event | category | flops | bytes accessed | tf_op | source)
XLA Modules:
  0.0 107.4 jit_solution(7740592975022320894)
XLA Ops:
  0.0 0.0 copy-start.5
  0.0 0.0 copy-start.7
  0.0 0.0 copy-start.2
  0.0 0.0 copy-start.6
  0.0 0.0 copy-start.1
  0.0 0.8 copy.15.refs_5_
  0.9 1.1 %copy.13.hidden_ref = bf16[256,288]{1,0:T(8,128)(2,1)S(1)} copy(bf16[256,288]{0,1:T(8,128)(2,1)} %param.12) | data formatting | bytes 294912 | tf_op args[0]
  1.9 1.1 copy.14.wbeta_hbm
  3.0 0.0 copy-start
  3.0 1.1 copy-done
  4.1 0.0 copy-start.3
  4.1 0.7 copy-done.3
  4.7 0.0 copy-start.4
  4.7 0.7 copy-done.4
  5.4 36.7 %gather_project.1 = (bf16[272,1536]{1,0:T(8,128)(2,1)S(1)}, bf16[256,128]{1,0:T(8,128)(2,1)S(1)}, f32[256,4]{1,0:T(8,128)S(1)}) custom-call(s32[1,256]{1,0:T(1,128)S(1)} %bitcast.6, s32[1,256]{1,0:T(1,128)S(1)} %bitcast.7, bf16[256,288]{1,0:T(8,128)(2,1)S(1)} %copy.13.hidden_ref, bf16[3,2304,512]{2,1,0:T(8,128)(2,1)} %wqkv_hbm.1, ...), custom_call_target="tpu_custom_call" | custom-call | tf_op jit(solution)/shard_map/gather_project/pallas_call | solution.py:192
  42.2 0.0 copy-done.5
  42.2 0.0 copy-done.2
  42.2 0.0 copy-done.6
  42.2 0.0 copy-done.1
  42.2 23.7 %delta_chunk.1 = (f32[4,128,256]{2,1,0:T(8,128)S(1)}, f32[4,256,128]{2,1,0:T(8,128)S(1)}, f32[4,256,128]{2,1,0:T(8,128)S(1)}) custom-call(s32[1]{0:T(128)} %bitcast.base_ref, s32[4]{0:T(128)S(1)} %copy-done.5, f32[4]{0:T(128)S(1)} %copy-done.6, bf16[272,1536]{1,0:T(8,128)(2,1)S(1)} %get-tuple-element.11.refs_2_, ...), custom_call_target="tpu_custom_call" | custom-call | tf_op jit(solution)/shard_map/delta_chunk/pallas_call | solution.py:373
  65.9 0.0 copy-done.7
  66.0 40.7 %relay.1 = bf16[256,512]{1,0:T(8,128)(2,1)S(1)} custom-call(f32[4,128,256]{2,1,0:T(8,128)S(1)} %get-tuple-element.14.ab_ref, f32[4,256,128]{2,1,0:T(8,128)S(1)} %get-tuple-element.15.local_ref, f32[4,256,128]{2,1,0:T(8,128)S(1)} %get-tuple-element.16.lift_ref, f32[1,128]{1,0:T(1,128)S(1)} %bitcast.8), custom_call_target="tpu_custom_call" | custom-call | tf_op jit(solution)/shard_map/relay/pallas_call | solution.py:511
  106.7 0.7 copy.17
Async XLA Ops:
  0.0 42.2 %copy-start.5 = (s32[4]{0:T(128)S(1)}, s32[4]{0:T(128)}, u32[]{:S(2)}) copy-start(s32[4]{0:T(128)} %refs_0_.1) | copy-start | bytes 52
  0.0 65.9 %copy-start.7 = (f32[128]{0:T(128)S(1)}, f32[128]{0:T(128)}, u32[]{:S(2)}) copy-start(f32[128]{0:T(128)} %param.20) | copy-start | bytes 1540
  0.0 42.2 %copy-start.2 = (f32[512]{0:T(512)S(1)}, f32[512]{0:T(512)}, u32[]{:S(2)}) copy-start(f32[512]{0:T(512)} %param.19) | copy-start | bytes 6148
  0.0 42.2 %copy-start.6 = (f32[4]{0:T(128)S(1)}, f32[4]{0:T(128)}, u32[]{:S(2)}) copy-start(f32[4]{0:T(128)} %refs_1_.1) | copy-start | bytes 52
  0.0 42.2 %copy-start.1 = (bf16[128,512]{1,0:T(8,128)(2,1)S(1)}, bf16[128,512]{1,0:T(8,128)(2,1)}, u32[]{:S(2)}) copy-start(bf16[128,512]{1,0:T(8,128)(2,1)} %refs_6_.1) | copy-start | bytes 393220
  3.0 1.1 copy-start
  4.1 0.7 copy-start.3
  4.7 0.7 copy-start.4

commit v2 on v1

v2 whole, which is shorter than its diff:
```python
import functools

import jax
import jax.numpy as jnp
from jax import lax
from jax.experimental import pallas as pl
from jax.experimental.pallas import tpu as pltpu
from jax.sharding import PartitionSpec as P

CONV = 4
SPAN = 64
RIM = 8
X_SIZE = 4
CORES = 2
GROUP = 8
MESH = pl.DeviceIdType.MESH
F32 = jnp.float32
BF16 = jnp.bfloat16
VMEM = pl.BlockSpec(memory_space=pltpu.VMEM)
SMEM = pl.BlockSpec(memory_space=pltpu.SMEM)
HBM = pl.BlockSpec(memory_space=pltpu.HBM)

NN = (((1,), (0,)), ((), ()))
NT = (((1,), (1,)), ((), ()))
TN = (((0,), (0,)), ((), ()))


def mm(a, b, dims=NN):
    return lax.dot_general(a, b, dims, preferred_element_type=F32)


def split(v):
    high = v.astype(BF16)
    return high, (v - high.astype(F32)).astype(BF16)


def mm3(a, b, dims=NN):
    return mm(a[0], b[0], dims) + (mm(a[0], b[1], dims) + mm(a[1], b[0], dims))


def mm3_narrow(a, b, dims=NN):
    axis = dims[0][1][0]
    wide = mm(jnp.concatenate(a, axis=1), jnp.concatenate([b[0], b[0]], axis=axis), dims)
    return wide + mm(a[0], b[1], dims)


def gather_kernel(
    slot_hbm, src_hbm, hidden_hbm, wqkv_hbm, wdown_hbm, wbeta_hbm,
    ext_ref, low_ref, beta_ref,
    slot_buf, src_buf, hidden_buf, wbeta_buf,
    send_buf, landed, shards, w_qkv, w_down, w_beta, acc, acc_low, acc_beta, rim_buf,
    w_sem, s_sem, r_sem, hs_sem, hf_sem, hr_sem, rim_sem,
):
    n_ctx = lax.axis_size("ctx")
    n_head = lax.axis_size("head")
    n_y = n_head // CORES
    me = lax.axis_index("ctx")
    head = lax.axis_index("head")
    y = head // CORES
    core = head % CORES
    sibling = y * CORES + (1 - core)
    width, rows = hidden_buf.shape
    slots = send_buf.shape[0]
    cap = slots // n_ctx

    early = [
        pltpu.make_async_copy(slot_hbm, slot_buf, w_sem.at[3]),
        pltpu.make_async_copy(hidden_hbm, hidden_buf, w_sem.at[4]),
        pltpu.make_async_copy(src_hbm, src_buf, w_sem.at[5]),
        pltpu.make_async_copy(wbeta_hbm, wbeta_buf, w_sem.at[2]),
    ]
    weights = [
        pltpu.make_async_copy(wqkv_hbm, w_qkv, w_sem.at[0]),
        pltpu.make_async_copy(wdown_hbm, w_down, w_sem.at[1]),
    ]
    for copy in early + weights:
        copy.start()

    barrier = pltpu.get_barrier_semaphore()

    def greet(k, carry):
        pl.semaphore_signal(
            barrier, inc=1, device_id={"ctx": lax.rem(me + k, n_ctx), "head": head}, device_id_type=MESH
        )
        return carry

    lax.fori_loop(1, n_ctx, greet, 0)
    for dy in range(1, n_y):
        other = lax.rem(y + dy, n_y) * CORES + core
        pl.semaphore_signal(barrier, inc=1, device_id={"ctx": me, "head": other}, device_id_type=MESH)
    pl.semaphore_signal(barrier, inc=1, device_id={"ctx": me, "head": sibling}, device_id_type=MESH)

    for copy in early:
        copy.wait()
    slot_ids = lax.broadcasted_iota(jnp.int32, (slots, rows), 0)
    place = (slot_ids == slot_buf[...]).astype(F32).astype(BF16)
    send_buf[...] = mm(place, hidden_buf[...], NT).astype(BF16)
    pick = (slot_ids == src_buf[...]).astype(F32).astype(BF16)

    for index in range(n_head):
        w_beta[index] = wbeta_buf[:, index * width : (index + 1) * width]

    pl.semaphore_wait(barrier, n_ctx - 1 + n_y)

    def piece(buf, index):
        return buf.at[pl.ds(pl.multiple_of(index * cap, cap), cap), :]

    def send(k, carry):
        to = lax.rem(me + k, n_ctx)
        pltpu.make_async_remote_copy(
            src_ref=piece(send_buf, to), dst_ref=piece(landed, me),
            send_sem=s_sem.at[to], recv_sem=r_sem.at[me],
            device_id={"ctx": to, "head": head}, device_id_type=MESH,
        ).start()
        return carry

    lax.fori_loop(1, n_ctx, send, 0)
    own = pl.ds(pl.multiple_of(me * cap, cap), cap)
    landed[own, :] = send_buf[own, :]

    def arrive(k, carry):
        frm = lax.rem(me + k, n_ctx)
        pltpu.make_async_remote_copy(
            src_ref=piece(send_buf, frm), dst_ref=piece(landed, frm),
            send_sem=s_sem.at[frm], recv_sem=r_sem.at[frm],
            device_id={"ctx": frm, "head": head}, device_id_type=MESH,
        ).wait_recv()
        return carry

    lax.fori_loop(1, n_ctx, arrive, 0)
    shards[head] = mm(pick, landed[...], TN).astype(BF16)

    def shard_copy(index, to, send_sem):
        return pltpu.make_async_remote_copy(
            src_ref=shards.at[index], dst_ref=shards.at[index],
            send_sem=send_sem, recv_sem=hr_sem.at[index],
            device_id={"ctx": me, "head": to}, device_id_type=MESH,
        )

    outgoing = [shard_copy(head, lax.rem(y + dy, n_y) * CORES + core, hs_sem.at[dy]) for dy in range(1, n_y)]
    outgoing.append(shard_copy(head, sibling, hs_sem.at[0]))
    for copy in outgoing:
        copy.start()
    for copy in weights:
        copy.wait()

    def multiply(index, first=False):
        part = shards[index]
        chunk = pl.ds(pl.multiple_of(index * width, 16), width)
        products = [(acc, j, mm(part, w_qkv[j, chunk, :])) for j in range(3)]
        for ref, j, value in products:
            ref[j] = value if first else ref[j] + value
        low = mm(part, w_down[chunk, :])
        beta = mm(part, w_beta[index], NT)
        acc_low[...] = low if first else acc_low[...] + low
        acc_beta[...] = beta if first else acc_beta[...] + beta

    multiply(head, True)
    shard_copy(sibling, sibling, hs_sem.at[0]).wait_recv()
    multiply(sibling)
    order = [dy for dy in (1, n_y - 1) if 0 < dy < n_y]
    order = sorted(set(order)) + [dy for dy in range(1, n_y) if dy not in order]
    pending = []
    for dy in order:
        index = lax.rem(y + dy, n_y) * CORES + core
        shard_copy(index, sibling, hf_sem.at[dy]).wait_recv()
        forward = shard_copy(index, sibling, hf_sem.at[dy])
        forward.start()
        outgoing.append(forward)
        multiply(index)
        pending.append(lax.rem(y + dy, n_y) * CORES + (1 - core))
    for index in pending:
        shard_copy(index, sibling, hs_sem.at[0]).wait_recv()
        multiply(index)

    columns = acc.shape[2]
    for j in range(3):
        ext_ref[RIM:, j * columns : (j + 1) * columns] = acc[j].astype(BF16).astype(F32)
    rim = pltpu.make_async_remote_copy(
        src_ref=ext_ref.at[pl.ds(rows, RIM), :], dst_ref=rim_buf,
        send_sem=rim_sem.at[0], recv_sem=rim_sem.at[1],
        device_id={"ctx": lax.rem(me + 1, n_ctx), "head": head}, device_id_type=MESH,
    )
    rim.start()
    low_ref[...] = acc_low[...].astype(BF16)
    beta_ref[...] = acc_beta[...]
    for copy in outgoing:
        copy.wait_send()

    def sent(k, carry):
        to = lax.rem(me + k, n_ctx)
        pltpu.make_async_remote_copy(
            src_ref=piece(send_buf, to), dst_ref=piece(landed, me),
            send_sem=s_sem.at[to], recv_sem=r_sem.at[me],
            device_id={"ctx": to, "head": head}, device_id_type=MESH,
        ).wait_send()
        return carry

    lax.fori_loop(1, n_ctx, sent, 0)
    rim.wait()
    ext_ref[:RIM, :] = rim_buf[...]


def gather_and_project(hidden, qkv_weight, gate_down, w_beta, send_slot, gather_src):
    width, rows = hidden.shape
    _, features, columns = qkv_weight.shape
    n_ctx, n_head = lax.axis_size("ctx"), lax.axis_size("head")
    slots = 2 * rows
    rank, betas = gate_down.shape[1], w_beta.shape[0]
    return pl.pallas_call(
        gather_kernel,
        out_shape=(
            jax.ShapeDtypeStruct((RIM + rows, 3 * columns), F32),
            jax.ShapeDtypeStruct((rows, rank), BF16),
            jax.ShapeDtypeStruct((rows, betas), F32),
        ),
        in_specs=[HBM] * 6,
        out_specs=(VMEM, VMEM, VMEM),
        scratch_shapes=[
            pltpu.VMEM((1, rows), jnp.int32),
            pltpu.VMEM((1, rows), jnp.int32),
            pltpu.VMEM((width, rows), BF16),
            pltpu.VMEM((betas, features), BF16),
            pltpu.VMEM((slots, width), BF16),
            pltpu.VMEM((slots, width), BF16),
            pltpu.VMEM((n_head, rows, width), BF16),
            pltpu.VMEM((3, features, columns), BF16),
            pltpu.VMEM((features, rank), BF16),
            pltpu.VMEM((n_head, betas, width), BF16),
            pltpu.VMEM((3, rows, columns), F32),
            pltpu.VMEM((rows, rank), F32),
            pltpu.VMEM((rows, betas), F32),
            pltpu.VMEM((RIM, 3 * columns), F32),
            pltpu.SemaphoreType.DMA((6,)),
            pltpu.SemaphoreType.DMA((n_ctx,)),
            pltpu.SemaphoreType.DMA((n_ctx,)),
            pltpu.SemaphoreType.DMA((n_head // CORES,)),
            pltpu.SemaphoreType.DMA((n_head // CORES,)),
            pltpu.SemaphoreType.DMA((n_head,)),
            pltpu.SemaphoreType.DMA((2,)),
        ],
        compiler_params=pltpu.CompilerParams(
            collective_id=0, has_side_effects=True, vmem_limit_bytes=48 * 1024 * 1024
        ),
        name="gather_project",
    )(send_slot.reshape(1, rows), gather_src.reshape(1, rows), hidden, qkv_weight, gate_down, w_beta)


def delta_kernel(
    lengths_ref, rate_ref, ext_ref, low_ref, beta_ref, conv_ref, up_ref, bias_ref, gain_ref,
    out_ref,
    stack, local, lift, maps, total, others, state, entry_out, entry,
    xs_sem, xr_sem, zs_sem, zr_sem, bs_sem, br_sem,
):
    n_ctx = lax.axis_size("ctx")
    n_groups = n_ctx // GROUP
    me = lax.axis_index("ctx")
    head = lax.axis_index("head")
    member = lax.rem(me, GROUP)
    group = me // GROUP
    x, side = lax.rem(member, X_SIZE), member // X_SIZE
    heads, rows, channels = local.shape
    columns = heads * channels
    half = channels // 2
    blocks = rows // SPAN
    base = me * rows

    def at(ctx):
        return {"ctx": ctx, "head": head}

    def mate(index):
        return at(group * GROUP + index)

    barrier = pltpu.get_barrier_semaphore()
    for k in range(1, GROUP):
        pl.semaphore_signal(
            barrier, inc=1, device_id=mate(lax.rem(member + k, GROUP)), device_id_type=MESH
        )
    for k in range(1, n_groups):
        pl.semaphore_signal(
            barrier, inc=1, device_id=at(lax.rem(me + k * GROUP, n_ctx)), device_id_type=MESH
        )

    ends, total_len = [], 0
    for i in range(lengths_ref.shape[0]):
        total_len = total_len + lengths_ref[i]
        ends.append(total_len)

    def doc_of(positions):
        ended = sum((positions >= end).astype(jnp.int32) for end in ends)
        return jnp.where(positions < 0, -1, ended)

    pos = base + lax.broadcasted_iota(jnp.int32, (rows, channels), 0)
    doc = doc_of(pos)
    valid = [None] + [(doc_of(pos - shift) == doc).astype(F32) for shift in range(1, CONV)]
    before = doc_of(jnp.zeros((1, channels), jnp.int32) + (base - 1))
    final = doc_of(jnp.zeros((1, channels), jnp.int32) + (base + rows - 1))
    first_doc = (doc == before).astype(F32)
    last_doc = (doc == final).astype(F32)
    carry = (final == before).astype(F32)
    row = lax.broadcasted_iota(jnp.int32, (rows, rows), 0)
    col = lax.broadcasted_iota(jnp.int32, (rows, rows), 1)
    col_doc = doc_of(base + lax.broadcasted_iota(jnp.int32, (1, rows), 1))
    same = jnp.concatenate([doc, doc], axis=1) == col_doc
    strict = (row > col) & same
    inclusive = (row >= col) & same
    apart = row ^ col
    running = ((row >= col) & (apart < SPAN)).astype(F32).astype(BF16)
    small_row = lax.broadcasted_iota(jnp.int32, (SPAN, rows), 0)
    small_col = lax.broadcasted_iota(jnp.int32, (SPAN, rows), 1)
    small_apart = small_row ^ (small_col & (SPAN - 1))
    small_block = small_col // SPAN
    small_eye = (small_apart == 0).astype(F32)

    def activated(j):
        lanes = slice(j * columns, (j + 1) * columns)
        out = None
        for tap in range(CONV):
            shift = CONV - 1 - tap
            part = conv_ref[j, tap : tap + 1, :] * ext_ref[pl.ds(RIM - shift, rows), lanes]
            if shift:
                part = part * jnp.concatenate([valid[shift]] * heads, axis=1)
            out = part if out is None else out + part
        return out / (1.0 + jnp.exp(-out))

    def of_head(v, h):
        return v[:, h * channels : (h + 1) * channels]

    def unit(v):
        return v * lax.rsqrt(jnp.sum(v * v, axis=-1, keepdims=True) + 1e-06)

    def block(v, b):
        return v[b * SPAN : (b + 1) * SPAN]

    drive = mm(low_ref[...], up_ref[...]) + bias_ref[...]
    soft = jnp.maximum(drive, 0.0) + jnp.log1p(jnp.exp(-jnp.abs(drive)))
    rates = jnp.concatenate(
        [jnp.exp(jnp.full((1, channels), rate_ref[h], F32)) for h in range(heads)], axis=1
    )
    decay = -rates * soft
    d_high, d_mid = split(decay)
    d_low = (decay - d_high.astype(F32) - d_mid.astype(F32)).astype(BF16)
    cum_all = mm(running, d_high) + (mm(running, d_mid) + mm(running, d_low))
    betas = 1.0 / (1.0 + jnp.exp(-beta_ref[...]))
    acts = [activated(j) for j in range(3)]

    every = range(heads)
    cums = [of_head(cum_all, h) for h in every]
    strengths = [jnp.broadcast_to(betas[:, h : h + 1], (rows, channels)) for h in every]
    queries = [unit(of_head(acts[0], h)) * channels ** (-0.5) for h in every]
    keys = [unit(of_head(acts[1], h)) for h in every]
    values = [strengths[h] * of_head(acts[2], h) for h in every]
    lasts = [[cums[h][(b + 1) * SPAN - 1 : (b + 1) * SPAN] for b in range(blocks)] for h in every]
    nothing = jnp.zeros((1, channels), F32)

    lower, score, solved = [], [], []
    bk_ups, q_ups, tails = [], [], []
    for h in every:
        grow = jnp.exp(cums[h])
        bk_ups.append(strengths[h] * keys[h] * grow)
        q_ups.append(queries[h] * grow)
        key_down = keys[h] * jnp.exp(-cums[h])
        tails.append([block(keys[h], b) * jnp.exp(lasts[h][b] - block(cums[h], b)) for b in range(blocks)])
        mixes, reads = [], []
        for i in range(blocks):
            cols = []
            for b in range(blocks):
                if b < i - 1:
                    cols.append(tails[h][b] * jnp.exp(sum(lasts[h][b + 1 : i], nothing)))
                elif b == i - 1:
                    cols.append(tails[h][b])
                elif b == i:
                    cols.append(block(key_down, b))
                else:
                    cols.append(jnp.zeros((SPAN, channels), F32))
            left = split(jnp.concatenate([block(bk_ups[h], i), block(q_ups[h], i)], axis=0))
            product = mm3_narrow(left, split(jnp.concatenate(cols, axis=0)), NT)
            mixes.append(jnp.where(block(strict, i), product[:SPAN], 0.0))
            reads.append(jnp.where(block(inclusive, i), product[SPAN:], 0.0))
        lower.append(mixes)
        score.append(reads)

    def spread(v):
        return jnp.concatenate(
            [jnp.where(small_block == b, v, 0.0) for b in range(blocks)], axis=0
        )

    def times(lefts, rights):
        return [mm3(split(a), split(spread(b))) for a, b in zip(lefts, rights)]

    diagonal = []
    for h in every:
        picked = jnp.zeros((SPAN, rows), F32)
        for b in range(blocks):
            picked = jnp.where(small_block == b, lower[h][b], picked)
        diagonal.append(picked)
    power = [jnp.where(small_apart < 8, d, 0.0) for d in diagonal]
    inverse = [small_eye - p for p in power]
    power = times(power, power)
    inverse = [i + t for i, t in zip(inverse, times(inverse, power))]
    power = times(power, power)
    inverse = [i + t for i, t in zip(inverse, times(inverse, power))]
    size = 8
    while size < SPAN:
        off = [jnp.where((small_apart >= size) & (small_apart < 2 * size), d, 0.0) for d in diagonal]
        inverse = [i - t for i, t in zip(inverse, times(inverse, times(off, inverse)))]
        size *= 2

    full_keys, full_queries, ends_k, keeps = [], [], [], []
    for h in every:
        prefix = nothing
        k_rows, q_rows, t_rows = [], [], []
        for b in range(blocks):
            scale = jnp.exp(prefix)
            k_rows.append(block(bk_ups[h], b) * scale)
            q_rows.append(block(q_ups[h], b) * scale)
            prefix = prefix + lasts[h][b]
            t_rows.append(tails[h][b] * jnp.exp(sum(lasts[h][b + 1 :], nothing)))
        full_keys.append(jnp.concatenate(k_rows, axis=0) * first_doc)
        full_queries.append(jnp.concatenate(q_rows, axis=0) * first_doc)
        ends_k.append(split(jnp.concatenate(t_rows, axis=0) * last_doc))
        keeps.append(carry * jnp.exp(prefix))
    rights = [jnp.concatenate([full_keys[h], values[h]], axis=1) for h in every]
    done = [[] for _ in every]
    for i in range(blocks):
        rest = []
        for h in every:
            part = block(rights[h], i)
            if i:
                seen = tuple(jnp.concatenate([d[k] for d in done[h]], axis=0) for k in range(2))
                part = part - mm3(split(lower[h][i][:, : i * SPAN]), seen)
            rest.append(split(part))
        for h in every:
            own = split(inverse[h][:, i * SPAN : (i + 1) * SPAN])
            done[h].append(split(mm3(own, rest[h])))
    solved = [tuple(jnp.concatenate([d[k] for d in done[h]], axis=0) for k in range(2)) for h in every]

    eye_channels = (
        lax.broadcasted_iota(jnp.int32, (channels, channels), 0)
        == lax.broadcasted_iota(jnp.int32, (channels, channels), 1)
    ).astype(F32)
    for h in every:
        summary = mm3(solved[h], ends_k[h], TN)
        stack[h, :half] = summary[channels : channels + half]
        stack[h, half : half + channels] = keeps[h] * eye_channels - summary[:channels]
        stack[h, half + channels :] = summary[channels + half :]

    pl.semaphore_wait(barrier, GROUP + n_groups - 2)

    def map_copy(k):
        to = lax.rem(member + k, GROUP)
        start = pl.multiple_of((to // X_SIZE) * half, half)
        return pltpu.make_async_remote_copy(
            src_ref=stack.at[lax.rem(to, X_SIZE), pl.ds(start, channels + half), :],
            dst_ref=maps.at[member],
            send_sem=xs_sem.at[k], recv_sem=xr_sem.at[member],
            device_id=mate(to), device_id_type=MESH,
        )

    sends = [map_copy(k) for k in range(1, GROUP)]
    for copy in sends:
        copy.start()
    maps[member] = stack[x, pl.ds(pl.multiple_of(side * half, half), channels + half), :]

    for h in every:
        combined = mm3(split(jnp.concatenate(score[h], axis=0)), solved[h])
        lift[h] = full_queries[h] - combined[:, :channels]
        local[h] = combined[:, channels:]

    for k in range(1, GROUP):
        frm = lax.rem(member + k, GROUP)
        pltpu.make_async_remote_copy(
            src_ref=maps.at[frm], dst_ref=maps.at[frm],
            send_sem=xs_sem.at[k], recv_sem=xr_sem.at[frm],
            device_id=mate(frm), device_id_type=MESH,
        ).wait_recv()

    map_at = pl.ds(pl.multiple_of((1 - side) * half, half), channels)
    feed_at = pl.ds(pl.multiple_of(side * channels, channels), half)

    def follow(whole, step):
        moved = mm3_narrow(split(whole), split(step[:channels]))
        return jnp.concatenate([moved[:channels], moved[channels:] + step[channels:]], axis=0)

    steps = [jnp.concatenate([maps[j, map_at, :], maps[j, feed_at, :]], axis=0) for j in range(GROUP)]
    prefixes = [steps[0]]
    late = [steps[X_SIZE]]
    for j in range(1, X_SIZE):
        prefixes.append(follow(prefixes[-1], steps[j]))
        late.append(follow(late[-1], steps[X_SIZE + j]))
    total[...] = follow(prefixes[-1], late[-1])

    def total_copy(k, only_feed):
        span = pl.ds(channels, half) if only_feed else pl.ds(0, channels + half)
        return pltpu.make_async_remote_copy(
            src_ref=total.at[span, :], dst_ref=others.at[group, span, :],
            send_sem=zs_sem.at[k], recv_sem=zr_sem.at[group],
            device_id=at(lax.rem(me + k * GROUP, n_ctx)), device_id_type=MESH,
        )

    def for_later_groups(act):
        for k in range(1, n_groups):
            @pl.when((group > 0) & (group + k < n_groups))
            def _():
                act(total_copy(k, False))

        @pl.when(group == 0)
        def _():
            for k in range(1, n_groups):
                act(total_copy(k, True))

    for_later_groups(lambda copy: copy.start())
    for j in range(X_SIZE - 1):
        prefixes.append(follow(prefixes[X_SIZE - 1], late[j]))
    into = split(jnp.concatenate([p[:channels] for p in prefixes], axis=1))

    state[...] = jnp.zeros_like(state)
    for frm in range(n_groups - 1):
        @pl.when(group > frm)
        def _():
            span = pl.ds(channels, half) if frm == 0 else pl.ds(0, channels + half)
            pltpu.make_async_remote_copy(
                src_ref=total.at[span, :], dst_ref=others.at[frm, span, :],
                send_sem=zs_sem.at[0], recv_sem=zr_sem.at[frm],
                device_id=at(lax.rem(me + GROUP, n_ctx)), device_id_type=MESH,
            ).wait_recv()
            feed = others[frm, pl.ds(channels, half), :]
            if frm:
                feed = feed + mm3_narrow(split(state[...]), split(others[frm, pl.ds(0, channels), :]))
            state[...] = feed

    start_state = state[...]
    moved = mm3_narrow(split(start_state), into)
    entry_out[0] = start_state
    for j in range(1, GROUP):
        entry_out[j] = moved[:, (j - 1) * channels : j * channels] + prefixes[j - 1][channels:]

    def entry_copy(k):
        to = lax.rem(member + k, GROUP)
        return pltpu.make_async_remote_copy(
            src_ref=entry_out.at[to], dst_ref=entry.at[member],
            send_sem=bs_sem.at[k], recv_sem=br_sem.at[member],
            device_id=mate(to), device_id_type=MESH,
        )

    returns = [entry_copy(k) for k in range(1, GROUP)]
    for copy in returns:
        copy.start()
    entry[member] = entry_out[member]
    for k in range(1, GROUP):
        frm = lax.rem(member + k, GROUP)
        pltpu.make_async_remote_copy(
            src_ref=entry_out.at[frm], dst_ref=entry.at[frm],
            send_sem=bs_sem.at[k], recv_sem=br_sem.at[frm],
            device_id=mate(frm), device_id_type=MESH,
        ).wait_recv()

    for h in every:
        incoming = jnp.concatenate([entry[h], entry[X_SIZE + h]], axis=0)
        result = local[h] + mm3_narrow(split(lift[h]), split(incoming), NT)
        mean = jnp.mean(result * result, axis=-1, keepdims=True)
        scaled = result * lax.rsqrt(mean + 1e-05) * gain_ref[...]
        out_ref[:, h * channels : (h + 1) * channels] = scaled.astype(BF16)

    for copy in sends + returns:
        copy.wait_send()
    for_later_groups(lambda copy: copy.wait_send())


def delta(ext, low, beta, conv_weight, gate_up, a_log, dt_bias, norm_gain, prompt_lengths):
    rows = low.shape[0]
    heads = a_log.shape[0]
    channels = norm_gain.shape[0]
    n_groups = lax.axis_size("ctx") // GROUP
    half = channels // 2
    return pl.pallas_call(
        delta_kernel,
        out_shape=jax.ShapeDtypeStruct((rows, heads * channels), BF16),
        in_specs=[SMEM, SMEM] + [VMEM] * 7,
        out_specs=VMEM,
        scratch_shapes=[
            pltpu.VMEM((heads, 2 * channels, channels), F32),
            pltpu.VMEM((heads, rows, channels), F32),
            pltpu.VMEM((heads, rows, channels), F32),
            pltpu.VMEM((GROUP, channels + half, channels), F32),
            pltpu.VMEM((channels + half, channels), F32),
            pltpu.VMEM((n_groups, channels + half, channels), F32),
            pltpu.VMEM((half, channels), F32),
            pltpu.VMEM((GROUP, half, channels), F32),
            pltpu.VMEM((GROUP, half, channels), F32),
            pltpu.SemaphoreType.DMA((GROUP,)),
            pltpu.SemaphoreType.DMA((GROUP,)),
            pltpu.SemaphoreType.DMA((n_groups,)),
            pltpu.SemaphoreType.DMA((n_groups,)),
            pltpu.SemaphoreType.DMA((GROUP,)),
            pltpu.SemaphoreType.DMA((GROUP,)),
        ],
        compiler_params=pltpu.CompilerParams(
            collective_id=1, has_side_effects=True, vmem_limit_bytes=48 * 1024 * 1024
        ),
        name="delta",
    )(
        prompt_lengths, a_log, ext, low, beta, conv_weight, gate_up,
        dt_bias.reshape(1, -1), norm_gain.reshape(1, -1),
    )


def on_device(
    hidden, qkv_weight, conv_weight, w_beta, gate_down, gate_up,
    a_log, dt_bias, norm_gain, prompt_lengths, send_slot, gather_src,
):
    ext, low, beta = gather_and_project(hidden.T, qkv_weight, gate_down, w_beta.T, send_slot, gather_src)
    return delta(
        ext, low, beta, conv_weight.transpose(1, 0, 2), gate_up, a_log, dt_bias, norm_gain, prompt_lengths
    )


def solution(mesh):
    placed = (
        P("ctx", "head"),
        P(None, None, "head"),
        P(None, None, "head"),
        P(None, "head"),
        P(),
        P(None, "head"),
        P("head"),
        P("head"),
        P(),
        P(),
        P("ctx"),
        P("ctx"),
    )
    return jax.shard_map(
        on_device, mesh=mesh, in_specs=placed, out_specs=P("ctx", "head"), check_vma=False
    )
```

time: 108 us -> 76.3 us (0.71)
  Pallas kernels: 101 us -> 71.1 us
  local copies, waits for them, and re-layouts: 6.1 us -> 4.82 us
    pallas_call x2 -> x1, Pallas kernels: 64.5 us -> 34.3 us  [delta(): pl.pallas_call(delta_kernel, out_shape=jax.ShapeDtypeStruct((rows, heads...]
    unnamed x20 -> x23, local copies, waits for them, and re-layouts: 6.1 us -> 4.82 us
where the time goes in v2:
time: 76.3 us; the launch traced here: 76.1 us
  Pallas kernels  71.1 us (93%)
  local copies, waits for them, and re-layouts  4.82 us (6%)
    pallas_call x1, Pallas kernels, gather_and_project(): pl.pallas_call(gather_kernel, out_shape=(jax.ShapeDtypeStruct((RIM + rows...  36.8 us
    pallas_call x1, Pallas kernels, delta(): pl.pallas_call(delta_kernel, out_shape=jax.ShapeDtypeStruct((rows, heads...  34.3 us
    unnamed x23, local copies, waits for them, and re-layouts  4.82 us

profile of v2, /device:TPU:224, one launch (start us, length us, event | category | flops | bytes accessed | tf_op | source)
XLA Modules:
  0.0 76.1 jit_solution(1326404081959483013)
XLA Ops:
  0.0 0.0 copy-start.8
  0.0 0.0 copy-start.10
  0.0 0.0 copy-start.5
  0.0 0.0 copy-start.9
  0.0 0.0 copy-start
  0.0 1.1 %copy-done = bf16[2304,128]{1,0:T(8,128)(2,1)S(1)} copy-done((bf16[2304,128]{1,0:T(8,128)(2,1)S(1)}, bf16[2304,128]{1,0:T(8,128)(2,1)}, u32[]{:S(2)}) %copy-start) | copy-done | bytes 589848
  1.1 0.0 copy-start.1
  1.1 0.9 %copy-done.1 = bf16[256,288]{0,1:T(8,128)(2,1)S(1)} copy-done((bf16[256,288]{0,1:T(8,128)(2,1)S(1)}, bf16[256,288]{0,1:T(8,128)(2,1)}, u32[]{:S(2)}) %copy-start.1) | copy-done | bytes 147480
  2.0 0.0 copy-start.4
  2.0 0.7 copy-done.4
  2.8 0.0 copy-start.6
  2.8 0.7 copy-done.6
  3.4 0.0 copy-start.7
  3.4 0.7 copy-done.7
  4.1 0.0 copy-start.2
  4.1 0.0 copy-start.3
  4.1 36.8 %gather_project.1 = (f32[264,1536]{1,0:T(8,128)S(1)}, bf16[256,128]{1,0:T(8,128)(2,1)S(1)}, f32[256,4]{1,0:T(8,128)S(1)}) custom-call(s32[1,256]{1,0:T(1,128)S(1)} %bitcast.11, s32[1,256]{1,0:T(1,128)S(1)} %bitcast.12, bf16[288,256]{1,0:T(8,128)(2,1)S(1)} %bitcast.7, bf16[3,2304,512]{2,1,0:T(8,128)(2,1)} %wqkv_hbm.1, bf16[2304,128]{1,0:T(8,128)(2,1)S(1)} %copy-done, ...), custom_call_target="tpu_custom_call" | custom-call | tf_op jit(solution)/shard_map/gather_project/pallas_call | solution.py:210
  41.0 0.0 copy-done.8
  41.0 0.0 copy-done.10
  41.0 0.0 copy-done.5
  41.0 0.0 copy-done.9
  41.0 0.0 copy-done.2
  41.0 0.0 copy-done.3
  41.0 34.3 %delta.1 = bf16[256,512]{1,0:T(8,128)(2,1)S(1)} custom-call(s32[4]{0:T(128)S(1)} %copy-done.8, f32[4]{0:T(128)S(1)} %copy-done.9, f32[264,1536]{1,0:T(8,128)S(1)} %get-tuple-element.8.ext_ref, bf16[256,128]{1,0:T(8,128)(2,1)S(1)} %get-tuple-element.9.low_ref, f32[256,4]{1,0:T(8,128)S(1)} %get-tuple-element.10.beta_ref, f32[3,4,512]{2,1,0:T(4,128)S(1)} %bitcast.8, ...), custom_call_target="tpu_custom_call" | custom-call | tf_op jit(solution)/shard_map/delta/pallas_call | solution.py:576
  75.3 0.7 copy.14
Async XLA Ops:
  0.0 41.0 %copy-start.8 = (s32[4]{0:T(128)S(1)}, s32[4]{0:T(128)}, u32[]{:S(2)}) copy-start(s32[4]{0:T(128)} %lengths_ref.1) | copy-start | bytes 52
  0.0 41.0 %copy-start.10 = (f32[128]{0:T(128)S(1)}, f32[128]{0:T(128)}, u32[]{:S(2)}) copy-start(f32[128]{0:T(128)} %param.20) | copy-start | bytes 1540
  0.0 41.0 %copy-start.5 = (f32[512]{0:T(512)S(1)}, f32[512]{0:T(512)}, u32[]{:S(2)}) copy-start(f32[512]{0:T(512)} %param.19) | copy-start | bytes 6148
  0.0 41.0 %copy-start.9 = (f32[4]{0:T(128)S(1)}, f32[4]{0:T(128)}, u32[]{:S(2)}) copy-start(f32[4]{0:T(128)} %rate_ref.1) | copy-start | bytes 52
  0.0 1.1 %copy-start = (bf16[2304,128]{1,0:T(8,128)(2,1)S(1)}, bf16[2304,128]{1,0:T(8,128)(2,1)}, u32[]{:S(2)}) copy-start(bf16[2304,128]{1,0:T(8,128)(2,1)} %wdown_hbm.1) | copy-start | bytes 1769476
  1.1 0.9 %copy-start.1 = (bf16[256,288]{0,1:T(8,128)(2,1)S(1)}, bf16[256,288]{0,1:T(8,128)(2,1)}, u32[]{:S(2)}) copy-start(bf16[256,288]{0,1:T(8,128)(2,1)} %param.12) | copy-start | bytes 442372
  2.0 0.7 copy-start.4
  2.8 0.7 copy-start.6
  3.4 0.7 copy-start.7
  4.1 36.9 %copy-start.2 = (bf16[128,512]{1,0:T(8,128)(2,1)S(1)}, bf16[128,512]{1,0:T(8,128)(2,1)}, u32[]{:S(2)}) copy-start(bf16[128,512]{1,0:T(8,128)(2,1)} %up_ref.1) | copy-start | bytes 393220
  4.1 36.9 %copy-start.3 = (f32[4,3,512]{2,0,1:T(4,128)S(1)}, f32[4,3,512]{2,0,1:T(4,128)}, u32[]{:S(2)}) copy-start(f32[4,3,512]{2,0,1:T(4,128)} %param.14) | copy-start | bytes 73732

commit v3 on v2

--- a/solution.py
+++ b/solution.py
@@ -16,7 +16,6 @@
 MESH = pl.DeviceIdType.MESH
 F32 = jnp.float32
 BF16 = jnp.bfloat16
-VMEM = pl.BlockSpec(memory_space=pltpu.VMEM)
 SMEM = pl.BlockSpec(memory_space=pltpu.SMEM)
 HBM = pl.BlockSpec(memory_space=pltpu.HBM)
 
@@ -44,242 +43,165 @@
     return wide + mm(a[0], b[1], dims)
 
 
-def gather_kernel(
-    slot_hbm, src_hbm, hidden_hbm, wqkv_hbm, wdown_hbm, wbeta_hbm,
-    ext_ref, low_ref, beta_ref,
-    slot_buf, src_buf, hidden_buf, wbeta_buf,
-    send_buf, landed, shards, w_qkv, w_down, w_beta, acc, acc_low, acc_beta, rim_buf,
-    w_sem, s_sem, r_sem, hs_sem, hf_sem, hr_sem, rim_sem,
+def fused_kernel(
+    lengths_ref, rate_ref, slot_hbm, src_hbm, hidden_hbm, wqkv_hbm, wdown_hbm, wbeta_hbm,
+    conv_hbm, up_hbm, bias_hbm, gain_hbm,
+    out_hbm,
+    slot_buf, src_buf, hidden_buf, w_qkv, w_down, wbeta_buf, conv_ref, up_ref, bias_ref, gain_ref,
+    send_buf, landed, shards, w_beta, acc, acc_low, acc_beta, ext_ref,
+    stack, local, lift, maps, total, others, state, entry_out, entry, out_buf,
+    in_sem, s_sem, r_sem, hs_sem, hr_sem, rim_sem,
+    xs_sem, xr_sem, zs_sem, zr_sem, bs_sem, br_sem, out_sem,
 ):
     n_ctx = lax.axis_size("ctx")
+    n_z = n_ctx // X_SIZE
     n_head = lax.axis_size("head")
     n_y = n_head // CORES
+    n_groups = n_ctx // GROUP
     me = lax.axis_index("ctx")
     head = lax.axis_index("head")
-    y = head // CORES
-    core = head % CORES
+    z, own_x = me // X_SIZE, lax.rem(me, X_SIZE)
+    y, core = head // CORES, lax.rem(head, CORES)
     sibling = y * CORES + (1 - core)
+    member = lax.rem(me, GROUP)
+    group = me // GROUP
+    x, side = lax.rem(member, X_SIZE), member // X_SIZE
     width, rows = hidden_buf.shape
     slots = send_buf.shape[0]
     cap = slots // n_ctx
-
-    early = [
-        pltpu.make_async_copy(slot_hbm, slot_buf, w_sem.at[3]),
-        pltpu.make_async_copy(hidden_hbm, hidden_buf, w_sem.at[4]),
-        pltpu.make_async_copy(src_hbm, src_buf, w_sem.at[5]),
-        pltpu.make_async_copy(wbeta_hbm, wbeta_buf, w_sem.at[2]),
+    heads, _, channels = local.shape
+    columns = heads * channels
+    half = channels // 2
+    blocks = rows // SPAN
+    base = me * rows
+
+    def at(ctx):
+        return {"ctx": ctx, "head": head}
+
+    def mate(index):
+        return at(group * GROUP + index)
+
+    operands = [
+        (slot_hbm, slot_buf), (hidden_hbm, hidden_buf), (src_hbm, src_buf), (wbeta_hbm, wbeta_buf),
+        (wqkv_hbm, w_qkv), (wdown_hbm, w_down),
+        (up_hbm, up_ref), (bias_hbm, bias_ref), (conv_hbm, conv_ref), (gain_hbm, gain_ref),
     ]
-    weights = [
-        pltpu.make_async_copy(wqkv_hbm, w_qkv, w_sem.at[0]),
-        pltpu.make_async_copy(wdown_hbm, w_down, w_sem.at[1]),
-    ]
-    for copy in early + weights:
+    loads = [pltpu.make_async_copy(a, b, in_sem.at[i]) for i, (a, b) in enumerate(operands)]
+    for copy in loads:
         copy.start()
 
+    far = sorted(
+        ((dz, dx) for dz in range(n_z) for dx in range(X_SIZE) if dz or dx),
+        key=lambda d: -(min(d[0], n_z - d[0]) * 2 + min(d[1], X_SIZE - d[1])),
+    )
+    peers = [lax.rem(z + dz, n_z) * X_SIZE + lax.rem(own_x + dx, X_SIZE) for dz, dx in far]
+    ring = {dy: lax.rem(y + dy, n_y) for dy in range(n_y)}
+
     barrier = pltpu.get_barrier_semaphore()
-
-    def greet(k, carry):
-        pl.semaphore_signal(
-            barrier, inc=1, device_id={"ctx": lax.rem(me + k, n_ctx), "head": head}, device_id_type=MESH
-        )
-        return carry
-
-    lax.fori_loop(1, n_ctx, greet, 0)
-    for dy in range(1, n_y):
-        other = lax.rem(y + dy, n_y) * CORES + core
-        pl.semaphore_signal(barrier, inc=1, device_id={"ctx": me, "head": other}, device_id_type=MESH)
-    pl.semaphore_signal(barrier, inc=1, device_id={"ctx": me, "head": sibling}, device_id_type=MESH)
-
-    for copy in early:
+    for to in peers:
+        pl.semaphore_signal(barrier, inc=1, device_id=at(to), device_id_type=MESH)
+    for to in (ring[1] * CORES + core, ring[n_y - 1] * CORES + core, sibling):
+        pl.semaphore_signal(barrier, inc=1, device_id={"ctx": me, "head": to}, device_id_type=MESH)
+
+    for copy in loads[:4]:
         copy.wait()
     slot_ids = lax.broadcasted_iota(jnp.int32, (slots, rows), 0)
     place = (slot_ids == slot_buf[...]).astype(F32).astype(BF16)
     send_buf[...] = mm(place, hidden_buf[...], NT).astype(BF16)
     pick = (slot_ids == src_buf[...]).astype(F32).astype(BF16)
-
-    for index in range(n_head):
-        w_beta[index] = wbeta_buf[:, index * width : (index + 1) * width]
-
-    pl.semaphore_wait(barrier, n_ctx - 1 + n_y)
-
-    def piece(buf, index):
-        return buf.at[pl.ds(pl.multiple_of(index * cap, cap), cap), :]
-
-    def send(k, carry):
-        to = lax.rem(me + k, n_ctx)
-        pltpu.make_async_remote_copy(
-            src_ref=piece(send_buf, to), dst_ref=piece(landed, me),
-            send_sem=s_sem.at[to], recv_sem=r_sem.at[me],
-            device_id={"ctx": to, "head": head}, device_id_type=MESH,
-        ).start()
-        return carry
-
-    lax.fori_loop(1, n_ctx, send, 0)
-    own = pl.ds(pl.multiple_of(me * cap, cap), cap)
-    landed[own, :] = send_buf[own, :]
-
-    def arrive(k, carry):
-        frm = lax.rem(me + k, n_ctx)
-        pltpu.make_async_remote_copy(
-            src_ref=piece(send_buf, frm), dst_ref=piece(landed, frm),
-            send_sem=s_sem.at[frm], recv_sem=r_sem.at[frm],
-            device_id={"ctx": frm, "head": head}, device_id_type=MESH,
-        ).wait_recv()
-        return carry
-
-    lax.fori_loop(1, n_ctx, arrive, 0)
-    shards[head] = mm(pick, landed[...], TN).astype(BF16)
-
-    def shard_copy(index, to, send_sem):
+    pair = CORES * width
+    w_beta[...] = jnp.zeros_like(w_beta)
+    for i in range(n_y):
+        w_beta[i, : wbeta_buf.shape[0], :] = wbeta_buf[:, i * pair : (i + 1) * pair]
+
+    pl.semaphore_wait(barrier, n_ctx - 1 + 3)
+
+    def slots_of(index):
+        return pl.ds(pl.multiple_of(index * cap, cap), cap)
+
+    def slot_copy(to, frm):
         return pltpu.make_async_remote_copy(
-            src_ref=shards.at[index], dst_ref=shards.at[index],
-            send_sem=send_sem, recv_sem=hr_sem.at[index],
+            src_ref=send_buf.at[slots_of(to), :], dst_ref=landed.at[slots_of(frm), :],
+            send_sem=s_sem.at[to], recv_sem=r_sem.at[frm],
+            device_id=at(to), device_id_type=MESH,
+        )
+
+    for to in peers:
+        slot_copy(to, me).start()
+    landed[slots_of(me), :] = send_buf[slots_of(me), :]
+    for frm in reversed(peers):
+        slot_copy(frm, frm).wait_recv()
+
+    def features(index, start=0, size=None):
+        return pl.ds(pl.multiple_of(index * width + start, 16), width if size is None else size)
+
+    shards[features(head), :] = mm(landed[...], pick, TN).astype(BF16)
+    middle = width // 2
+
+    def shard_copy(index, to, send, recv, start=0, size=None):
+        return pltpu.make_async_remote_copy(
+            src_ref=shards.at[features(index, start, size), :],
+            dst_ref=shards.at[features(index, start, size), :],
+            send_sem=hs_sem.at[send], recv_sem=hr_sem.at[recv],
             device_id={"ctx": me, "head": to}, device_id_type=MESH,
         )
 
-    outgoing = [shard_copy(head, lax.rem(y + dy, n_y) * CORES + core, hs_sem.at[dy]) for dy in range(1, n_y)]
-    outgoing.append(shard_copy(head, sibling, hs_sem.at[0]))
-    for copy in outgoing:
+    here = [ring[dy] * CORES + core for dy in range(n_y)]
+    there = [ring[dy] * CORES + (1 - core) for dy in range(n_y)]
+    up_y, down_y = here[1], here[n_y - 1]
+    passed = [
+        shard_copy(head, up_y, 0, n_y - 1),
+        shard_copy(head, down_y, 1, 1),
+        shard_copy(head, sibling, 2, n_y + 1),
+    ]
+    for copy in passed:
         copy.start()
-    for copy in weights:
+    for copy in loads[4:6]:
         copy.wait()
 
-    def multiply(index, first=False):
-        part = shards[index]
-        chunk = pl.ds(pl.multiple_of(index * width, 16), width)
-        products = [(acc, j, mm(part, w_qkv[j, chunk, :])) for j in range(3)]
-        for ref, j, value in products:
-            ref[j] = value if first else ref[j] + value
+    def multiply(dy, first=False):
+        part = shards[pl.ds(pl.multiple_of(ring[dy] * pair, 16), pair), :].T
+        chunk = pl.ds(pl.multiple_of(ring[dy] * pair, 16), pair)
+        products = [mm(part, w_qkv[j, chunk, :]) for j in range(3)]
         low = mm(part, w_down[chunk, :])
-        beta = mm(part, w_beta[index], NT)
+        beta = mm(part, w_beta[ring[dy]], NT)
+        for j in range(3):
+            acc[j] = products[j] if first else acc[j] + products[j]
         acc_low[...] = low if first else acc_low[...] + low
         acc_beta[...] = beta if first else acc_beta[...] + beta
 
-    multiply(head, True)
-    shard_copy(sibling, sibling, hs_sem.at[0]).wait_recv()
-    multiply(sibling)
-    order = [dy for dy in (1, n_y - 1) if 0 < dy < n_y]
-    order = sorted(set(order)) + [dy for dy in range(1, n_y) if dy not in order]
-    pending = []
-    for dy in order:
-        index = lax.rem(y + dy, n_y) * CORES + core
-        shard_copy(index, sibling, hf_sem.at[dy]).wait_recv()
-        forward = shard_copy(index, sibling, hf_sem.at[dy])
-        forward.start()
-        outgoing.append(forward)
-        multiply(index)
-        pending.append(lax.rem(y + dy, n_y) * CORES + (1 - core))
-    for index in pending:
-        shard_copy(index, sibling, hs_sem.at[0]).wait_recv()
-        multiply(index)
-
-    columns = acc.shape[2]
+    def pass_on(copy):
+        copy.start()
+        passed.append(copy)
+
+    shard_copy(there[0], sibling, 2, n_y + 1).wait_recv()
+    multiply(0, True)
+    shard_copy(here[3], sibling, 3, 3).wait_recv()
+    pass_on(shard_copy(here[3], up_y, 3, 2, 0, middle))
+    pass_on(shard_copy(here[3], sibling, 4, n_y + 1 + 3))
+    shard_copy(here[1], sibling, 5, 1).wait_recv()
+    pass_on(shard_copy(here[1], down_y, 5, n_y, middle, width - middle))
+    pass_on(shard_copy(here[1], sibling, 6, n_y + 1 + 1))
+    shard_copy(there[3], sibling, 4, n_y + 1 + 3).wait_recv()
+    multiply(3)
+    shard_copy(here[2], sibling, 7, 2, 0, middle).wait_recv()
+    shard_copy(here[2], sibling, 7, n_y, middle, width - middle).wait_recv()
+    pass_on(shard_copy(here[2], sibling, 7, n_y + 1 + 2))
+    shard_copy(there[1], sibling, 6, n_y + 1 + 1).wait_recv()
+    multiply(1)
+    shard_copy(there[2], sibling, 7, n_y + 1 + 2).wait_recv()
+    multiply(2)
+
     for j in range(3):
         ext_ref[RIM:, j * columns : (j + 1) * columns] = acc[j].astype(BF16).astype(F32)
     rim = pltpu.make_async_remote_copy(
-        src_ref=ext_ref.at[pl.ds(rows, RIM), :], dst_ref=rim_buf,
+        src_ref=ext_ref.at[pl.ds(rows, RIM), :], dst_ref=ext_ref.at[pl.ds(0, RIM), :],
         send_sem=rim_sem.at[0], recv_sem=rim_sem.at[1],
-        device_id={"ctx": lax.rem(me + 1, n_ctx), "head": head}, device_id_type=MESH,
+        device_id=at(lax.rem(me + 1, n_ctx)), device_id_type=MESH,
     )
     rim.start()
-    low_ref[...] = acc_low[...].astype(BF16)
-    beta_ref[...] = acc_beta[...]
-    for copy in outgoing:
-        copy.wait_send()
-
-    def sent(k, carry):
-        to = lax.rem(me + k, n_ctx)
-        pltpu.make_async_remote_copy(
-            src_ref=piece(send_buf, to), dst_ref=piece(landed, me),
-            send_sem=s_sem.at[to], recv_sem=r_sem.at[me],
-            device_id={"ctx": to, "head": head}, device_id_type=MESH,
-        ).wait_send()
-        return carry
-
-    lax.fori_loop(1, n_ctx, sent, 0)
-    rim.wait()
-    ext_ref[:RIM, :] = rim_buf[...]
-
-
-def gather_and_project(hidden, qkv_weight, gate_down, w_beta, send_slot, gather_src):
-    width, rows = hidden.shape
-    _, features, columns = qkv_weight.shape
-    n_ctx, n_head = lax.axis_size("ctx"), lax.axis_size("head")
-    slots = 2 * rows
-    rank, betas = gate_down.shape[1], w_beta.shape[0]
-    return pl.pallas_call(
-        gather_kernel,
-        out_shape=(
-            jax.ShapeDtypeStruct((RIM + rows, 3 * columns), F32),
-            jax.ShapeDtypeStruct((rows, rank), BF16),
-            jax.ShapeDtypeStruct((rows, betas), F32),
-        ),
-        in_specs=[HBM] * 6,
-        out_specs=(VMEM, VMEM, VMEM),
-        scratch_shapes=[
-            pltpu.VMEM((1, rows), jnp.int32),
-            pltpu.VMEM((1, rows), jnp.int32),
-            pltpu.VMEM((width, rows), BF16),
-            pltpu.VMEM((betas, features), BF16),
-            pltpu.VMEM((slots, width), BF16),
-            pltpu.VMEM((slots, width), BF16),
-            pltpu.VMEM((n_head, rows, width), BF16),
-            pltpu.VMEM((3, features, columns), BF16),
-            pltpu.VMEM((features, rank), BF16),
-            pltpu.VMEM((n_head, betas, width), BF16),
-            pltpu.VMEM((3, rows, columns), F32),
-            pltpu.VMEM((rows, rank), F32),
-            pltpu.VMEM((rows, betas), F32),
-            pltpu.VMEM((RIM, 3 * columns), F32),
-            pltpu.SemaphoreType.DMA((6,)),
-            pltpu.SemaphoreType.DMA((n_ctx,)),
-            pltpu.SemaphoreType.DMA((n_ctx,)),
-            pltpu.SemaphoreType.DMA((n_head // CORES,)),
-            pltpu.SemaphoreType.DMA((n_head // CORES,)),
-            pltpu.SemaphoreType.DMA((n_head,)),
-            pltpu.SemaphoreType.DMA((2,)),
-        ],
-        compiler_params=pltpu.CompilerParams(
-            collective_id=0, has_side_effects=True, vmem_limit_bytes=48 * 1024 * 1024
-        ),
-        name="gather_project",
-    )(send_slot.reshape(1, rows), gather_src.reshape(1, rows), hidden, qkv_weight, gate_down, w_beta)
-
-
-def delta_kernel(
-    lengths_ref, rate_ref, ext_ref, low_ref, beta_ref, conv_ref, up_ref, bias_ref, gain_ref,
-    out_ref,
-    stack, local, lift, maps, total, others, state, entry_out, entry,
-    xs_sem, xr_sem, zs_sem, zr_sem, bs_sem, br_sem,
-):
-    n_ctx = lax.axis_size("ctx")
-    n_groups = n_ctx // GROUP
-    me = lax.axis_index("ctx")
-    head = lax.axis_index("head")
-    member = lax.rem(me, GROUP)
-    group = me // GROUP
-    x, side = lax.rem(member, X_SIZE), member // X_SIZE
-    heads, rows, channels = local.shape
-    columns = heads * channels
-    half = channels // 2
-    blocks = rows // SPAN
-    base = me * rows
-
-    def at(ctx):
-        return {"ctx": ctx, "head": head}
-
-    def mate(index):
-        return at(group * GROUP + index)
-
-    barrier = pltpu.get_barrier_semaphore()
-    for k in range(1, GROUP):
-        pl.semaphore_signal(
-            barrier, inc=1, device_id=mate(lax.rem(member + k, GROUP)), device_id_type=MESH
-        )
-    for k in range(1, n_groups):
-        pl.semaphore_signal(
-            barrier, inc=1, device_id=at(lax.rem(me + k * GROUP, n_ctx)), device_id_type=MESH
-        )
+    for copy in loads[6:]:
+        copy.wait()
 
     ends, total_len = [], 0
     for i in range(lengths_ref.shape[0]):
@@ -332,7 +254,7 @@
     def block(v, b):
         return v[b * SPAN : (b + 1) * SPAN]
 
-    drive = mm(low_ref[...], up_ref[...]) + bias_ref[...]
+    drive = mm(acc_low[...].astype(BF16), up_ref[...]) + bias_ref[...]
     soft = jnp.maximum(drive, 0.0) + jnp.log1p(jnp.exp(-jnp.abs(drive)))
     rates = jnp.concatenate(
         [jnp.exp(jnp.full((1, channels), rate_ref[h], F32)) for h in range(heads)], axis=1
@@ -341,7 +263,8 @@
     d_high, d_mid = split(decay)
     d_low = (decay - d_high.astype(F32) - d_mid.astype(F32)).astype(BF16)
     cum_all = mm(running, d_high) + (mm(running, d_mid) + mm(running, d_low))
-    betas = 1.0 / (1.0 + jnp.exp(-beta_ref[...]))
+    betas = 1.0 / (1.0 + jnp.exp(-acc_beta[...]))
+    rim.wait_recv()
     acts = [activated(j) for j in range(3)]
 
     every = range(heads)
@@ -445,8 +368,6 @@
         stack[h, half : half + channels] = keeps[h] * eye_channels - summary[:channels]
         stack[h, half + channels :] = summary[channels + half :]
 
-    pl.semaphore_wait(barrier, GROUP + n_groups - 2)
-
     def map_copy(k):
         to = lax.rem(member + k, GROUP)
         start = pl.multiple_of((to // X_SIZE) * half, half)
@@ -560,25 +481,58 @@
         result = local[h] + mm3_narrow(split(lift[h]), split(incoming), NT)
         mean = jnp.mean(result * result, axis=-1, keepdims=True)
         scaled = result * lax.rsqrt(mean + 1e-05) * gain_ref[...]
-        out_ref[:, h * channels : (h + 1) * channels] = scaled.astype(BF16)
-
-    for copy in sends + returns:
+        lanes = pl.ds(h * channels, channels)
+        out_buf[:, lanes] = scaled.astype(BF16)
+        pltpu.make_async_copy(out_buf.at[:, lanes], out_hbm.at[:, lanes], out_sem.at[h]).start()
+
+    for to in peers:
+        slot_copy(to, me).wait_send()
+    for copy in passed + sends + returns:
         copy.wait_send()
+    rim.wait_send()
     for_later_groups(lambda copy: copy.wait_send())
-
-
-def delta(ext, low, beta, conv_weight, gate_up, a_log, dt_bias, norm_gain, prompt_lengths):
-    rows = low.shape[0]
-    heads = a_log.shape[0]
-    channels = norm_gain.shape[0]
-    n_groups = lax.axis_size("ctx") // GROUP
+    for h in every:
+        lanes = pl.ds(h * channels, channels)
+        pltpu.make_async_copy(out_buf.at[:, lanes], out_hbm.at[:, lanes], out_sem.at[h]).wait()
+
+
+def on_device(
+    hidden, qkv_weight, conv_weight, w_beta, gate_down, gate_up,
+    a_log, dt_bias, norm_gain, prompt_lengths, send_slot, gather_src,
+):
+    rows, width = hidden.shape
+    _, features, columns = qkv_weight.shape
+    n_ctx, n_head = lax.axis_size("ctx"), lax.axis_size("head")
+    n_y, n_groups = n_head // CORES, n_ctx // GROUP
+    heads, channels = a_log.shape[0], norm_gain.shape[0]
+    rank = gate_down.shape[1]
     half = channels // 2
+    slots = 2 * rows
+    dma = pltpu.SemaphoreType.DMA
     return pl.pallas_call(
-        delta_kernel,
-        out_shape=jax.ShapeDtypeStruct((rows, heads * channels), BF16),
-        in_specs=[SMEM, SMEM] + [VMEM] * 7,
-        out_specs=VMEM,
+        fused_kernel,
+        out_shape=jax.ShapeDtypeStruct((rows, columns), BF16),
+        in_specs=[SMEM, SMEM] + [HBM] * 10,
+        out_specs=HBM,
         scratch_shapes=[
+            pltpu.VMEM((1, rows), jnp.int32),
+            pltpu.VMEM((1, rows), jnp.int32),
+            pltpu.VMEM((width, rows), BF16),
+            pltpu.VMEM((3, features, columns), BF16),
+            pltpu.VMEM((features, rank), BF16),
+            pltpu.VMEM((heads, features), BF16),
+            pltpu.VMEM((3, CONV, columns), F32),
+            pltpu.VMEM((rank, columns), BF16),
+            pltpu.VMEM((1, columns), F32),
+            pltpu.VMEM((1, channels), F32),
+            pltpu.VMEM((slots, width), BF16),
+            pltpu.VMEM((slots, width), BF16),
+            pltpu.VMEM((features, rows), BF16),
+            pltpu.VMEM((n_y, 16, CORES * width), BF16),
+            pltpu.VMEM((3, rows, columns), F32),
+            pltpu.VMEM((rows, rank), F32),
+            pltpu.VMEM((rows, 16), F32),
+            pltpu.VMEM((RIM + rows, 3 * columns), F32),
             pltpu.VMEM((heads, 2 * channels, channels), F32),
             pltpu.VMEM((heads, rows, channels), F32),
             pltpu.VMEM((heads, rows, channels), F32),
@@ -588,30 +542,19 @@
             pltpu.VMEM((half, channels), F32),
             pltpu.VMEM((GROUP, half, channels), F32),
             pltpu.VMEM((GROUP, half, channels), F32),
-            pltpu.SemaphoreType.DMA((GROUP,)),
-            pltpu.SemaphoreType.DMA((GROUP,)),
-            pltpu.SemaphoreType.DMA((n_groups,)),
-            pltpu.SemaphoreType.DMA((n_groups,)),
-            pltpu.SemaphoreType.DMA((GROUP,)),
-            pltpu.SemaphoreType.DMA((GROUP,)),
+            pltpu.VMEM((rows, columns), BF16),
+            dma((10,)), dma((n_ctx,)), dma((n_ctx,)), dma((2 * n_y,)), dma((2 * n_y + 1,)), dma((2,)),
+            dma((GROUP,)), dma((GROUP,)), dma((n_groups,)), dma((n_groups,)), dma((GROUP,)), dma((GROUP,)),
+            dma((heads,)),
         ],
         compiler_params=pltpu.CompilerParams(
-            collective_id=1, has_side_effects=True, vmem_limit_bytes=48 * 1024 * 1024
+            collective_id=0, has_side_effects=True, vmem_limit_bytes=60 * 1024 * 1024
         ),
-        name="delta",
+        name="delta_prefill",
     )(
-        prompt_lengths, a_log, ext, low, beta, conv_weight, gate_up,
-        dt_bias.reshape(1, -1), norm_gain.reshape(1, -1),
-    )
-
-
-def on_device(
-    hidden, qkv_weight, conv_weight, w_beta, gate_down, gate_up,
-    a_log, dt_bias, norm_gain, prompt_lengths, send_slot, gather_src,
-):
-    ext, low, beta = gather_and_project(hidden.T, qkv_weight, gate_down, w_beta.T, send_slot, gather_src)
-    return delta(
-        ext, low, beta, conv_weight.transpose(1, 0, 2), gate_up, a_log, dt_bias, norm_gain, prompt_lengths
+        prompt_lengths, a_log, send_slot.reshape(1, rows), gather_src.reshape(1, rows), hidden.T,
+        qkv_weight, gate_down, w_beta.T, conv_weight.transpose(1, 0, 2), gate_up,
+        dt_bias.reshape(1, columns), norm_gain.reshape(1, channels),
     )
 
 

time: 76.3 us -> 71.1 us (0.932)
  the two profiles are of different devices: /device:TPU:224 before, /device:TPU:128 now
where the time goes in v3:
time: 71.1 us; the launch traced here: 69.7 us
  Pallas kernels  68.1 us (96%)
  local copies, waits for them, and re-layouts  1.67 us (2%)
    pallas_call x1, Pallas kernels, on_device(): pl.pallas_call(fused_kernel, out_shape=jax.ShapeDtypeStruct((rows, column...  68.1 us
    unnamed x1, local copies, waits for them, and re-layouts  1.67 us

profile of v3, /device:TPU:128, one launch (start us, length us, event | category | flops | bytes accessed | tf_op | source)
XLA Modules:
  0.0 69.7 jit_solution(16073299842199140362)
XLA Ops:
  0.0 68.1 %delta_prefill.1 = bf16[256,512]{1,0:T(8,128)(2,1)} custom-call(s32[4]{0:T(128)} %lengths_ref.1, f32[4]{0:T(128)} %rate_ref.1, s32[1,256]{1,0:T(1,128)} %bitcast.11, s32[1,256]{1,0:T(1,128)} %bitcast.12, bf16[288,256]{1,0:T(8,128)(2,1)} %bitcast.7, bf16[3,2304,512]{2,1,0:T(8,128)(2,1)} %wqkv_hbm.1, bf16[2304,128]{1,0:T(8,128)(2,1)} %wdown_hbm.1, ...), custom_call_target="tpu_custom_call" | custom-call | tf_op jit(solution)/shard_map/delta_prefill/pallas_call | solution.py:512
  68.1 1.7 %copy.14 = bf16[256,512]{1,0:T(8,128)(2,1)} copy(bf16[256,512]{1,0:T(8,128)(2,1)} %delta_prefill.1) | data formatting | bytes 524288

commit v4 on v3

--- a/solution.py
+++ b/solution.py
@@ -13,6 +13,7 @@
 X_SIZE = 4
 CORES = 2
 GROUP = 8
+KEEP = 16
 MESH = pl.DeviceIdType.MESH
 F32 = jnp.float32
 BF16 = jnp.bfloat16
@@ -234,56 +235,70 @@
     small_block = small_col // SPAN
     small_eye = (small_apart == 0).astype(F32)
 
-    def activated(j):
+    every = range(heads)
+    nothing = jnp.zeros((1, channels), F32)
+
+    def of_head(v, h):
+        return v[:, h * channels : (h + 1) * channels]
+
+    def block(v, b):
+        return v[b * SPAN : (b + 1) * SPAN]
+
+    def activated(j, first, size):
         lanes = slice(j * columns, (j + 1) * columns)
         out = None
         for tap in range(CONV):
             shift = CONV - 1 - tap
-            part = conv_ref[j, tap : tap + 1, :] * ext_ref[pl.ds(RIM - shift, rows), lanes]
+            part = conv_ref[j, tap : tap + 1, :] * ext_ref[pl.ds(RIM - shift + first, size), lanes]
             if shift:
-                part = part * jnp.concatenate([valid[shift]] * heads, axis=1)
+                part = part * jnp.concatenate([valid[shift][first : first + size]] * heads, axis=1)
             out = part if out is None else out + part
         return out / (1.0 + jnp.exp(-out))
 
-    def of_head(v, h):
-        return v[:, h * channels : (h + 1) * channels]
-
     def unit(v):
         return v * lax.rsqrt(jnp.sum(v * v, axis=-1, keepdims=True) + 1e-06)
 
-    def block(v, b):
-        return v[b * SPAN : (b + 1) * SPAN]
+    def activations(first, size):
+        query, key, value = [activated(j, first, size) for j in range(3)]
+        return (
+            [unit(of_head(query, h)) * channels ** (-0.5) for h in every],
+            [unit(of_head(key, h)) for h in every],
+            [of_head(value, h) for h in every],
+        )
 
     drive = mm(acc_low[...].astype(BF16), up_ref[...]) + bias_ref[...]
     soft = jnp.maximum(drive, 0.0) + jnp.log1p(jnp.exp(-jnp.abs(drive)))
-    rates = jnp.concatenate(
-        [jnp.exp(jnp.full((1, channels), rate_ref[h], F32)) for h in range(heads)], axis=1
-    )
+    rates = jnp.concatenate([jnp.exp(jnp.full((1, channels), rate_ref[h], F32)) for h in every], axis=1)
     decay = -rates * soft
     d_high, d_mid = split(decay)
     d_low = (decay - d_high.astype(F32) - d_mid.astype(F32)).astype(BF16)
     cum_all = mm(running, d_high) + (mm(running, d_mid) + mm(running, d_low))
     betas = 1.0 / (1.0 + jnp.exp(-acc_beta[...]))
-    rim.wait_recv()
-    acts = [activated(j) for j in range(3)]
-
-    every = range(heads)
     cums = [of_head(cum_all, h) for h in every]
     strengths = [jnp.broadcast_to(betas[:, h : h + 1], (rows, channels)) for h in every]
-    queries = [unit(of_head(acts[0], h)) * channels ** (-0.5) for h in every]
-    keys = [unit(of_head(acts[1], h)) for h in every]
-    values = [strengths[h] * of_head(acts[2], h) for h in every]
     lasts = [[cums[h][(b + 1) * SPAN - 1 : (b + 1) * SPAN] for b in range(blocks)] for h in every]
-    nothing = jnp.zeros((1, channels), F32)
+    grows = [jnp.exp(c) for c in cums]
+    shrinks = [jnp.exp(-c) for c in cums]
+    fades = [
+        jnp.concatenate([jnp.exp(lasts[h][b] - block(cums[h], b)) for b in range(blocks)], axis=0)
+        for h in every
+    ]
+    later_rows = activations(SPAN, rows - SPAN)
+    rim.wait_recv()
+    first_rows = activations(0, SPAN)
+    queries, keys, values = [
+        [jnp.concatenate([a, b], axis=0) for a, b in zip(f, l)] for f, l in zip(first_rows, later_rows)
+    ]
+    values = [strengths[h] * values[h] for h in every]
 
     lower, score, solved = [], [], []
     bk_ups, q_ups, tails = [], [], []
     for h in every:
-        grow = jnp.exp(cums[h])
-        bk_ups.append(strengths[h] * keys[h] * grow)
-        q_ups.append(queries[h] * grow)
-        key_down = keys[h] * jnp.exp(-cums[h])
-        tails.append([block(keys[h], b) * jnp.exp(lasts[h][b] - block(cums[h], b)) for b in range(blocks)])
+        bk_ups.append(strengths[h] * keys[h] * grows[h])
+        q_ups.append(queries[h] * grows[h])
+        key_down = keys[h] * shrinks[h]
+        tail = keys[h] * fades[h]
+        tails.append([block(tail, b) for b in range(blocks)])
         mixes, reads = [], []
         for i in range(blocks):
             cols = []
@@ -362,57 +377,90 @@
         lax.broadcasted_iota(jnp.int32, (channels, channels), 0)
         == lax.broadcasted_iota(jnp.int32, (channels, channels), 1)
     ).astype(F32)
+    keep_at, late_at = half + channels, half + channels + KEEP
+    message = late_at
+
+    def keep_rows(keep):
+        high, middle = split(keep)
+        low = (keep - high.astype(F32) - middle.astype(F32)).astype(BF16)
+        return jnp.concatenate([high, middle, low, jnp.zeros((KEEP - 3, channels), BF16)], axis=0)
+
+    def keep_of(rows3):
+        wide = rows3.astype(F32)
+        return wide[0:1] + (wide[1:2] + wide[2:3])
+
     for h in every:
-        summary = mm3(solved[h], ends_k[h], TN)
-        stack[h, :half] = summary[channels : channels + half]
-        stack[h, half : half + channels] = keeps[h] * eye_channels - summary[:channels]
-        stack[h, half + channels :] = summary[channels + half :]
-
-    def map_copy(k):
-        to = lax.rem(member + k, GROUP)
+        summary = mm3(solved[h], ends_k[h], TN).astype(BF16)
+        stack[h, :half, :] = summary[channels : channels + half]
+        stack[h, half:keep_at, :] = -summary[:channels]
+        stack[h, keep_at:late_at, :] = keep_rows(keeps[h])
+        stack[h, late_at:, :] = summary[channels + half :]
+
+    mates = [(1, 2), (1, 1), (1, 3), (0, 2), (1, 0), (0, 1), (0, 3)]
+    mates = [lax.rem(side + ds, 2) * X_SIZE + lax.rem(x + dx, X_SIZE) for ds, dx in mates]
+
+    def map_copy(k, to):
         start = pl.multiple_of((to // X_SIZE) * half, half)
         return pltpu.make_async_remote_copy(
-            src_ref=stack.at[lax.rem(to, X_SIZE), pl.ds(start, channels + half), :],
+            src_ref=stack.at[lax.rem(to, X_SIZE), pl.ds(start, message), :],
             dst_ref=maps.at[member],
             send_sem=xs_sem.at[k], recv_sem=xr_sem.at[member],
             device_id=mate(to), device_id_type=MESH,
         )
 
-    sends = [map_copy(k) for k in range(1, GROUP)]
+    sends = [map_copy(k, to) for k, to in enumerate(mates)]
     for copy in sends:
         copy.start()
-    maps[member] = stack[x, pl.ds(pl.multiple_of(side * half, half), channels + half), :]
+    maps[member] = stack[x, pl.ds(pl.multiple_of(side * half, half), message), :]
 
     for h in every:
         combined = mm3(split(jnp.concatenate(score[h], axis=0)), solved[h])
         lift[h] = full_queries[h] - combined[:, :channels]
         local[h] = combined[:, channels:]
 
-    for k in range(1, GROUP):
-        frm = lax.rem(member + k, GROUP)
+    for frm in mates:
         pltpu.make_async_remote_copy(
             src_ref=maps.at[frm], dst_ref=maps.at[frm],
-            send_sem=xs_sem.at[k], recv_sem=xr_sem.at[frm],
+            send_sem=xs_sem.at[0], recv_sem=xr_sem.at[frm],
             device_id=mate(frm), device_id_type=MESH,
         ).wait_recv()
 
     map_at = pl.ds(pl.multiple_of((1 - side) * half, half), channels)
-    feed_at = pl.ds(pl.multiple_of(side * channels, channels), half)
-
-    def follow(whole, step):
-        moved = mm3_narrow(split(whole), split(step[:channels]))
-        return jnp.concatenate([moved[:channels], moved[channels:] + step[channels:]], axis=0)
-
-    steps = [jnp.concatenate([maps[j, map_at, :], maps[j, feed_at, :]], axis=0) for j in range(GROUP)]
-    prefixes = [steps[0]]
-    late = [steps[X_SIZE]]
+    keeps_at = pl.ds(pl.multiple_of(channels + (1 - side) * half, 16), KEEP)
+    feed_at = pl.ds(pl.multiple_of(side * (channels + KEEP), 16), half)
+
+    def apply(v, keep, exact_map):
+        parts = jnp.concatenate(split(v), axis=1)
+        return v * keep + mm(parts, jnp.concatenate([exact_map, exact_map], axis=0))
+
+    def follow(whole, j):
+        moved = apply(whole, step_keeps[j], maps[j, map_at, :])
+        return jnp.concatenate([moved[:channels], moved[channels:] + maps[j, feed_at, :].astype(F32)], axis=0)
+
+    def single(j):
+        return jnp.concatenate(
+            [step_keeps[j] * eye_channels + maps[j, map_at, :].astype(F32), maps[j, feed_at, :].astype(F32)], axis=0
+        )
+
+    def join(first, second):
+        moved = mm3_narrow(split(first), split(second[:channels]))
+        return jnp.concatenate([moved[:channels], moved[channels:] + second[channels:]], axis=0)
+
+    step_keeps = [keep_of(maps[j, keeps_at, :]) for j in range(GROUP)]
+    prefixes = [single(0)]
+    late = [single(X_SIZE)]
     for j in range(1, X_SIZE):
-        prefixes.append(follow(prefixes[-1], steps[j]))
-        late.append(follow(late[-1], steps[X_SIZE + j]))
-    total[...] = follow(prefixes[-1], late[-1])
+        prefixes.append(follow(prefixes[-1], j))
+        late.append(follow(late[-1], X_SIZE + j))
+    group_total = join(prefixes[-1], late[-1])
+    group_keep = functools.reduce(lambda a, b: a * b, step_keeps)
+    total[:channels, :] = (group_total[:channels] - group_keep * eye_channels).astype(BF16)
+    total[channels : channels + KEEP, :] = keep_rows(group_keep)
+    total[channels + KEEP :, :] = group_total[channels:].astype(BF16)
+    whole_span, feed_span = pl.ds(0, message), pl.ds(channels + KEEP, half)
 
     def total_copy(k, only_feed):
-        span = pl.ds(channels, half) if only_feed else pl.ds(0, channels + half)
+        span = feed_span if only_feed else whole_span
         return pltpu.make_async_remote_copy(
             src_ref=total.at[span, :], dst_ref=others.at[group, span, :],
             send_sem=zs_sem.at[k], recv_sem=zr_sem.at[group],
@@ -432,53 +480,54 @@
 
     for_later_groups(lambda copy: copy.start())
     for j in range(X_SIZE - 1):
-        prefixes.append(follow(prefixes[X_SIZE - 1], late[j]))
+        prefixes.append(join(prefixes[X_SIZE - 1], late[j]))
     into = split(jnp.concatenate([p[:channels] for p in prefixes], axis=1))
 
     state[...] = jnp.zeros_like(state)
     for frm in range(n_groups - 1):
         @pl.when(group > frm)
         def _():
-            span = pl.ds(channels, half) if frm == 0 else pl.ds(0, channels + half)
+            span = whole_span if frm else feed_span
             pltpu.make_async_remote_copy(
                 src_ref=total.at[span, :], dst_ref=others.at[frm, span, :],
                 send_sem=zs_sem.at[0], recv_sem=zr_sem.at[frm],
                 device_id=at(lax.rem(me + GROUP, n_ctx)), device_id_type=MESH,
             ).wait_recv()
-            feed = others[frm, pl.ds(channels, half), :]
+            feed = others[frm, feed_span, :].astype(F32)
             if frm:
-                feed = feed + mm3_narrow(split(state[...]), split(others[frm, pl.ds(0, channels), :]))
+                keep = keep_of(others[frm, pl.ds(channels, KEEP), :])
+                feed = feed + apply(state[...], keep, others[frm, pl.ds(0, channels), :])
             state[...] = feed
 
     start_state = state[...]
     moved = mm3_narrow(split(start_state), into)
-    entry_out[0] = start_state
+    entry_out[0] = start_state.astype(BF16)
     for j in range(1, GROUP):
-        entry_out[j] = moved[:, (j - 1) * channels : j * channels] + prefixes[j - 1][channels:]
-
-    def entry_copy(k):
-        to = lax.rem(member + k, GROUP)
+        there_state = moved[:, (j - 1) * channels : j * channels] + prefixes[j - 1][channels:]
+        entry_out[j] = there_state.astype(BF16)
+
+    def entry_copy(k, to):
         return pltpu.make_async_remote_copy(
             src_ref=entry_out.at[to], dst_ref=entry.at[member],
             send_sem=bs_sem.at[k], recv_sem=br_sem.at[member],
             device_id=mate(to), device_id_type=MESH,
         )
 
-    returns = [entry_copy(k) for k in range(1, GROUP)]
+    returns = [entry_copy(k, to) for k, to in enumerate(mates)]
     for copy in returns:
         copy.start()
     entry[member] = entry_out[member]
-    for k in range(1, GROUP):
-        frm = lax.rem(member + k, GROUP)
+    for frm in mates:
         pltpu.make_async_remote_copy(
             src_ref=entry_out.at[frm], dst_ref=entry.at[frm],
-            send_sem=bs_sem.at[k], recv_sem=br_sem.at[frm],
+            send_sem=bs_sem.at[0], recv_sem=br_sem.at[frm],
             device_id=mate(frm), device_id_type=MESH,
         ).wait_recv()
 
     for h in every:
         incoming = jnp.concatenate([entry[h], entry[X_SIZE + h]], axis=0)
-        result = local[h] + mm3_narrow(split(lift[h]), split(incoming), NT)
+        parts = jnp.concatenate(split(lift[h]), axis=1)
+        result = local[h] + mm(parts, jnp.concatenate([incoming, incoming], axis=1), NT)
         mean = jnp.mean(result * result, axis=-1, keepdims=True)
         scaled = result * lax.rsqrt(mean + 1e-05) * gain_ref[...]
         lanes = pl.ds(h * channels, channels)
@@ -507,6 +556,7 @@
     heads, channels = a_log.shape[0], norm_gain.shape[0]
     rank = gate_down.shape[1]
     half = channels // 2
+    message = channels + KEEP + half
     slots = 2 * rows
     dma = pltpu.SemaphoreType.DMA
     return pl.pallas_call(
@@ -533,15 +583,15 @@
             pltpu.VMEM((rows, rank), F32),
             pltpu.VMEM((rows, 16), F32),
             pltpu.VMEM((RIM + rows, 3 * columns), F32),
-            pltpu.VMEM((heads, 2 * channels, channels), F32),
+            pltpu.VMEM((heads, 2 * channels + KEEP, channels), BF16),
             pltpu.VMEM((heads, rows, channels), F32),
             pltpu.VMEM((heads, rows, channels), F32),
-            pltpu.VMEM((GROUP, channels + half, channels), F32),
-            pltpu.VMEM((channels + half, channels), F32),
-            pltpu.VMEM((n_groups, channels + half, channels), F32),
+            pltpu.VMEM((GROUP, message, channels), BF16),
+            pltpu.VMEM((message, channels), BF16),
+            pltpu.VMEM((n_groups, message, channels), BF16),
             pltpu.VMEM((half, channels), F32),
-            pltpu.VMEM((GROUP, half, channels), F32),
-            pltpu.VMEM((GROUP, half, channels), F32),
+            pltpu.VMEM((GROUP, half, channels), BF16),
+            pltpu.VMEM((GROUP, half, channels), BF16),
             pltpu.VMEM((rows, columns), BF16),
             dma((10,)), dma((n_ctx,)), dma((n_ctx,)), dma((2 * n_y,)), dma((2 * n_y + 1,)), dma((2,)),
             dma((GROUP,)), dma((GROUP,)), dma((n_groups,)), dma((n_groups,)), dma((GROUP,)), dma((GROUP,)),

time: 71.1 us -> 61.4 us (0.86)
  the two profiles are of different devices: /device:TPU:128 before, /device:TPU:224 now
where the time goes in v4:
time: 61.4 us; the launch traced here: 61.3 us
  Pallas kernels  59.6 us (97%)
  local copies, waits for them, and re-layouts  1.67 us (3%)
    pallas_call x1, Pallas kernels, on_device(): pl.pallas_call(fused_kernel, out_shape=jax.ShapeDtypeStruct((rows, column...  59.6 us
    unnamed x1, local copies, waits for them, and re-layouts  1.67 us

profile of v4, /device:TPU:224, one launch (start us, length us, event | category | flops | bytes accessed | tf_op | source)
XLA Modules:
  0.0 61.3 jit_solution(9150321936203654641)
XLA Ops:
  0.0 59.6 %delta_prefill.1 = bf16[256,512]{1,0:T(8,128)(2,1)} custom-call(s32[4]{0:T(128)} %lengths_ref.1, f32[4]{0:T(128)} %rate_ref.1, s32[1,256]{1,0:T(1,128)} %bitcast.11, s32[1,256]{1,0:T(1,128)} %bitcast.12, bf16[288,256]{1,0:T(8,128)(2,1)} %bitcast.7, bf16[3,2304,512]{2,1,0:T(8,128)(2,1)} %wqkv_hbm.1, bf16[2304,128]{1,0:T(8,128)(2,1)} %wdown_hbm.1, ...), custom_call_target="tpu_custom_call" | custom-call | tf_op jit(solution)/shard_map/delta_prefill/pallas_call | solution.py:562
  59.6 1.7 %copy.14 = bf16[256,512]{1,0:T(8,128)(2,1)} copy(bf16[256,512]{1,0:T(8,128)(2,1)} %delta_prefill.1) | data formatting | bytes 524288

commit v5 on v4

--- a/solution.py
+++ b/solution.py
@@ -17,6 +17,7 @@
 MESH = pl.DeviceIdType.MESH
 F32 = jnp.float32
 BF16 = jnp.bfloat16
+VMEM = pl.BlockSpec(memory_space=pltpu.VMEM)
 SMEM = pl.BlockSpec(memory_space=pltpu.SMEM)
 HBM = pl.BlockSpec(memory_space=pltpu.HBM)
 
@@ -47,12 +48,12 @@
 def fused_kernel(
     lengths_ref, rate_ref, slot_hbm, src_hbm, hidden_hbm, wqkv_hbm, wdown_hbm, wbeta_hbm,
     conv_hbm, up_hbm, bias_hbm, gain_hbm,
-    out_hbm,
+    out_ref,
     slot_buf, src_buf, hidden_buf, w_qkv, w_down, wbeta_buf, conv_ref, up_ref, bias_ref, gain_ref,
     send_buf, landed, shards, w_beta, acc, acc_low, acc_beta, ext_ref,
-    stack, local, lift, maps, total, others, state, entry_out, entry, out_buf,
+    stack, local, lift, maps, total, others, state, entry_out, entry,
     in_sem, s_sem, r_sem, hs_sem, hr_sem, rim_sem,
-    xs_sem, xr_sem, zs_sem, zr_sem, bs_sem, br_sem, out_sem,
+    xs_sem, xr_sem, zs_sem, zr_sem, bs_sem, br_sem,
 ):
     n_ctx = lax.axis_size("ctx")
     n_z = n_ctx // X_SIZE
@@ -138,8 +139,11 @@
 
     shards[features(head), :] = mm(landed[...], pick, TN).astype(BF16)
     middle = width // 2
-
-    def shard_copy(index, to, send, recv, start=0, size=None):
+    parts_of = ((0, middle), (middle, width - middle))
+    passed = []
+
+    def shard_copy(index, to, send, recv, part=None):
+        start, size = (0, width) if part is None else parts_of[part]
         return pltpu.make_async_remote_copy(
             src_ref=shards.at[features(index, start, size), :],
             dst_ref=shards.at[features(index, start, size), :],
@@ -147,54 +151,66 @@
             device_id={"ctx": me, "head": to}, device_id_type=MESH,
         )
 
+    def push(index, to, recv, part=None):
+        copy = shard_copy(index, to, len(passed), recv, part)
+        copy.start()
+        passed.append(copy)
+
     here = [ring[dy] * CORES + core for dy in range(n_y)]
     there = [ring[dy] * CORES + (1 - core) for dy in range(n_y)]
-    up_y, down_y = here[1], here[n_y - 1]
-    passed = [
-        shard_copy(head, up_y, 0, n_y - 1),
-        shard_copy(head, down_y, 1, 1),
-        shard_copy(head, sibling, 2, n_y + 1),
-    ]
-    for copy in passed:
-        copy.start()
+    up_y, down_y, across = here[1], here[n_y - 1], 2 * n_y
+    push(head, up_y, 2 * 3, 0)
+    push(head, down_y, 2 * 1 + 1, 1)
+    push(head, sibling, across)
+    push(head, up_y, 2 * 3 + 1, 1)
+    push(head, down_y, 2 * 1, 0)
     for copy in loads[4:6]:
         copy.wait()
 
-    def multiply(dy, first=False):
+    def landed_half(dy, part, other=False):
+        index, offset = (there[dy], across) if other else (here[dy], 0)
+        shard_copy(index, sibling, 0, offset + 2 * dy + part, part).wait_recv()
+
+    def products(dy):
         part = shards[pl.ds(pl.multiple_of(ring[dy] * pair, 16), pair), :].T
         chunk = pl.ds(pl.multiple_of(ring[dy] * pair, 16), pair)
-        products = [mm(part, w_qkv[j, chunk, :]) for j in range(3)]
-        low = mm(part, w_down[chunk, :])
-        beta = mm(part, w_beta[ring[dy]], NT)
-        for j in range(3):
-            acc[j] = products[j] if first else acc[j] + products[j]
-        acc_low[...] = low if first else acc_low[...] + low
-        acc_beta[...] = beta if first else acc_beta[...] + beta
-
-    def pass_on(copy):
-        copy.start()
-        passed.append(copy)
-
-    shard_copy(there[0], sibling, 2, n_y + 1).wait_recv()
+        return [mm(part, w_qkv[j, chunk, :]) for j in range(3)] + [
+            mm(part, w_down[chunk, :]), mm(part, w_beta[ring[dy]], NT)
+        ]
+
+    def multiply(dy, first=False):
+        for ref, value in zip(sums, products(dy)):
+            ref[...] = value if first else ref[...] + value
+
+    sums = [acc.at[0], acc.at[1], acc.at[2], acc_low, acc_beta]
+    shard_copy(there[0], sibling, 0, across).wait_recv()
     multiply(0, True)
-    shard_copy(here[3], sibling, 3, 3).wait_recv()
-    pass_on(shard_copy(here[3], up_y, 3, 2, 0, middle))
-    pass_on(shard_copy(here[3], sibling, 4, n_y + 1 + 3))
-    shard_copy(here[1], sibling, 5, 1).wait_recv()
-    pass_on(shard_copy(here[1], down_y, 5, n_y, middle, width - middle))
-    pass_on(shard_copy(here[1], sibling, 6, n_y + 1 + 1))
-    shard_copy(there[3], sibling, 4, n_y + 1 + 3).wait_recv()
+    landed_half(3, 0)
+    push(here[3], up_y, 2 * 2, 0)
+    landed_half(1, 1)
+    push(here[1], down_y, 2 * 2 + 1, 1)
+    push(here[3], sibling, across + 2 * 3, 0)
+    push(here[1], sibling, across + 2 * 1 + 1, 1)
+    landed_half(3, 1)
+    push(here[3], sibling, across + 2 * 3 + 1, 1)
+    landed_half(1, 0)
+    push(here[1], sibling, across + 2 * 1, 0)
+    landed_half(3, 0, True)
+    landed_half(3, 1, True)
     multiply(3)
-    shard_copy(here[2], sibling, 7, 2, 0, middle).wait_recv()
-    shard_copy(here[2], sibling, 7, n_y, middle, width - middle).wait_recv()
-    pass_on(shard_copy(here[2], sibling, 7, n_y + 1 + 2))
-    shard_copy(there[1], sibling, 6, n_y + 1 + 1).wait_recv()
+    landed_half(2, 0)
+    push(here[2], sibling, across + 2 * 2, 0)
+    landed_half(2, 1)
+    push(here[2], sibling, across + 2 * 2 + 1, 1)
+    landed_half(1, 0, True)
+    landed_half(1, 1, True)
     multiply(1)
-    shard_copy(there[2], sibling, 7, n_y + 1 + 2).wait_recv()
-    multiply(2)
-
+    landed_half(2, 0, True)
+    landed_half(2, 1, True)
+    last = [ref[...] + value for ref, value in zip(sums, products(2))]
     for j in range(3):
-        ext_ref[RIM:, j * columns : (j + 1) * columns] = acc[j].astype(BF16).astype(F32)
+        ext_ref[RIM:, j * columns : (j + 1) * columns] = last[j].astype(BF16).astype(F32)
+    low_rank, beta_logit = last[3].astype(BF16), last[4]
     rim = pltpu.make_async_remote_copy(
         src_ref=ext_ref.at[pl.ds(rows, RIM), :], dst_ref=ext_ref.at[pl.ds(0, RIM), :],
         send_sem=rim_sem.at[0], recv_sem=rim_sem.at[1],
@@ -266,14 +282,14 @@
             [of_head(value, h) for h in every],
         )
 
-    drive = mm(acc_low[...].astype(BF16), up_ref[...]) + bias_ref[...]
+    drive = mm(low_rank, up_ref[...]) + bias_ref[...]
     soft = jnp.maximum(drive, 0.0) + jnp.log1p(jnp.exp(-jnp.abs(drive)))
     rates = jnp.concatenate([jnp.exp(jnp.full((1, channels), rate_ref[h], F32)) for h in every], axis=1)
     decay = -rates * soft
     d_high, d_mid = split(decay)
     d_low = (decay - d_high.astype(F32) - d_mid.astype(F32)).astype(BF16)
     cum_all = mm(running, d_high) + (mm(running, d_mid) + mm(running, d_low))
-    betas = 1.0 / (1.0 + jnp.exp(-acc_beta[...]))
+    betas = 1.0 / (1.0 + jnp.exp(-beta_logit))
     cums = [of_head(cum_all, h) for h in every]
     strengths = [jnp.broadcast_to(betas[:, h : h + 1], (rows, channels)) for h in every]
     lasts = [[cums[h][(b + 1) * SPAN - 1 : (b + 1) * SPAN] for b in range(blocks)] for h in every]
@@ -468,7 +484,7 @@
         )
 
     def for_later_groups(act):
-        for k in range(1, n_groups):
+        for k in sorted(range(1, n_groups), key=lambda k: -min(k, n_groups - k)):
             @pl.when((group > 0) & (group + k < n_groups))
             def _():
                 act(total_copy(k, False))
@@ -530,9 +546,7 @@
         result = local[h] + mm(parts, jnp.concatenate([incoming, incoming], axis=1), NT)
         mean = jnp.mean(result * result, axis=-1, keepdims=True)
         scaled = result * lax.rsqrt(mean + 1e-05) * gain_ref[...]
-        lanes = pl.ds(h * channels, channels)
-        out_buf[:, lanes] = scaled.astype(BF16)
-        pltpu.make_async_copy(out_buf.at[:, lanes], out_hbm.at[:, lanes], out_sem.at[h]).start()
+        out_ref[:, h * channels : (h + 1) * channels] = scaled.astype(BF16)
 
     for to in peers:
         slot_copy(to, me).wait_send()
@@ -540,9 +554,6 @@
         copy.wait_send()
     rim.wait_send()
     for_later_groups(lambda copy: copy.wait_send())
-    for h in every:
-        lanes = pl.ds(h * channels, channels)
-        pltpu.make_async_copy(out_buf.at[:, lanes], out_hbm.at[:, lanes], out_sem.at[h]).wait()
 
 
 def on_device(
@@ -559,11 +570,11 @@
     message = channels + KEEP + half
     slots = 2 * rows
     dma = pltpu.SemaphoreType.DMA
-    return pl.pallas_call(
+    call = pl.pallas_call(
         fused_kernel,
         out_shape=jax.ShapeDtypeStruct((rows, columns), BF16),
         in_specs=[SMEM, SMEM] + [HBM] * 10,
-        out_specs=HBM,
+        out_specs=VMEM,
         scratch_shapes=[
             pltpu.VMEM((1, rows), jnp.int32),
             pltpu.VMEM((1, rows), jnp.int32),
@@ -592,20 +603,20 @@
             pltpu.VMEM((half, channels), F32),
             pltpu.VMEM((GROUP, half, channels), BF16),
             pltpu.VMEM((GROUP, half, channels), BF16),
-            pltpu.VMEM((rows, columns), BF16),
-            dma((10,)), dma((n_ctx,)), dma((n_ctx,)), dma((2 * n_y,)), dma((2 * n_y + 1,)), dma((2,)),
+            dma((10,)), dma((n_ctx,)), dma((n_ctx,)), dma((13,)), dma((4 * n_y,)), dma((2,)),
             dma((GROUP,)), dma((GROUP,)), dma((n_groups,)), dma((n_groups,)), dma((GROUP,)), dma((GROUP,)),
-            dma((heads,)),
         ],
         compiler_params=pltpu.CompilerParams(
-            collective_id=0, has_side_effects=True, vmem_limit_bytes=60 * 1024 * 1024
+            collective_id=0, has_side_effects=True, vmem_limit_bytes=48 * 1024 * 1024
         ),
         name="delta_prefill",
-    )(
+    )
+    operands = (
         prompt_lengths, a_log, send_slot.reshape(1, rows), gather_src.reshape(1, rows), hidden.T,
         qkv_weight, gate_down, w_beta.T, conv_weight.transpose(1, 0, 2), gate_up,
         dt_bias.reshape(1, columns), norm_gain.reshape(1, channels),
     )
+    return call(*[pltpu.with_memory_space_constraint(v, pltpu.HBM) for v in operands])
 
 
 def solution(mesh):

time: 61.4 us -> 58.5 us (0.953)
  the two profiles are of different devices: /device:TPU:224 before, /device:TPU:128 now
where the time goes in v5:
time: 58.5 us; the launch traced here: 57.7 us
  Pallas kernels  57 us (97%)
  local copies, waits for them, and re-layouts  0.71 us (1%)
    pallas_call x1, Pallas kernels, on_device(): call(*[pltpu.with_memory_space_constraint(v, pltpu.HBM) for v in operands])  57 us

profile of v5, /device:TPU:128, one launch (start us, length us, event | category | flops | bytes accessed | tf_op | source)
XLA Modules:
  0.0 57.7 jit_solution(7737337215112187291)
XLA Ops:
  0.0 57.0 %delta_prefill.1 = bf16[256,512]{1,0:T(8,128)(2,1)S(1)} custom-call(s32[4]{0:T(128)} %lengths_ref.1, f32[4]{0:T(128)} %rate_ref.1, s32[1,256]{1,0:T(1,128)} %bitcast.11, s32[1,256]{1,0:T(1,128)} %bitcast.12, bf16[288,256]{1,0:T(8,128)(2,1)} %bitcast.7, bf16[3,2304,512]{2,1,0:T(8,128)(2,1)} %wqkv_hbm.1, bf16[2304,128]{1,0:T(8,128)(2,1)} %wdown_hbm.1, ...), custom_call_target="tpu_custom_call" | custom-call | tf_op jit(solution)/shard_map/delta_prefill/pallas_call | solution.py:619
  57.0 0.7 %copy.14 = bf16[256,512]{1,0:T(8,128)(2,1)} copy(bf16[256,512]{1,0:T(8,128)(2,1)S(1)} %delta_prefill.1) | data formatting | bytes 524288

commit v6 on v5

--- a/solution.py
+++ b/solution.py
@@ -14,6 +14,7 @@
 CORES = 2
 GROUP = 8
 KEEP = 16
+LANES = 128
 MESH = pl.DeviceIdType.MESH
 F32 = jnp.float32
 BF16 = jnp.bfloat16
@@ -50,7 +51,7 @@
     conv_hbm, up_hbm, bias_hbm, gain_hbm,
     out_ref,
     slot_buf, src_buf, hidden_buf, w_qkv, w_down, wbeta_buf, conv_ref, up_ref, bias_ref, gain_ref,
-    send_buf, landed, shards, w_beta, acc, acc_low, acc_beta, ext_ref,
+    send_a, send_b, send_c, landed_a, landed_b, landed_c, shards, w_beta, acc, acc_low, acc_beta, ext_ref,
     stack, local, lift, maps, total, others, state, entry_out, entry,
     in_sem, s_sem, r_sem, hs_sem, hr_sem, rim_sem,
     xs_sem, xr_sem, zs_sem, zr_sem, bs_sem, br_sem,
@@ -69,7 +70,7 @@
     group = me // GROUP
     x, side = lax.rem(member, X_SIZE), member // X_SIZE
     width, rows = hidden_buf.shape
-    slots = send_buf.shape[0]
+    slots = send_a.shape[0]
     cap = slots // n_ctx
     heads, _, channels = local.shape
     columns = heads * channels
@@ -102,111 +103,115 @@
     barrier = pltpu.get_barrier_semaphore()
     for to in peers:
         pl.semaphore_signal(barrier, inc=1, device_id=at(to), device_id_type=MESH)
-    for to in (ring[1] * CORES + core, ring[n_y - 1] * CORES + core, sibling):
+    here = [ring[dy] * CORES + core for dy in range(n_y)]
+    there = [ring[dy] * CORES + (1 - core) for dy in range(n_y)]
+    for to in here[1:] + [sibling]:
         pl.semaphore_signal(barrier, inc=1, device_id={"ctx": me, "head": to}, device_id_type=MESH)
 
     for copy in loads[:4]:
         copy.wait()
     slot_ids = lax.broadcasted_iota(jnp.int32, (slots, rows), 0)
     place = (slot_ids == slot_buf[...]).astype(F32).astype(BF16)
-    send_buf[...] = mm(place, hidden_buf[...], NT).astype(BF16)
+    spans, start = [], 0
+    while start < width:
+        spans.append((start, min(LANES, width - start)))
+        start += LANES
+    sent, landed = (send_a, send_b, send_c), (landed_a, landed_b, landed_c)
+    for c, (start, size) in enumerate(spans):
+        sent[c][...] = mm(place, hidden_buf[start : start + size, :], NT).astype(BF16)
     pick = (slot_ids == src_buf[...]).astype(F32).astype(BF16)
-    pair = CORES * width
     w_beta[...] = jnp.zeros_like(w_beta)
-    for i in range(n_y):
-        w_beta[i, : wbeta_buf.shape[0], :] = wbeta_buf[:, i * pair : (i + 1) * pair]
-
-    pl.semaphore_wait(barrier, n_ctx - 1 + 3)
+    for c, (start, size) in enumerate(spans):
+        for i in range(n_head):
+            at_lane = i * width + start
+            w_beta[c, : wbeta_buf.shape[0], i * size : (i + 1) * size] = wbeta_buf[:, at_lane : at_lane + size]
+
+    pl.semaphore_wait(barrier, n_ctx - 1 + n_y)
 
     def slots_of(index):
         return pl.ds(pl.multiple_of(index * cap, cap), cap)
 
-    def slot_copy(to, frm):
+    def slot_copy(c, to, frm):
         return pltpu.make_async_remote_copy(
-            src_ref=send_buf.at[slots_of(to), :], dst_ref=landed.at[slots_of(frm), :],
-            send_sem=s_sem.at[to], recv_sem=r_sem.at[frm],
+            src_ref=sent[c].at[slots_of(to), :], dst_ref=landed[c].at[slots_of(frm), :],
+            send_sem=s_sem.at[c * n_ctx + to], recv_sem=r_sem.at[c * n_ctx + frm],
             device_id=at(to), device_id_type=MESH,
         )
 
-    for to in peers:
-        slot_copy(to, me).start()
-    landed[slots_of(me), :] = send_buf[slots_of(me), :]
-    for frm in reversed(peers):
-        slot_copy(frm, frm).wait_recv()
-
-    def features(index, start=0, size=None):
-        return pl.ds(pl.multiple_of(index * width + start, 16), width if size is None else size)
-
-    shards[features(head), :] = mm(landed[...], pick, TN).astype(BF16)
-    middle = width // 2
-    parts_of = ((0, middle), (middle, width - middle))
+    for c in range(len(spans)):
+        for to in peers:
+            slot_copy(c, to, me).start()
+    for c in range(len(spans)):
+        landed[c][slots_of(me), :] = sent[c][slots_of(me), :]
+
     passed = []
 
-    def shard_copy(index, to, send, recv, part=None):
-        start, size = (0, width) if part is None else parts_of[part]
+    def shard_copy(c, index, to, send, recv):
+        start, size = spans[c]
+        rows_at = pl.ds(pl.multiple_of(index * width + start, 16), size)
         return pltpu.make_async_remote_copy(
-            src_ref=shards.at[features(index, start, size), :],
-            dst_ref=shards.at[features(index, start, size), :],
+            src_ref=shards.at[rows_at, :], dst_ref=shards.at[rows_at, :],
             send_sem=hs_sem.at[send], recv_sem=hr_sem.at[recv],
             device_id={"ctx": me, "head": to}, device_id_type=MESH,
         )
 
-    def push(index, to, recv, part=None):
-        copy = shard_copy(index, to, len(passed), recv, part)
+    def push(c, index, to, recv):
+        copy = shard_copy(c, index, to, len(passed), recv)
         copy.start()
         passed.append(copy)
 
-    here = [ring[dy] * CORES + core for dy in range(n_y)]
-    there = [ring[dy] * CORES + (1 - core) for dy in range(n_y)]
-    up_y, down_y, across = here[1], here[n_y - 1], 2 * n_y
-    push(head, up_y, 2 * 3, 0)
-    push(head, down_y, 2 * 1 + 1, 1)
-    push(head, sibling, across)
-    push(head, up_y, 2 * 3 + 1, 1)
-    push(head, down_y, 2 * 1, 0)
+    def mine(c, dy):
+        return c * 2 * n_y + dy
+
+    def other(c, dy):
+        return c * 2 * n_y + n_y + dy
+
+    def collect(c):
+        start, size = spans[c]
+        for frm in reversed(peers):
+            slot_copy(c, frm, frm).wait_recv()
+        own_at = pl.ds(pl.multiple_of(head * width + start, 16), size)
+        shards[own_at, :] = mm(landed[c][...], pick, TN).astype(BF16)
+        for dy in (2, 1, 3):
+            push(c, head, here[dy], mine(c, n_y - dy))
+        push(c, head, sibling, other(c, 0))
+
+    def hand_over(c, dy):
+        shard_copy(c, here[dy], sibling, 0, mine(c, dy)).wait_recv()
+        push(c, here[dy], sibling, other(c, dy))
+
+    def products(c):
+        start, size = spans[c]
+        for dy in range(n_y):
+            shard_copy(c, there[dy], sibling, 0, other(c, dy)).wait_recv()
+        at_rows = [slice(i * width + start, i * width + start + size) for i in range(n_head)]
+        part = jnp.concatenate([shards[r, :] for r in at_rows], axis=0).T
+
+        def chunk(ref):
+            return jnp.concatenate([ref[r, :] for r in at_rows], axis=0)
+
+        return [mm(part, chunk(w_qkv.at[j])) for j in range(3)] + [
+            mm(part, chunk(w_down)), mm(part, w_beta[c, :, : n_head * size], NT)
+        ]
+
+    collect(0)
+    collect(1)
+    hand_over(0, 1)
+    hand_over(0, 3)
+    collect(2)
+    hand_over(0, 2)
+    for c in (1, 2):
+        hand_over(c, 1)
+        hand_over(c, 3)
     for copy in loads[4:6]:
         copy.wait()
-
-    def landed_half(dy, part, other=False):
-        index, offset = (there[dy], across) if other else (here[dy], 0)
-        shard_copy(index, sibling, 0, offset + 2 * dy + part, part).wait_recv()
-
-    def products(dy):
-        part = shards[pl.ds(pl.multiple_of(ring[dy] * pair, 16), pair), :].T
-        chunk = pl.ds(pl.multiple_of(ring[dy] * pair, 16), pair)
-        return [mm(part, w_qkv[j, chunk, :]) for j in range(3)] + [
-            mm(part, w_down[chunk, :]), mm(part, w_beta[ring[dy]], NT)
-        ]
-
-    def multiply(dy, first=False):
-        for ref, value in zip(sums, products(dy)):
-            ref[...] = value if first else ref[...] + value
-
     sums = [acc.at[0], acc.at[1], acc.at[2], acc_low, acc_beta]
-    shard_copy(there[0], sibling, 0, across).wait_recv()
-    multiply(0, True)
-    landed_half(3, 0)
-    push(here[3], up_y, 2 * 2, 0)
-    landed_half(1, 1)
-    push(here[1], down_y, 2 * 2 + 1, 1)
-    push(here[3], sibling, across + 2 * 3, 0)
-    push(here[1], sibling, across + 2 * 1 + 1, 1)
-    landed_half(3, 1)
-    push(here[3], sibling, across + 2 * 3 + 1, 1)
-    landed_half(1, 0)
-    push(here[1], sibling, across + 2 * 1, 0)
-    landed_half(3, 0, True)
-    landed_half(3, 1, True)
-    multiply(3)
-    landed_half(2, 0)
-    push(here[2], sibling, across + 2 * 2, 0)
-    landed_half(2, 1)
-    push(here[2], sibling, across + 2 * 2 + 1, 1)
-    landed_half(1, 0, True)
-    landed_half(1, 1, True)
-    multiply(1)
-    landed_half(2, 0, True)
-    landed_half(2, 1, True)
+    for ref, value in zip(sums, products(0)):
+        ref[...] = value
+    hand_over(1, 2)
+    hand_over(2, 2)
+    for ref, value in zip(sums, products(1)):
+        ref[...] = ref[...] + value
     last = [ref[...] + value for ref, value in zip(sums, products(2))]
     for j in range(3):
         ext_ref[RIM:, j * columns : (j + 1) * columns] = last[j].astype(BF16).astype(F32)
@@ -269,7 +274,9 @@
             if shift:
                 part = part * jnp.concatenate([valid[shift][first : first + size]] * heads, axis=1)
             out = part if out is None else out + part
-        return out / (1.0 + jnp.exp(-out))
+        grown = 1.0 + jnp.exp(jnp.minimum(-out, 80.0))
+        inverted = pl.reciprocal(grown, approx=True)
+        return out * (inverted * (2.0 - grown * inverted))
 
     def unit(v):
         return v * lax.rsqrt(jnp.sum(v * v, axis=-1, keepdims=True) + 1e-06)
@@ -283,7 +290,7 @@
         )
 
     drive = mm(low_rank, up_ref[...]) + bias_ref[...]
-    soft = jnp.maximum(drive, 0.0) + jnp.log1p(jnp.exp(-jnp.abs(drive)))
+    soft = jnp.maximum(drive, 0.0) + jnp.log(1.0 + jnp.exp(-jnp.abs(drive)))
     rates = jnp.concatenate([jnp.exp(jnp.full((1, channels), rate_ref[h], F32)) for h in every], axis=1)
     decay = -rates * soft
     d_high, d_mid = split(decay)
@@ -548,8 +555,9 @@
         scaled = result * lax.rsqrt(mean + 1e-05) * gain_ref[...]
         out_ref[:, h * channels : (h + 1) * channels] = scaled.astype(BF16)
 
-    for to in peers:
-        slot_copy(to, me).wait_send()
+    for c in range(len(spans)):
+        for to in peers:
+            slot_copy(c, to, me).wait_send()
     for copy in passed + sends + returns:
         copy.wait_send()
     rim.wait_send()
@@ -569,6 +577,7 @@
     half = channels // 2
     message = channels + KEEP + half
     slots = 2 * rows
+    pieces = [pltpu.VMEM((slots, min(LANES, width - start)), BF16) for start in range(0, width, LANES)]
     dma = pltpu.SemaphoreType.DMA
     call = pl.pallas_call(
         fused_kernel,
@@ -586,10 +595,10 @@
             pltpu.VMEM((rank, columns), BF16),
             pltpu.VMEM((1, columns), F32),
             pltpu.VMEM((1, channels), F32),
-            pltpu.VMEM((slots, width), BF16),
-            pltpu.VMEM((slots, width), BF16),
+            *pieces,
+            *pieces,
             pltpu.VMEM((features, rows), BF16),
-            pltpu.VMEM((n_y, 16, CORES * width), BF16),
+            pltpu.VMEM((len(pieces), 16, n_head * LANES), BF16),
             pltpu.VMEM((3, rows, columns), F32),
             pltpu.VMEM((rows, rank), F32),
             pltpu.VMEM((rows, 16), F32),
@@ -603,7 +612,7 @@
             pltpu.VMEM((half, channels), F32),
             pltpu.VMEM((GROUP, half, channels), BF16),
             pltpu.VMEM((GROUP, half, channels), BF16),
-            dma((10,)), dma((n_ctx,)), dma((n_ctx,)), dma((13,)), dma((4 * n_y,)), dma((2,)),
+            dma((10,)), dma((3 * n_ctx,)), dma((3 * n_ctx,)), dma((21,)), dma((6 * n_y,)), dma((2,)),
             dma((GROUP,)), dma((GROUP,)), dma((n_groups,)), dma((n_groups,)), dma((GROUP,)), dma((GROUP,)),
         ],
         compiler_params=pltpu.CompilerParams(

time: 58.5 us -> 58.9 us (level); the launches traced: 57.7 us -> 58.7 us
  Pallas kernels: 57 us -> 58 us
    pallas_call x1, Pallas kernels: 57 us -> 58 us  [on_device(): call(*[pltpu.with_memory_space_constraint(v, pltpu.HBM) for v in operands])]
where the time goes in v6:
time: 58.9 us; the launch traced here: 58.7 us
  Pallas kernels  58 us (98%)
  local copies, waits for them, and re-layouts  0.71 us (1%)
    pallas_call x1, Pallas kernels, on_device(): call(*[pltpu.with_memory_space_constraint(v, pltpu.HBM) for v in operands])  58 us

profile of v6, /device:TPU:128, one launch (start us, length us, event | category | flops | bytes accessed | tf_op | source)
XLA Modules:
  0.0 58.7 jit_solution(16585209257303046309)
XLA Ops:
  0.0 58.0 %delta_prefill.1 = bf16[256,512]{1,0:T(8,128)(2,1)S(1)} custom-call(s32[4]{0:T(128)} %lengths_ref.1, f32[4]{0:T(128)} %rate_ref.1, s32[1,256]{1,0:T(1,128)} %bitcast.11, s32[1,256]{1,0:T(1,128)} %bitcast.12, bf16[288,256]{1,0:T(8,128)(2,1)} %bitcast.7, bf16[3,2304,512]{2,1,0:T(8,128)(2,1)} %wqkv_hbm.1, bf16[2304,128]{1,0:T(8,128)(2,1)} %wdown_hbm.1, ...), custom_call_target="tpu_custom_call" | custom-call | tf_op jit(solution)/shard_map/delta_prefill/pallas_call | solution.py:628
  58.0 0.7 %copy.14 = bf16[256,512]{1,0:T(8,128)(2,1)} copy(bf16[256,512]{1,0:T(8,128)(2,1)S(1)} %delta_prefill.1) | data formatting | bytes 524288

commit v7 on v6

--- a/solution.py
+++ b/solution.py
@@ -37,7 +37,10 @@
 
 
 def mm3(a, b, dims=NN):
-    return mm(a[0], b[0], dims) + (mm(a[0], b[1], dims) + mm(a[1], b[0], dims))
+    axis = 1 - dims[0][0][0]
+    count = a[0].shape[axis]
+    both = mm(jnp.concatenate(a, axis=axis), b[0], dims)
+    return both[:count] + (both[count:] + mm(a[0], b[1], dims))
 
 
 def mm3_narrow(a, b, dims=NN):
@@ -51,7 +54,7 @@
     conv_hbm, up_hbm, bias_hbm, gain_hbm,
     out_ref,
     slot_buf, src_buf, hidden_buf, w_qkv, w_down, wbeta_buf, conv_ref, up_ref, bias_ref, gain_ref,
-    send_a, send_b, send_c, landed_a, landed_b, landed_c, shards, w_beta, acc, acc_low, acc_beta, ext_ref,
+    send_a, send_b, send_c, landed_a, landed_b, landed_c, shards, acc, acc_low, ext_ref,
     stack, local, lift, maps, total, others, state, entry_out, entry,
     in_sem, s_sem, r_sem, hs_sem, hr_sem, rim_sem,
     xs_sem, xr_sem, zs_sem, zr_sem, bs_sem, br_sem,
@@ -90,7 +93,7 @@
         (up_hbm, up_ref), (bias_hbm, bias_ref), (conv_hbm, conv_ref), (gain_hbm, gain_ref),
     ]
     loads = [pltpu.make_async_copy(a, b, in_sem.at[i]) for i, (a, b) in enumerate(operands)]
-    for copy in loads:
+    for copy in loads[:4]:
         copy.start()
 
     far = sorted(
@@ -105,7 +108,7 @@
         pl.semaphore_signal(barrier, inc=1, device_id=at(to), device_id_type=MESH)
     here = [ring[dy] * CORES + core for dy in range(n_y)]
     there = [ring[dy] * CORES + (1 - core) for dy in range(n_y)]
-    for to in here[1:] + [sibling]:
+    for to in here[1:] + there:
         pl.semaphore_signal(barrier, inc=1, device_id={"ctx": me, "head": to}, device_id_type=MESH)
 
     for copy in loads[:4]:
@@ -117,16 +120,14 @@
         spans.append((start, min(LANES, width - start)))
         start += LANES
     sent, landed = (send_a, send_b, send_c), (landed_a, landed_b, landed_c)
-    for c, (start, size) in enumerate(spans):
+
+    def fill(c):
+        start, size = spans[c]
         sent[c][...] = mm(place, hidden_buf[start : start + size, :], NT).astype(BF16)
-    pick = (slot_ids == src_buf[...]).astype(F32).astype(BF16)
-    w_beta[...] = jnp.zeros_like(w_beta)
-    for c, (start, size) in enumerate(spans):
-        for i in range(n_head):
-            at_lane = i * width + start
-            w_beta[c, : wbeta_buf.shape[0], i * size : (i + 1) * size] = wbeta_buf[:, at_lane : at_lane + size]
-
-    pl.semaphore_wait(barrier, n_ctx - 1 + n_y)
+
+    fill(0)
+
+    pl.semaphore_wait(barrier, n_ctx - 1 + n_head - 1)
 
     def slots_of(index):
         return pl.ds(pl.multiple_of(index * cap, cap), cap)
@@ -139,12 +140,18 @@
         )
 
     for c in range(len(spans)):
+        if c:
+            fill(c)
         for to in peers:
             slot_copy(c, to, me).start()
+    for copy in loads[4:]:
+        copy.start()
+    pick = (slot_ids == src_buf[...]).astype(F32).astype(BF16)
     for c in range(len(spans)):
         landed[c][slots_of(me), :] = sent[c][slots_of(me), :]
 
     passed = []
+    last_chunk = len(spans) - 1
 
     def shard_copy(c, index, to, send, recv):
         start, size = spans[c]
@@ -172,9 +179,12 @@
             slot_copy(c, frm, frm).wait_recv()
         own_at = pl.ds(pl.multiple_of(head * width + start, 16), size)
         shards[own_at, :] = mm(landed[c][...], pick, TN).astype(BF16)
-        for dy in (2, 1, 3):
+        for dy in (2, 1, 3) if c else (1, 3):
             push(c, head, here[dy], mine(c, n_y - dy))
         push(c, head, sibling, other(c, 0))
+        if c == last_chunk:
+            for dy in (2, 1, 3):
+                push(c, head, there[dy], other(c, n_y - dy))
 
     def hand_over(c, dy):
         shard_copy(c, here[dy], sibling, 0, mine(c, dy)).wait_recv()
@@ -182,6 +192,9 @@
 
     def products(c):
         start, size = spans[c]
+        if c == last_chunk:
+            for dy in range(1, n_y):
+                shard_copy(c, here[dy], sibling, 0, mine(c, dy)).wait_recv()
         for dy in range(n_y):
             shard_copy(c, there[dy], sibling, 0, other(c, dy)).wait_recv()
         at_rows = [slice(i * width + start, i * width + start + size) for i in range(n_head)]
@@ -190,32 +203,29 @@
         def chunk(ref):
             return jnp.concatenate([ref[r, :] for r in at_rows], axis=0)
 
-        return [mm(part, chunk(w_qkv.at[j])) for j in range(3)] + [
-            mm(part, chunk(w_down)), mm(part, w_beta[c, :, : n_head * size], NT)
-        ]
+        return [mm(part, chunk(w_qkv.at[j])) for j in range(3)] + [mm(part, chunk(w_down))]
 
     collect(0)
     collect(1)
     hand_over(0, 1)
+    push(0, here[1], here[n_y - 1], mine(0, 2))
     hand_over(0, 3)
     collect(2)
     hand_over(0, 2)
-    for c in (1, 2):
-        hand_over(c, 1)
-        hand_over(c, 3)
+    hand_over(1, 1)
+    hand_over(1, 3)
     for copy in loads[4:6]:
         copy.wait()
-    sums = [acc.at[0], acc.at[1], acc.at[2], acc_low, acc_beta]
+    sums = [acc.at[0], acc.at[1], acc.at[2], acc_low]
     for ref, value in zip(sums, products(0)):
         ref[...] = value
     hand_over(1, 2)
-    hand_over(2, 2)
     for ref, value in zip(sums, products(1)):
         ref[...] = ref[...] + value
     last = [ref[...] + value for ref, value in zip(sums, products(2))]
     for j in range(3):
         ext_ref[RIM:, j * columns : (j + 1) * columns] = last[j].astype(BF16).astype(F32)
-    low_rank, beta_logit = last[3].astype(BF16), last[4]
+    low_rank = last[3].astype(BF16)
     rim = pltpu.make_async_remote_copy(
         src_ref=ext_ref.at[pl.ds(rows, RIM), :], dst_ref=ext_ref.at[pl.ds(0, RIM), :],
         send_sem=rim_sem.at[0], recv_sem=rim_sem.at[1],
@@ -296,7 +306,9 @@
     d_high, d_mid = split(decay)
     d_low = (decay - d_high.astype(F32) - d_mid.astype(F32)).astype(BF16)
     cum_all = mm(running, d_high) + (mm(running, d_mid) + mm(running, d_low))
-    betas = 1.0 / (1.0 + jnp.exp(-beta_logit))
+    logits = mm(wbeta_buf[...], shards[...])
+    logits = jnp.concatenate([logits, jnp.zeros((8 - heads, rows), F32)], axis=0).T
+    betas = 1.0 / (1.0 + jnp.exp(-logits))
     cums = [of_head(cum_all, h) for h in every]
     strengths = [jnp.broadcast_to(betas[:, h : h + 1], (rows, channels)) for h in every]
     lasts = [[cums[h][(b + 1) * SPAN - 1 : (b + 1) * SPAN] for b in range(blocks)] for h in every]
@@ -342,12 +354,13 @@
         score.append(reads)
 
     def spread(v):
-        return jnp.concatenate(
-            [jnp.where(small_block == b, v, 0.0) for b in range(blocks)], axis=0
+        return tuple(
+            jnp.concatenate([jnp.where(small_block == b, part, 0.0).astype(BF16) for b in range(blocks)], axis=0)
+            for part in split(v)
         )
 
     def times(lefts, rights):
-        return [mm3(split(a), split(spread(b))) for a, b in zip(lefts, rights)]
+        return [mm3(split(a), spread(b)) for a, b in zip(lefts, rights)]
 
     diagonal = []
     for h in every:
@@ -598,10 +611,8 @@
             *pieces,
             *pieces,
             pltpu.VMEM((features, rows), BF16),
-            pltpu.VMEM((len(pieces), 16, n_head * LANES), BF16),
             pltpu.VMEM((3, rows, columns), F32),
             pltpu.VMEM((rows, rank), F32),
-            pltpu.VMEM((rows, 16), F32),
             pltpu.VMEM((RIM + rows, 3 * columns), F32),
             pltpu.VMEM((heads, 2 * channels + KEEP, channels), BF16),
             pltpu.VMEM((heads, rows, channels), F32),

time: 58.9 us -> 57 us (0.968)
  Pallas kernels: 58 us -> 55.9 us
    pallas_call x1, Pallas kernels: 58 us -> 55.9 us  [on_device(): call(*[pltpu.with_memory_space_constraint(v, pltpu.HBM) for v in operands])]
where the time goes in v7:
time: 57 us; the launch traced here: 56.6 us
  Pallas kernels  55.9 us (98%)
  local copies, waits for them, and re-layouts  0.71 us (1%)
    pallas_call x1, Pallas kernels, on_device(): call(*[pltpu.with_memory_space_constraint(v, pltpu.HBM) for v in operands])  55.9 us

profile of v7, /device:TPU:128, one launch (start us, length us, event | category | flops | bytes accessed | tf_op | source)
XLA Modules:
  0.0 56.6 jit_solution(13404534333305758686)
XLA Ops:
  0.0 55.9 %delta_prefill.1 = bf16[256,512]{1,0:T(8,128)(2,1)S(1)} custom-call(s32[4]{0:T(128)} %lengths_ref.1, f32[4]{0:T(128)} %rate_ref.1, s32[1,256]{1,0:T(1,128)} %bitcast.11, s32[1,256]{1,0:T(1,128)} %bitcast.12, bf16[288,256]{1,0:T(8,128)(2,1)} %bitcast.7, bf16[3,2304,512]{2,1,0:T(8,128)(2,1)} %wqkv_hbm.1, bf16[2304,128]{1,0:T(8,128)(2,1)} %wdown_hbm.1, ...), custom_call_target="tpu_custom_call" | custom-call | tf_op jit(solution)/shard_map/delta_prefill/pallas_call | solution.py:639
  55.9 0.7 %copy.14 = bf16[256,512]{1,0:T(8,128)(2,1)} copy(bf16[256,512]{1,0:T(8,128)(2,1)S(1)} %delta_prefill.1) | data formatting | bytes 524288

commit v8 on v7

--- a/solution.py
+++ b/solution.py
@@ -451,8 +451,15 @@
 
     for h in every:
         combined = mm3(split(jnp.concatenate(score[h], axis=0)), solved[h])
-        lift[h] = full_queries[h] - combined[:, :channels]
+        lift[h] = jnp.concatenate(split(full_queries[h] - combined[:, :channels]), axis=1)
         local[h] = combined[:, channels:]
+
+    for c in range(len(spans)):
+        for to in peers:
+            slot_copy(c, to, me).wait_send()
+    for copy in passed:
+        copy.wait_send()
+    rim.wait_send()
 
     for frm in mates:
         pltpu.make_async_remote_copy(
@@ -553,6 +560,9 @@
     for copy in returns:
         copy.start()
     entry[member] = entry_out[member]
+    for copy in sends:
+        copy.wait_send()
+    for_later_groups(lambda copy: copy.wait_send())
     for frm in mates:
         pltpu.make_async_remote_copy(
             src_ref=entry_out.at[frm], dst_ref=entry.at[frm],
@@ -562,19 +572,13 @@
 
     for h in every:
         incoming = jnp.concatenate([entry[h], entry[X_SIZE + h]], axis=0)
-        parts = jnp.concatenate(split(lift[h]), axis=1)
-        result = local[h] + mm(parts, jnp.concatenate([incoming, incoming], axis=1), NT)
+        result = local[h] + mm(lift[h], jnp.concatenate([incoming, incoming], axis=1), NT)
         mean = jnp.mean(result * result, axis=-1, keepdims=True)
         scaled = result * lax.rsqrt(mean + 1e-05) * gain_ref[...]
         out_ref[:, h * channels : (h + 1) * channels] = scaled.astype(BF16)
 
-    for c in range(len(spans)):
-        for to in peers:
-            slot_copy(c, to, me).wait_send()
-    for copy in passed + sends + returns:
+    for copy in returns:
         copy.wait_send()
-    rim.wait_send()
-    for_later_groups(lambda copy: copy.wait_send())
 
 
 def on_device(
@@ -616,7 +620,7 @@
             pltpu.VMEM((RIM + rows, 3 * columns), F32),
             pltpu.VMEM((heads, 2 * channels + KEEP, channels), BF16),
             pltpu.VMEM((heads, rows, channels), F32),
-            pltpu.VMEM((heads, rows, channels), F32),
+            pltpu.VMEM((heads, rows, 2 * channels), BF16),
             pltpu.VMEM((GROUP, message, channels), BF16),
             pltpu.VMEM((message, channels), BF16),
             pltpu.VMEM((n_groups, message, channels), BF16),

time: 57 us -> 56.8 us (level)
  no operation moved by 1% of the time
where the time goes in v8:
time: 56.8 us; the launch traced here: 56.4 us
  Pallas kernels  55.6 us (98%)
  local copies, waits for them, and re-layouts  0.71 us (1%)
    pallas_call x1, Pallas kernels, on_device(): call(*[pltpu.with_memory_space_constraint(v, pltpu.HBM) for v in operands])  55.6 us

profile of v8, /device:TPU:128, one launch (start us, length us, event | category | flops | bytes accessed | tf_op | source)
XLA Modules:
  0.0 56.4 jit_solution(9981927427557366149)
XLA Ops:
  0.0 55.6 %delta_prefill.1 = bf16[256,512]{1,0:T(8,128)(2,1)S(1)} custom-call(s32[4]{0:T(128)} %lengths_ref.1, f32[4]{0:T(128)} %rate_ref.1, s32[1,256]{1,0:T(1,128)} %bitcast.11, s32[1,256]{1,0:T(1,128)} %bitcast.12, bf16[288,256]{1,0:T(8,128)(2,1)} %bitcast.7, bf16[3,2304,512]{2,1,0:T(8,128)(2,1)} %wqkv_hbm.1, bf16[2304,128]{1,0:T(8,128)(2,1)} %wdown_hbm.1, ...), custom_call_target="tpu_custom_call" | custom-call | tf_op jit(solution)/shard_map/delta_prefill/pallas_call | solution.py:643
  55.7 0.7 %copy.14 = bf16[256,512]{1,0:T(8,128)(2,1)} copy(bf16[256,512]{1,0:T(8,128)(2,1)S(1)} %delta_prefill.1) | data formatting | bytes 524288

commit v9 on v8

--- a/solution.py
+++ b/solution.py
@@ -306,8 +306,7 @@
     d_high, d_mid = split(decay)
     d_low = (decay - d_high.astype(F32) - d_mid.astype(F32)).astype(BF16)
     cum_all = mm(running, d_high) + (mm(running, d_mid) + mm(running, d_low))
-    logits = mm(wbeta_buf[...], shards[...])
-    logits = jnp.concatenate([logits, jnp.zeros((8 - heads, rows), F32)], axis=0).T
+    logits = mm(wbeta_buf[...], shards[...])[:8].T
     betas = 1.0 / (1.0 + jnp.exp(-logits))
     cums = [of_head(cum_all, h) for h in every]
     strengths = [jnp.broadcast_to(betas[:, h : h + 1], (rows, channels)) for h in every]
@@ -607,7 +606,7 @@
             pltpu.VMEM((width, rows), BF16),
             pltpu.VMEM((3, features, columns), BF16),
             pltpu.VMEM((features, rank), BF16),
-            pltpu.VMEM((heads, features), BF16),
+            pltpu.VMEM((16, features), BF16),
             pltpu.VMEM((3, CONV, columns), F32),
             pltpu.VMEM((rank, columns), BF16),
             pltpu.VMEM((1, columns), F32),
@@ -637,7 +636,7 @@
     )
     operands = (
         prompt_lengths, a_log, send_slot.reshape(1, rows), gather_src.reshape(1, rows), hidden.T,
-        qkv_weight, gate_down, w_beta.T, conv_weight.transpose(1, 0, 2), gate_up,
+        qkv_weight, gate_down, jnp.pad(w_beta.T, ((0, 16 - heads), (0, 0))), conv_weight.transpose(1, 0, 2), gate_up,
         dt_bias.reshape(1, columns), norm_gain.reshape(1, channels),
     )
     return call(*[pltpu.with_memory_space_constraint(v, pltpu.HBM) for v in operands])

time: 56.8 us -> 58.2 us (1.025)
  local copies, waits for them, and re-layouts: 0.71 us -> 2.07 us
    pad x0 -> x1, local copies, waits for them, and re-layouts: none -> 1.36 us  [on_device(): jnp.pad(w_beta.T, ((0, 16 - heads), (0, 0)))]
where the time goes in v9:
time: 58.2 us; the launch traced here: 57.7 us
  Pallas kernels  55.6 us (96%)
  local copies, waits for them, and re-layouts  2.07 us (4%)
    pallas_call x1, Pallas kernels, on_device(): call(*[pltpu.with_memory_space_constraint(v, pltpu.HBM) for v in operands])  55.6 us
    pad x1, local copies, waits for them, and re-layouts, on_device(): jnp.pad(w_beta.T, ((0, 16 - heads), (0, 0)))  1.36 us

profile of v9, /device:TPU:128, one launch (start us, length us, event | category | flops | bytes accessed | tf_op | source)
XLA Modules:
  0.0 57.7 jit_solution(18116487873959024166)
XLA Ops:
  0.0 1.4 %pad.4.wbeta_hbm = bf16[16,2304]{1,0:T(8,128)(2,1)} pad(bf16[4,2304]{1,0:T(4,128)(2,1)} %bitcast.9, bf16[]{:T(256)} %constant.2.clone.1), padding=0_12x0_0 | pad | bytes 92162 | tf_op jit(solution)/shard_map/jit(_pad)/pad | solution.py:639
  1.4 55.6 %delta_prefill.1 = bf16[256,512]{1,0:T(8,128)(2,1)S(1)} custom-call(s32[4]{0:T(128)} %lengths_ref.1, f32[4]{0:T(128)} %rate_ref.1, s32[1,256]{1,0:T(1,128)} %bitcast.11, s32[1,256]{1,0:T(1,128)} %bitcast.12, bf16[288,256]{1,0:T(8,128)(2,1)} %bitcast.7, bf16[3,2304,512]{2,1,0:T(8,128)(2,1)} %wqkv_hbm.1, bf16[2304,128]{1,0:T(8,128)(2,1)} %wdown_hbm.1, ...), custom_call_target="tpu_custom_call" | custom-call | tf_op jit(solution)/shard_map/delta_prefill/pallas_call | solution.py:642
  57.0 0.7 %copy.14 = bf16[256,512]{1,0:T(8,128)(2,1)} copy(bf16[256,512]{1,0:T(8,128)(2,1)S(1)} %delta_prefill.1) | data formatting | bytes 524288
